TPU v7x, 128 devices: a whole 4x4x4 slice. The times are simulated.
128 devices in a mesh: dp: 32 (over y, z, core), mp: 4 (over x).
Axes of the slice: x: 4, y: 4, z: 4, core: 2. Of those that a mesh axis runs over, the one named last changes fastest.
Arguments:
- prompt_hidden: bfloat16 [4096, 5120], P('dp'), may hold values from -6 to 6
- kv_weight: bfloat16 [5120, 2, 1024], P(None, None, 'mp'), may hold values from -0.078125 to 0.078125
- queries: bfloat16 [256, 128, 5120], P('dp', None, 'mp'), may hold values from -88 to 88
- out_grad: bfloat16 [256, 128, 5120], P('dp', None, 'mp'), may hold values from -6 to 6
- own_kv: bfloat16 [256, 128, 2, 1024], P('dp', None, None, 'mp'), may hold values from -4 to 4
- pack_counts: int32 [32], replicated, may hold values from 0 to 8, as said below
- slot_groups: int32 [32, 8], replicated, may hold values from 0 to 7, as said below
- block_group: int32 [32], replicated, may hold values from 0 to 7, as said below
Outputs:
- attn_out: bfloat16 [256, 128, 5120], P('dp', None, 'mp')
- query_grad: bfloat16 [256, 128, 5120], P('dp', None, 'mp')
- own_kv_grad: bfloat16 [256, 128, 2, 1024], P('dp', None, None, 'mp')
- weight_grad: float32 [5120, 2, 1024], P('dp', None, 'mp')
- prompt_grad: bfloat16 [4096, 5120], P('dp', 'mp')
Inputs may be any that keep to these rules, and one draw needn't show every extreme that they name: `pack_counts`: device d and device d + 16 together use 8 slots; some device uses all 8. `slot_groups`: used slots name every prompt exactly 16 times; unused slots hold arbitrary prompt numbers. `block_group`: every prompt has exactly 4 blocks.
All inputs are finite; a program needn't handle non-finite values.
Results may differ from a plain program's by a relative error of at most 0.028.
Values may be sent and summed in bfloat16 or wider, within the bound.
No kernel may reach another device: no remote copies, remote signals or barrier semaphores. Data moves between devices by JAX's collectives and lax.ppermute only.
A program may use at most 128 MiB of HBM per device.

v0:
```python
import math

import jax
import jax.numpy as jnp
from jax import lax
from jax.sharding import PartitionSpec as P

HD = 128
GROUP = 16


def slot_attention(queries, grads, own, prefix, score_scale):
    plen = prefix.shape[0]
    keys = jnp.concatenate([prefix[:, 0], own[:, 0]], 0)
    values = jnp.concatenate([prefix[:, 1], own[:, 1]], 0)
    scores = (
        jnp.einsum("rkgd,lkd->kgrl", queries, keys, preferred_element_type=jnp.float32)
        * score_scale
    )
    query_pos = jnp.arange(queries.shape[0], dtype=jnp.int32)
    key_pos = jnp.arange(keys.shape[0], dtype=jnp.int32)
    visible = (key_pos[None, :] < plen) | (key_pos[None, :] - plen <= query_pos[:, None])
    scores = jnp.where(visible, scores, -1e30)
    row_max = jnp.max(scores, axis=-1, keepdims=True)
    expd = jnp.exp(scores - row_max)
    prob = expd / jnp.sum(expd, axis=-1, keepdims=True)
    prob_b = prob.astype(jnp.bfloat16)
    attended = jnp.einsum("kgrl,lkd->rkgd", prob_b, values, preferred_element_type=jnp.float32)
    delta = jnp.transpose(jnp.sum(grads.astype(jnp.float32) * attended, axis=-1), (1, 2, 0))
    dprob = jnp.einsum("rkgd,lkd->kgrl", grads, values, preferred_element_type=jnp.float32)
    dscore = (prob * (dprob - delta[..., None])).astype(jnp.bfloat16)
    query_grad = (
        jnp.einsum("kgrl,lkd->rkgd", dscore, keys, preferred_element_type=jnp.float32) * score_scale
    )
    key_grads = (
        jnp.einsum("kgrl,rkgd->lkd", dscore, queries, preferred_element_type=jnp.float32)
        * score_scale
    )
    value_grads = jnp.einsum("kgrl,rkgd->lkd", prob_b, grads, preferred_element_type=jnp.float32)
    both = jnp.stack([key_grads, value_grads], 1)
    return (
        attended.astype(jnp.bfloat16),
        query_grad.astype(jnp.bfloat16),
        both[plen:].astype(jnp.bfloat16),
        both[:plen],
    )


def body(
    prompt_hidden, kv_weight, queries, out_grad, own_kv, pack_counts, slot_groups, block_group
):
    block_rows = prompt_hidden.shape[0]
    model_width = prompt_hidden.shape[1]
    kv_width = kv_weight.shape[2]
    slot_count = queries.shape[0]
    resp_rows = queries.shape[1]
    query_width = queries.shape[2]
    kv_local = kv_width // HD
    repeats = query_width // kv_width
    devices = lax.axis_size("dp")
    my_index = lax.axis_index("dp")
    groups_all = devices * slot_count // (2 * GROUP)
    per_group = devices // groups_all
    score_scale = 1.0 / math.sqrt(HD)
    projected = jnp.dot(
        prompt_hidden,
        kv_weight.reshape(model_width, 2 * kv_width),
        preferred_element_type=jnp.float32,
    ).astype(jnp.bfloat16)
    everyone = lax.all_gather(projected.reshape(block_rows, 2, kv_width), "dp", axis=0, tiled=True)
    everyone = everyone.reshape(devices, block_rows, 2, kv_local, HD)
    group_blocks = jnp.argsort(block_group, stable=True).reshape(groups_all, per_group)
    my_groups = lax.dynamic_index_in_dim(slot_groups, my_index, 0, keepdims=False)
    my_count = lax.dynamic_index_in_dim(pack_counts, my_index, 0, keepdims=False)

    def advance(position, carry):
        outs, qgrads, owngrads, accum = carry
        q_slot = lax.dynamic_index_in_dim(queries, position, 0, keepdims=False)
        g_slot = lax.dynamic_index_in_dim(out_grad, position, 0, keepdims=False)
        own_slot = lax.dynamic_index_in_dim(own_kv, position, 0, keepdims=False)
        chosen = group_blocks[my_groups[position]]
        prefix = everyone[chosen].reshape(per_group * block_rows, 2, kv_local, HD)
        attended, query_grad, own_grad, prefix_grad = slot_attention(
            q_slot.reshape(resp_rows, kv_local, repeats, HD),
            g_slot.reshape(resp_rows, kv_local, repeats, HD),
            own_slot.reshape(resp_rows, 2, kv_local, HD),
            prefix,
            score_scale,
        )
        outs = lax.dynamic_update_index_in_dim(
            outs, attended.reshape(resp_rows, query_width), position, 0
        )
        qgrads = lax.dynamic_update_index_in_dim(
            qgrads, query_grad.reshape(resp_rows, query_width), position, 0
        )
        owngrads = lax.dynamic_update_index_in_dim(
            owngrads, own_grad.reshape(resp_rows, 2, kv_width), position, 0
        )
        accum = accum.at[chosen].add(prefix_grad.reshape(per_group, block_rows, 2, kv_width))
        return (outs, qgrads, owngrads, accum)

    start = (
        jnp.zeros(queries.shape, jnp.bfloat16),
        jnp.zeros(queries.shape, jnp.bfloat16),
        jnp.zeros(own_kv.shape, jnp.bfloat16),
        jnp.zeros((devices, block_rows, 2, kv_width), jnp.float32),
    )
    outs, qgrads, owngrads, accum = lax.fori_loop(0, my_count, advance, start)
    block_total = lax.psum_scatter(
        accum.reshape(devices * block_rows, 2, kv_width).astype(jnp.bfloat16),
        "dp",
        scatter_dimension=0,
        tiled=True,
    )
    block_b = block_total.reshape(block_rows, 2 * kv_width)
    term = jnp.einsum("pd,pc->dc", prompt_hidden, block_b, preferred_element_type=jnp.float32)
    weight_grad = lax.psum_scatter(
        term.reshape(lax.axis_size("dp") * (model_width // devices), 2, kv_width).astype(
            jnp.bfloat16
        ),
        "dp",
        scatter_dimension=0,
        tiled=True,
    ).astype(jnp.float32)
    hidden_term = jnp.einsum(
        "pc,dc->pd",
        block_b,
        kv_weight.reshape(model_width, 2 * kv_width),
        preferred_element_type=jnp.float32,
    )
    prompt_grad = lax.psum_scatter(
        hidden_term.astype(jnp.bfloat16), "mp", scatter_dimension=1, tiled=True
    )
    return (outs, qgrads, owngrads, weight_grad, prompt_grad)


def solution(mesh):
    return jax.shard_map(
        body,
        mesh=mesh,
        in_specs=(
            P("dp", None),
            P(None, None, "mp"),
            P("dp", None, "mp"),
            P("dp", None, "mp"),
            P("dp", None, None, "mp"),
            P(),
            P(),
            P(),
        ),
        out_specs=(
            P("dp", None, "mp"),
            P("dp", None, "mp"),
            P("dp", None, None, "mp"),
            P("dp", None, "mp"),
            P("dp", "mp"),
        ),
        check_vma=False,
    )
```

profile of v0, /device:TPU:1, one launch (start us, length us, event | category | flops | bytes accessed | tf_op | source)
XLA Modules:
  0.0 700.3 jit_solution(8972919780626909576)
XLA Ops:
  7.2 3.5 copy.100
  15.5 47.1 %all-gather.2.cloned.1.call-done = bf16[4096,2,256]{2,1,0:T(2,128)(2,1)} async-done(((bf16[128,2,256]{2,1,0:T(2,128)(2,1)}), bf16[4096,2,256]{2,1,0:T(2,128)(2,1)}) %all-gather.2.cloned.1.call-update) | async-done | bytes 4194320 | tf_op jit(solution)/shard_map/all_gather | solution.py:70
  62.5 11.7 %reshape.120 = bf16[32,128,2,2,128]{4,3,2,1,0:T(2,128)(2,1)} reshape(bf16[4096,2,256]{2,1,0:T(2,128)(2,1)} %all-gather.2.cloned.1.call-done) | data formatting | bytes 8388608 | tf_op jit(solution)/shard_map/reshape | solution.py:71
  74.2 4.2 broadcast_in_dim.49
  83.3 184.0 %while.18 = (s32[]{:T(128)}, bf16[8,128,1280]{2,1,0:T(8,128)(2,1)}, bf16[8,128,1280]{2,1,0:T(8,128)(2,1)}, bf16[8,128,2,256]{3,2,1,0:T(2,128)(2,1)}, f32[32,128,...) while((s32[]{:T(128)}, bf16[8,128,1280]{2,1,0:T(8,128)(2,1)}, ...), condition=%wide.region_6.7_spmd, body=%wide.region_1.6_spmd.sunk | while | flops 1271006848 | bytes 68423456 | solution.py:108
  87.4 3.8 gather_fusion
  95.5 2.8 fusion.74
  98.3 2.2 fusion.75
  100.6 1.7 constant_dynamic-slice_fusion.7
  105.0 2.2 multiply_reduce_fusion.2
  107.3 2.7 fusion.76
  113.8 2.7 copy.124
  116.5 3.5 scatter_fusion
  125.0 2.1 fusion.77
  133.2 3.8 gather_fusion
  141.3 2.8 fusion.74
  144.1 2.2 fusion.75
  146.3 1.7 constant_dynamic-slice_fusion.7
  150.8 2.2 multiply_reduce_fusion.2
  153.1 2.7 fusion.76
  159.6 2.7 copy.124
  162.3 3.6 scatter_fusion
  170.8 2.1 fusion.77
  179.0 3.8 gather_fusion
  187.1 2.8 fusion.74
  189.9 2.2 fusion.75
  192.2 1.7 constant_dynamic-slice_fusion.7
  196.6 2.2 multiply_reduce_fusion.2
  198.9 2.7 fusion.76
  205.4 2.7 copy.124
  208.1 3.5 scatter_fusion
  216.6 2.1 fusion.77
  224.8 3.8 gather_fusion
  232.8 2.8 fusion.74
  235.7 2.2 fusion.75
  242.4 2.2 multiply_reduce_fusion.2
  244.6 2.7 fusion.76
  251.2 2.7 copy.124
  253.8 3.5 scatter_fusion
  262.4 2.1 fusion.77
  267.4 6.0 copy.104
  273.4 261.0 %reduce-scatter.3.cloned.1.call-done = bf16[128,2,256]{2,0,1:T(8,128)(2,1)} async-done(((bf16[4096,2,256]{2,0,1:T(8,128)(2,1)}), bf16[128,2,256]{2,0,1:T(8,128)(2,1)}) %reduce-scatter.3.cloned.1.call-update) | async-done | bytes 131088 | tf_op jit(solution)/shard_map/reduce_scatter | solution.py:109
  535.4 3.9 convolution_convert_fusion
  539.3 13.6 %copy.68 = bf16[5120,2,256]{2,1,0:T(2,128)(2,1)} copy(bf16[5120,2,256]{0,2,1:T(8,128)(2,1)} %bitcast.192) | data formatting | bytes 10485760 | tf_op jit(solution)/shard_map/convert_element_type | solution.py:118
  553.8 5.4 fusion.28
  560.5 107.5 %all-reduce.3.cloned.1.call-done = bf16[5120,2,256]{2,1,0:T(2,128)(2,1)} async-done(((bf16[5120,2,256]{2,1,0:T(2,128)(2,1)}), bf16[5120,2,256]{2,1,0:T(2,128)(2,1)}) %all-reduce.3.cloned.1.call-update) | async-done | bytes 5242896
  668.0 1.8 dynamic-slice_convert_fusion
  669.7 24.0 %reduce-scatter.5.cloned.1.call-done = bf16[128,1280]{1,0:T(8,128)(2,1)} async-done(((bf16[128,5120]{1,0:T(8,128)(2,1)}), bf16[128,1280]{1,0:T(8,128)(2,1)}) %reduce-scatter.5.cloned.1.call-update) | async-done | bytes 327696 | tf_op jit(solution)/shard_map/reduce_scatter | solution.py:131
  (201 shorter events, 90.4 us)
Async XLA Ops:
  7.2 3.5 copy-start
  7.2 55.3 %all-gather.2.cloned.1.call-start = ((), (), s32[]{:S(2)}) async-start(), calls=%async_computation.2 | async-start | bytes 4325376 | tf_op jit(solution)/shard_map/all_gather | solution.py:70
  10.7 1.7 copy-start.11
  10.7 2.3 copy-start.10
  10.7 3.0 copy-start.12
  12.3 522.1 %reduce-scatter.3.cloned.1.call-start = ((), (), s32[]{:S(2)}) async-start(), calls=%async_computation.3 | async-start | bytes 4325376 | tf_op jit(solution)/shard_map/reduce_scatter | solution.py:109
  93.9 4.4 copy-start.8
  95.2 3.1 copy-start.6
  107.3 2.7 copy-start.7
  110.0 1.3 copy-start.1
  110.6 0.9 copy-start.3
  111.5 0.9 copy-start.4
  113.8 11.2 %copy-start.2 = (bf16[2,5,128,640]{2,3,1,0:T(8,128)(2,1)S(1)}, bf16[2,5,128,640]{2,3,1,0:T(8,128)(2,1)}, u32[]{:S(2)}) copy-start(bf16[2,5,128,640]{2,3,1,0:T(8,128)(2,1)} %copy-done.1) | copy-start | bytes 4915204 | tf_op jit(solution)/shard_map/while
  116.5 11.7 %copy-start.5 = (bf16[128,2,5,128]{0,3,2,1:T(8,128)(2,1)S(1)}, bf16[128,2,5,128]{0,3,2,1:T(8,128)(2,1)}, u32[]{:S(2)}) copy-start(bf16[128,2,5,128]{0,3,2,1:T(8,128)(2,1)} %get-tuple-element.343) | copy-start | bytes 983044 | tf_op jit(solution)/shard_map/while
  139.7 4.4 copy-start.8
  141.0 3.1 copy-start.6
  153.1 2.7 copy-start.7
  155.8 1.3 copy-start.1
  156.4 0.9 copy-start.3
  157.3 0.9 copy-start.4
  159.6 11.2 %copy-start.2 = (bf16[2,5,128,640]{2,3,1,0:T(8,128)(2,1)S(1)}, bf16[2,5,128,640]{2,3,1,0:T(8,128)(2,1)}, u32[]{:S(2)}) copy-start(bf16[2,5,128,640]{2,3,1,0:T(8,128)(2,1)} %copy-done.1) | copy-start | bytes 4915204 | tf_op jit(solution)/shard_map/while
  162.3 11.8 %copy-start.5 = (bf16[128,2,5,128]{0,3,2,1:T(8,128)(2,1)S(1)}, bf16[128,2,5,128]{0,3,2,1:T(8,128)(2,1)}, u32[]{:S(2)}) copy-start(bf16[128,2,5,128]{0,3,2,1:T(8,128)(2,1)} %get-tuple-element.343) | copy-start | bytes 983044 | tf_op jit(solution)/shard_map/while
  185.6 4.4 copy-start.8
  186.8 3.1 copy-start.6
  198.9 2.7 copy-start.7
  201.6 1.3 copy-start.1
  202.2 0.9 copy-start.3
  203.1 0.9 copy-start.4
  205.4 11.1 %copy-start.2 = (bf16[2,5,128,640]{2,3,1,0:T(8,128)(2,1)S(1)}, bf16[2,5,128,640]{2,3,1,0:T(8,128)(2,1)}, u32[]{:S(2)}) copy-start(bf16[2,5,128,640]{2,3,1,0:T(8,128)(2,1)} %copy-done.1) | copy-start | bytes 4915204 | tf_op jit(solution)/shard_map/while
  208.1 11.7 %copy-start.5 = (bf16[128,2,5,128]{0,3,2,1:T(8,128)(2,1)S(1)}, bf16[128,2,5,128]{0,3,2,1:T(8,128)(2,1)}, u32[]{:S(2)}) copy-start(bf16[128,2,5,128]{0,3,2,1:T(8,128)(2,1)} %get-tuple-element.343) | copy-start | bytes 983044 | tf_op jit(solution)/shard_map/while
  231.3 4.4 copy-start.8
  232.6 3.1 copy-start.6
  244.6 2.7 copy-start.7
  247.4 1.3 copy-start.1
  248.0 0.9 copy-start.3
  248.9 0.9 copy-start.4
  251.2 11.2 %copy-start.2 = (bf16[2,5,128,640]{2,3,1,0:T(8,128)(2,1)S(1)}, bf16[2,5,128,640]{2,3,1,0:T(8,128)(2,1)}, u32[]{:S(2)}) copy-start(bf16[2,5,128,640]{2,3,1,0:T(8,128)(2,1)} %copy-done.1) | copy-start | bytes 4915204 | tf_op jit(solution)/shard_map/while
  253.8 11.8 %copy-start.5 = (bf16[128,2,5,128]{0,3,2,1:T(8,128)(2,1)S(1)}, bf16[128,2,5,128]{0,3,2,1:T(8,128)(2,1)}, u32[]{:S(2)}) copy-start(bf16[128,2,5,128]{0,3,2,1:T(8,128)(2,1)} %get-tuple-element.343) | copy-start | bytes 983044 | tf_op jit(solution)/shard_map/while
  273.4 394.6 %all-reduce.3.cloned.1.call-start = ((), (), s32[]{:S(2)}) async-start(), calls=%async_computation.5 | async-start | bytes 10485760
  552.9 0.9 copy-start.9
  552.9 6.3 copy-start.13
  552.9 140.8 %reduce-scatter.5.cloned.1.call-start = ((), (), s32[]{:S(2)}) async-start(), calls=%async_computation.4 | async-start | bytes 1638400 | tf_op jit(solution)/shard_map/reduce_scatter | solution.py:131
Sparse Core Ops, SparseCore 0:
  12.4 50.0 all-gather.1
  273.5 260.8 reduce-scatter.2
  553.0 114.8 all-reduce.2
  670.8 22.8 reduce-scatter.4
where the time goes:
time: 705 us; the launch traced here: 700 us
  waiting for transfers between devices  440 us (62%)
  local copies, waits for them, and re-layouts  145 us (21%)
  matrix products  54.5 us (8%)
  other arithmetic  34.6 us (5%)
  between operations  14.5 us (2%)
  loops' own time  12.2 us (2%)
    reduce_scatter x1, waiting for transfers between devices, body(): lax.psum_scatter(accum.reshape(devices * block_rows, 2, kv_width).astype(...  261 us
    unnamed x5, waiting for transfers between devices  108 us
    all_gather x1, waiting for transfers between devices, body(): lax.all_gather(projected.reshape(block_rows, 2, kv_width), 'dp', axis=0,...  47.1 us
    reduce_scatter x1, waiting for transfers between devices, body(): lax.psum_scatter(hidden_term.astype(jnp.bfloat16), 'mp', scatter_dimensio...  24 us
    reshape x8, local copies, waits for them, and re-layouts, advance(): prefix_grad.reshape(per_group, block_rows, 2, kv_width)  16 us
    gather x8, local copies, waits for them, and re-layouts, advance(): prefix = everyone[chosen].reshape(per_group * block_rows, 2, kv_local, HD)  15.5 us
    scatter-add x4, other arithmetic, advance(): accum.at[chosen]  14.2 us
  transfers between devices with their start and end apart: 4, of which 4 were waited for; matrix products, arithmetic and copies ran while one was open for 2% of the time, Pallas kernels for 0%

commit v1 on v0

v1 whole, which is shorter than its diff:
```python
import functools
import math

import jax
import jax.numpy as jnp
from jax import lax
from jax.experimental import pallas as pl
from jax.experimental.pallas import tpu as pltpu
from jax.sharding import Mesh, PartitionSpec as P

HD = 128
GROUP = 16
GROUPS = 8
BLOCKS = 4
SLOTS = 8
RESP = 128
REPEATS = 5
N_DP = 32
F32 = jnp.float32
BF16 = jnp.bfloat16
SCALE = 1.0 / math.sqrt(HD)
LOG2_SCALE = SCALE * math.log2(math.e)
NT = (((1,), (1,)), ((), ()))
NN = (((1,), (0,)), ((), ()))


def dot(a, b, dims):
    return lax.dot_general(a, b, dims, preferred_element_type=F32)


def attention_kernel(
    chosen_ref, info_ref, q_ref, g_ref, own_k_ref, own_v_ref, near_ref, far_ref, *rest
):
    out_ref, qgrad_ref, own_kg_ref, own_vg_ref, keep_ref, send_ref, accum = rest[-7:]
    slot = pl.program_id(0)
    used = slot < info_ref[0]
    core = info_ref[1]
    prefix_rows = BLOCKS * RESP

    @pl.when(slot == 0)
    def _():
        accum[...] = jnp.zeros_like(accum)

    @pl.when(jnp.logical_not(used))
    def _():
        out_ref[...] = jnp.zeros_like(out_ref)
        qgrad_ref[...] = jnp.zeros_like(qgrad_ref)
        own_kg_ref[...] = jnp.zeros_like(own_kg_ref)
        own_vg_ref[...] = jnp.zeros_like(own_vg_ref)

    @pl.when(used)
    def _():
        ids = [chosen_ref[slot, j] for j in range(BLOCKS)]
        near = jnp.concatenate([near_ref[i] for i in ids], 0)
        far = jnp.concatenate([far_ref[i] for i in ids], 0)
        first = core == 0
        keys = jnp.concatenate([jnp.where(first, near, far), own_k_ref[0]], 0)
        values = jnp.concatenate([jnp.where(first, far, near), own_v_ref[0]], 0)
        q_wide, g_wide = q_ref[0], g_ref[0]
        heads = [slice(r * HD, (r + 1) * HD) for r in range(REPEATS)]
        queries = jnp.concatenate([q_wide[:, h] for h in heads], 0)
        grads = jnp.concatenate([g_wide[:, h] for h in heads], 0)
        key_pos = lax.broadcasted_iota(jnp.int32, (RESP, RESP), 0)
        query_pos = lax.broadcasted_iota(jnp.int32, (RESP, RESP), 1)
        visible = jnp.concatenate([key_pos <= query_pos] * REPEATS, 1)
        scores = dot(keys, queries, NT)
        scores = jnp.concatenate(
            [scores[:prefix_rows], jnp.where(visible, scores[prefix_rows:], -1e30)], 0
        )
        top = jnp.max(scores, 0, keepdims=True)
        expd = jnp.exp2((scores - top) * LOG2_SCALE)
        prob = expd * (1.0 / jnp.sum(expd, 0, keepdims=True))
        prob_b = prob.astype(BF16)
        dprob = dot(values, grads, NT)
        delta = jnp.sum(prob_b.astype(F32) * dprob, 0, keepdims=True)
        dscore = (prob * (dprob - delta)).astype(BF16)
        attended = dot(values.T, prob_b, NN)
        query_grad = dot(keys.T, dscore, NN)
        for r, h in enumerate(heads):
            out_ref[0, :, h] = attended[:, h].T.astype(BF16)
            qgrad_ref[0, :, h] = (query_grad[:, h].T * SCALE).astype(BF16)
        value_grads = dot(prob_b, grads, NN)
        key_grads = dot(dscore, queries, NN) * SCALE
        for j, i in enumerate(ids):
            rows = slice(j * RESP, (j + 1) * RESP)
            accum[i, :, :HD] += key_grads[rows]
            accum[i, :, HD:] += value_grads[rows]
        own_kg_ref[0] = key_grads[prefix_rows:].astype(BF16)
        own_vg_ref[0] = value_grads[prefix_rows:].astype(BF16)

    @pl.when(slot == SLOTS - 1)
    def _():
        for chip in range(N_DP // 2):
            keep_ref[chip] = accum[2 * chip + core].astype(BF16)
            send_ref[chip] = accum[2 * chip + 1 - core].astype(BF16)


def attention(head, chosen, info, queries, out_grad, own, near, far, written):
    wide = pl.BlockSpec((1, RESP, REPEATS * HD), lambda s, *_: (s, 0, head))
    whole = pl.BlockSpec((N_DP, RESP, HD), lambda s, *_: (0, 0, 0))
    narrow = pl.BlockSpec((1, RESP, HD), lambda s, *_: (s, 0, 0))
    shared = pl.BlockSpec((N_DP // 2, RESP, 2 * HD), lambda s, *_: (0, 0, 0))
    in_specs = [
        wide,
        wide,
        pl.BlockSpec((1, RESP, HD), lambda s, *_: (s, 0, head)),
        pl.BlockSpec((1, RESP, HD), lambda s, *_: (s, 0, 2 + head)),
        whole,
        whole,
    ] + [pl.BlockSpec(memory_space=pl.ANY)] * len(written)
    return pl.pallas_call(
        attention_kernel,
        grid_spec=pltpu.PrefetchScalarGridSpec(
            num_scalar_prefetch=2,
            grid=(SLOTS,),
            in_specs=in_specs,
            out_specs=[wide, wide, narrow, narrow, shared, shared],
            scratch_shapes=[pltpu.VMEM((N_DP, RESP, 2 * HD), F32)],
        ),
        out_shape=[
            jax.ShapeDtypeStruct(queries.shape, BF16),
            jax.ShapeDtypeStruct(queries.shape, BF16),
            jax.ShapeDtypeStruct((SLOTS, RESP, HD), BF16),
            jax.ShapeDtypeStruct((SLOTS, RESP, HD), BF16),
            jax.ShapeDtypeStruct((N_DP // 2, RESP, 2 * HD), BF16),
            jax.ShapeDtypeStruct((N_DP // 2, RESP, 2 * HD), BF16),
        ],
        input_output_aliases={8 + i: i for i in range(len(written))},
        cost_estimate=pl.CostEstimate(
            flops=6 * 2 * SLOTS * REPEATS * RESP * (BLOCKS + 1) * RESP * HD,
            bytes_accessed=16 * 2**20,
            transcendentals=SLOTS * REPEATS * RESP * (BLOCKS + 1) * RESP,
        ),
        compiler_params=pltpu.CompilerParams(vmem_limit_bytes=56 * 2**20),
        name="attention",
    )(chosen, info, queries, out_grad, own, own, near, far, *written)


def swap_cores(array):
    return lax.ppermute(array, "c", [(0, 1), (1, 0)])


def exchange(array, axes):
    return lax.all_to_all(array, axes, 0, 0, tiled=True)


def body(
    prompt_hidden, kv_weight, queries, out_grad, own_kv, pack_counts, slot_groups, block_group
):
    width = prompt_hidden.shape[1]
    core = lax.axis_index("c")
    first = core == 0
    me = lax.axis_index(("y", "z", "c"))
    weight = kv_weight.reshape(width, 4 * HD)
    projected = jnp.dot(prompt_hidden, weight, preferred_element_type=F32).astype(BF16)

    keys, values = projected[:, : 2 * HD], projected[:, 2 * HD :]
    kept = jnp.where(first, keys, values)
    got = swap_cores(jnp.where(first, values, keys))
    chip = jnp.concatenate([jnp.where(first, kept, got), jnp.where(first, got, kept)], 0)

    def gather(head):
        piece = chip[:, head * HD : (head + 1) * HD]
        return exchange(jnp.broadcast_to(piece[None], (16, 2 * RESP, HD)), ("y", "z"))

    halves = [gather(head).reshape(N_DP, RESP, HD) for head in range(2)]

    block = jnp.arange(N_DP, dtype=jnp.int32)
    before = (block_group[None, :] < block_group[:, None]) | (
        (block_group[None, :] == block_group[:, None]) & (block[None, :] < block[:, None])
    )
    rank = jnp.sum(before.astype(jnp.int32), 1)
    order = jnp.sum(jnp.where(rank[None, :] == block[:, None], block[None, :], 0), 1)
    mine = lax.dynamic_index_in_dim(slot_groups, me, 0, keepdims=False)
    place = mine[:, None] * BLOCKS + jnp.arange(BLOCKS, dtype=jnp.int32)[None, :]
    chosen = jnp.sum(
        jnp.where(place[:, :, None] == block[None, None, :], order[None, None, :], 0), 2
    )
    count = lax.dynamic_index_in_dim(pack_counts, me, 0, keepdims=False)
    info = jnp.stack([count, core.astype(jnp.int32)])
    own = own_kv.reshape(SLOTS, RESP, 4 * HD)

    share = width // N_DP
    columns = prompt_hidden.reshape(RESP, 4, 8, share).transpose(2, 0, 1, 3)
    columns = columns.reshape(8, RESP, 4 * share)
    columns, halves[0] = lax.optimization_barrier((columns, halves[0]))
    hidden_y = exchange(columns, ("z", "c")).reshape(8 * RESP, 4 * share)

    written = ()
    own_keys, own_values, keeps, sends = [], [], [], []
    for head in range(2):
        near = halves[head]
        outs, qgrads, own_k, own_v, keep, send = attention(
            head, chosen, info, queries, out_grad, own, near, swap_cores(near), written
        )
        written = (outs, qgrads)
        own_keys.append(own_k)
        own_values.append(own_v)
        keeps.append(keep)
        sends.append(send)
    own_grad = jnp.stack(
        [jnp.concatenate(own_keys, 2), jnp.concatenate(own_values, 2)], 2
    )

    partial = [
        (keep.astype(F32) + swap_cores(send).astype(F32)).astype(BF16)
        for keep, send in zip(keeps, sends)
    ]
    partial = jnp.concatenate(
        [p[:, :, :HD] for p in partial] + [p[:, :, HD:] for p in partial], 2
    )
    block_b = jnp.sum(exchange(partial, ("y", "z")).astype(F32), 0).astype(BF16)

    hidden_term = jnp.einsum(
        "pc,xdc->xpd",
        block_b,
        weight.reshape(4, width // 4, 4 * HD),
        preferred_element_type=F32,
    ).astype(BF16)
    prompt_grad = jnp.sum(exchange(hidden_term, "x").astype(F32), 0).astype(BF16)

    line = exchange(jnp.broadcast_to(block_b[None], (4,) + block_b.shape), "z")
    other = swap_cores(line)
    pair = jnp.stack([jnp.where(first, line, other), jnp.where(first, other, line)], 1)
    term = jnp.einsum(
        "pd,pc->dc",
        hidden_y,
        pair.reshape(8 * RESP, 4 * HD),
        preferred_element_type=F32,
    ).astype(BF16)
    weight_grad = jnp.sum(exchange(term.reshape(4, share, 4 * HD), "y").astype(F32), 0)
    return (outs, qgrads, own_grad, weight_grad.reshape(share, 2, 2 * HD), prompt_grad)


def solution(mesh):
    grid = Mesh(mesh.devices.reshape(4, 4, 2, 4), ("y", "z", "c", "x"))
    dp = ("y", "z", "c")
    return jax.shard_map(
        body,
        mesh=grid,
        in_specs=(
            P(dp, None),
            P(None, None, "x"),
            P(dp, None, "x"),
            P(dp, None, "x"),
            P(dp, None, None, "x"),
            P(),
            P(),
            P(),
        ),
        out_specs=(
            P(dp, None, "x"),
            P(dp, None, "x"),
            P(dp, None, None, "x"),
            P(dp, None, "x"),
            P(dp, "x"),
        ),
        check_vma=False,
    )
```

time: 705 us -> 211 us (0.30)
  waiting for transfers between devices: 440 us -> 34.1 us
  local copies, waits for them, and re-layouts: 145 us -> 27.3 us
  blocking collectives: 0 us -> 67.7 us
  matrix products: 54.5 us -> 10.4 us
  Pallas kernels: 0 us -> 35.7 us
  other arithmetic: 34.6 us -> 5.89 us
  starting transfers between devices: 0.16 us -> 25.9 us
  between operations: 14.5 us -> 0.95 us
  loops' own time: 12.2 us -> 0 us
    reduce_scatter x2 -> x0, waiting for transfers between devices: 285 us -> none  [the longest x1 261 us: body(): lax.psum_scatter(accum.reshape(devices * block_rows, 2, kv_width).astype(...]
    unnamed x5 -> x0, waiting for transfers between devices: 108 us -> none
    all_to_all x0 -> x3, blocking collectives: none -> 67.7 us  [exchange(): return lax.all_to_all(array, axes, 0, 0, tiled=True)]
    all_gather x1 -> x0, waiting for transfers between devices: 47.1 us -> none  [body(): lax.all_gather(projected.reshape(block_rows, 2, kv_width), 'dp', axis=0,...]
    pallas_call x0 -> x2, Pallas kernels: none -> 35.7 us  [attention(): pl.pallas_call(attention_kernel, grid_spec=pltpu.PrefetchScalarGridSpec(n...]
    dot_general x23 -> x3, matrix products: 43.2 us -> 10.4 us  [the longest x1 5.36 us: body(): jnp.einsum('pc,xdc->xpd', block_b, weight.reshape(4, width // 4, 4 * HD),...]
    all_to_all x0 -> x4, waiting for transfers between devices: none -> 30.9 us  [exchange(): return lax.all_to_all(array, axes, 0, 0, tiled=True)]
    dynamic_slice x30 -> x1, local copies, waits for them, and re-layouts: 27.3 us -> 0.59 us  [body(): count = lax.dynamic_index_in_dim(pack_counts, me, 0, keepdims=False)]
  transfers between devices with their start and end apart: 4 -> 10, of which waited for: 4 -> 6; matrix products, arithmetic and copies ran while one was open for 2% -> 14% of each run, Pallas kernels for 0% -> 17%
where the time goes in v1:
time: 211 us; the launch traced here: 208 us
  blocking collectives  67.7 us (32%)
  Pallas kernels  35.7 us (17%)
  waiting for transfers between devices  34.1 us (16%)
  local copies, waits for them, and re-layouts  27.3 us (13%)
  starting transfers between devices  25.9 us (12%)
  matrix products  10.4 us (5%)
  other arithmetic  5.89 us (3%)
    all_to_all x3, blocking collectives, exchange(): return lax.all_to_all(array, axes, 0, 0, tiled=True)  67.7 us
    pallas_call x2, Pallas kernels, attention(): pl.pallas_call(attention_kernel, grid_spec=pltpu.PrefetchScalarGridSpec(n...  35.7 us
    all_to_all x4, waiting for transfers between devices, exchange(): return lax.all_to_all(array, axes, 0, 0, tiled=True)  30.9 us
    all_to_all x4, starting transfers between devices, exchange(): return lax.all_to_all(array, axes, 0, 0, tiled=True)  18.7 us
    unnamed x29, local copies, waits for them, and re-layouts  9.76 us
    another operation x1, local copies, waits for them, and re-layouts, body(): weight.reshape(4, width // 4, 4 * HD)  9.19 us
    ppermute x6, starting transfers between devices, swap_cores(): return lax.ppermute(array, 'c', [(0, 1), (1, 0)])  7.24 us
    dot_general x1, matrix products, body(): jnp.einsum('pc,xdc->xpd', block_b, weight.reshape(4, width // 4, 4 * HD),...  5.36 us
  transfers between devices with their start and end apart: 10, of which 6 were waited for; matrix products, arithmetic and copies ran while one was open for 14% of the time, Pallas kernels for 17%

profile of v1, /device:TPU:1, one launch (start us, length us, event | category | flops | bytes accessed | tf_op | source)
XLA Modules:
  0.0 207.9 jit_solution(16807391274365338920)
XLA Ops:
  0.6 5.8 %copy.32 = bf16[640,8,2,256]{3,1,2,0:T(8,128)(2,1)} copy(bf16[640,8,2,256]{3,2,1,0:T(2,128)(2,1)} %bitcast.32) | data formatting | bytes 10485760
  6.4 3.3 %convolution_convert_fusion.2 = bf16[128,512]{1,0:T(8,128)(2,1)S(1)} fusion(bf16[128,5120]{1,0:T(8,128)(2,1)S(1)} %copy-done, bf16[5120,512]{1,0:T(8,128)(2,1)} %bitcast.33), kind=kOutput, calls=%fused_computation.7 | convolution fusion | flops 671154176 | bytes 6684672 | tf_op jit(solution)/shard_map/dot_general | solution.py:155
  9.8 1.5 collective-permute-start
  11.3 0.9 collective-permute-done
  12.2 0.2 broadcast_in_dim.28
  12.4 23.7 %all_to_all.35 = bf16[16,256,128]{2,1,0:T(8,128)(2,1)} all-to-all(bf16[16,256,128]{2,1,0:T(8,128)(2,1)S(1)} %broadcast_in_dim.28), channel_id=1, replica_groups=mesh['y'=4,'z'=4,'c'=2,'x'=4] {'y','z'}, dimensions={0} | all-to-all | bytes 2097152 | tf_op jit(solution)/shard_map/all_to_all | solution.py:144
  36.2 1.2 broadcast_in_dim.27
  37.3 4.3 %all-to-all-start = ((bf16[16,256,128]{2,1,0:T(8,128)(2,1)}), bf16[16,256,128]{2,1,0:T(8,128)(2,1)}, u32[]{:S(2)}, u32[]{:S(2)}) async-start(bf16[16,256,128]{2,1,0:T(8,128)(2,1)} %broadcast_in_dim.27), calls=%async_computation | async-start | bytes 2097152 | tf_op jit(solution)/shard_map/all_to_all | solution.py:144
  41.7 0.8 copy.25
  42.5 1.2 copy.26
  43.8 2.1 %collective-permute-start.2 = (bf16[32,128,128]{2,1,0:T(8,128)(2,1)}, bf16[32,128,128]{2,1,0:T(8,128)(2,1)}, u32[]{:S(2)}, u32[]{:S(2)}) collective-permute-start(bf16[32,128,128]{2,1,0:T(8,128)(2,1)} %bitcast.5.near_ref), channel_id=1, source_target_pairs={{0,4},{4,0},{1,5},{5,1},{2,6},{6,2},{3,7},{7,3},{8,12},{12,8},{9,1... | collective-permute-start | bytes 3145736 | tf_op jit(solution)/shard_map/ppermute | solution.py:140
  45.8 0.2 convert_reduce_fusion.1
  46.0 10.5 %all-to-all-done = bf16[16,256,128]{2,1,0:T(8,128)(2,1)} async-done(((bf16[16,256,128]{2,1,0:T(8,128)(2,1)}), bf16[16,256,128]{2,1,0:T(8,128)(2,1)}, u32[]{:S(2)}, u32[]{:S(2)}) %all-to-all-start) | async-done | bytes 1048608 | tf_op jit(solution)/shard_map/all_to_all | solution.py:144
  56.6 3.2 %collective-permute-start.1 = (bf16[32,128,128]{2,1,0:T(8,128)(2,1)}, bf16[32,128,128]{2,1,0:T(8,128)(2,1)S(1)}, u32[]{:S(2)}, u32[]{:S(2)}) collective-permute-start(bf16[32,128,128]{2,1,0:T(8,128)(2,1)} %bitcast.1.near_ref), channel_id=1, source_target_pairs={{0,4},{4,0},{1,5},{5,1},{2,6},{6,2},{3,7},{7,3},{8,12},{12,8},{9,1... | collective-permute-start | bytes 3145736 | tf_op jit(solution)/shard_map/ppermute | solution.py:140
  59.9 0.6 dynamic_slice.9
  60.5 0.2 multiply_reduce_fusion
  60.7 0.2 select_reduce_fusion
  60.9 0.7 copy.28.chosen_ref
  61.6 1.5 reshape.77.own_k_ref.own_v_ref
  63.0 1.3 pad_add_fusion.info_ref
  64.3 17.8 %attention.2 = (bf16[8,128,1280]{2,1,0:T(8,128)(2,1)}, bf16[8,128,1280]{2,1,0:T(8,128)(2,1)}, bf16[8,128,128]{2,1,0:T(8,128)(2,1)}, bf16[8,128,128]{2,1,0:T(8,12...) custom-call(s32[8,4]{1,0:T(8,128)} %copy.28.chosen_ref, s32[2]{0:T(128)} %pad_add_fusion.info_ref, ...), custom_call_target="tpu_custom_call" | custom-call | flops 5033164800 | bytes 16777216 | tf_op jit(solution)/shard_map/attention/pallas_call | solution.py:111
  82.2 0.9 copy-done.10
  83.2 17.9 %attention.3 = (bf16[8,128,1280]{2,1,0:T(8,128)(2,1)}, bf16[8,128,1280]{2,1,0:T(8,128)(2,1)}, bf16[8,128,128]{2,1,0:T(8,128)(2,1)}, bf16[8,128,128]{2,1,0:T(8,12...) custom-call(s32[8,4]{1,0:T(8,128)} %copy.28.chosen_ref, ...), custom_call_target="tpu_custom_call", output_to_operand_aliasing={{0}: (8, {}), {1}: (9, {})} | custom-call | flops 5033164800 | bytes 16777216 | tf_op jit(solution)/shard_map/attention/pallas_call | solution.py:111
  101.2 0.3 add_convert_fusion.1
  101.5 0.3 fusion.5
  101.8 2.2 %collective-permute-done.4 = bf16[16,128,256]{2,1,0:T(8,128)(2,1)S(1)} collective-permute-done((bf16[16,128,256]{2,1,0:T(8,128)(2,1)}, bf16[16,128,256]{2,1,0:T(8,128)(2,1)S(1)}, u32[]{:S(2)}, u32[]{:S(2)}) %collective-permute-start.4) | collective-permute-done | bytes 1048608 | tf_op jit(solution)/shard_map/ppermute | solution.py:140
  104.0 0.3 add_convert_fusion
  104.4 0.3 fusion.6
  104.7 0.3 pad_maximum_fusion
  105.0 34.4 %all_to_all.36 = bf16[16,128,512]{2,1,0:T(8,128)(2,1)S(1)} all-to-all(bf16[16,128,512]{2,1,0:T(8,128)(2,1)S(1)} %pad_maximum_fusion), channel_id=1, replica_groups=mesh['y'=4,'z'=4,'c'=2,'x'=4] {'y','z'}, dimensions={0} | all-to-all | bytes 4194304 | tf_op jit(solution)/shard_map/all_to_all | solution.py:144
  139.4 0.3 reduce_sum.63
  139.7 9.6 %all_to_all.37 = bf16[4,128,512]{2,1,0:T(8,128)(2,1)S(1)} all-to-all(bf16[4,128,512]{2,1,0:T(8,128)(2,1)S(1)} %broadcast_in_dim.29), channel_id=1, replica_groups=mesh['y'=4,'z'=4,'c'=2,'x'=4] {'z'}, dimensions={0} | all-to-all | bytes 1048576 | tf_op jit(solution)/shard_map/all_to_all | solution.py:144
  149.3 6.8 %all-to-all-start.2 = ((bf16[8,128,640]{1,2,0:T(8,128)(2,1)}), bf16[8,128,640]{1,2,0:T(8,128)(2,1)S(1)}, u32[]{:S(2)}, u32[]{:S(2)}) async-start(bf16[8,128,640]{1,2,0:T(8,128)(2,1)} %bitcast.4), calls=%async_computation.2 | async-start | bytes 2621440 | tf_op jit(solution)/shard_map/all_to_all | solution.py:144
  156.1 9.2 %reshape_reshape.3 = bf16[4,1280,512]{2,1,0:T(8,128)(2,1)} reshape(bf16[5120,2,256]{2,1,0:T(2,128)(2,1)} %param.9) | data formatting | bytes 10485760 | tf_op jit(solution)/shard_map/reshape;reshape | solution.py:217
  165.3 0.3 collective-permute-start.5
  165.6 5.4 %fusion = bf16[4,128,1280]{2,1,0:T(8,128)(2,1)} fusion(bf16[4,1280,512]{2,1,0:T(8,128)(2,1)} %reshape_reshape.3, bf16[128,512]{1,0:T(8,128)(2,1)S(1)} %reduce_sum.63), kind=kOutput, calls=%fused_computation.1 | convolution fusion | flops 671744000 | bytes 6684672 | tf_op jit(solution)/shard_map/pc,xdc->xpd/dot_general | solution.py:214
  171.0 3.1 %all-to-all-done.2 = bf16[8,128,640]{1,2,0:T(8,128)(2,1)S(1)} async-done(((bf16[8,128,640]{1,2,0:T(8,128)(2,1)}), bf16[8,128,640]{1,2,0:T(8,128)(2,1)S(1)}, u32[]{:S(2)}, u32[]{:S(2)}) %all-to-all-start.2) | async-done | bytes 1310752 | tf_op jit(solution)/shard_map/all_to_all | solution.py:144
  174.1 4.0 %all-to-all-start.6 = ((bf16[4,128,1280]{2,1,0:T(8,128)(2,1)}), bf16[4,128,1280]{2,1,0:T(8,128)(2,1)S(1)}, u32[]{:S(2)}, u32[]{:S(2)}) async-start(bf16[4,128,1280]{2,1,0:T(8,128)(2,1)} %fusion), calls=%async_computation.6 | async-start | bytes 2621440 | tf_op jit(solution)/shard_map/all_to_all | solution.py:144
  178.1 1.4 copy.29
  179.6 1.2 select_bitcast_fusion.1
  181.0 1.7 convolution_convert_fusion.1
  182.7 12.1 %all-to-all-done.6 = bf16[4,128,1280]{2,1,0:T(8,128)(2,1)S(1)} async-done(((bf16[4,128,1280]{2,1,0:T(8,128)(2,1)}), bf16[4,128,1280]{2,1,0:T(8,128)(2,1)S(1)}, u32[]{:S(2)}, u32[]{:S(2)}) %all-to-all-start.6) | async-done | bytes 1310752 | tf_op jit(solution)/shard_map/all_to_all | solution.py:144
  194.9 3.5 %all-to-all-start.5 = ((bf16[4,160,512]{2,1,0:T(8,128)(2,1)}), bf16[4,160,512]{2,1,0:T(8,128)(2,1)S(1)}, u32[]{:S(2)}, u32[]{:S(2)}) async-start(bf16[4,160,512]{2,1,0:T(8,128)(2,1)} %bitcast.13), calls=%async_computation.5 | async-start | bytes 1310720 | tf_op jit(solution)/shard_map/all_to_all | solution.py:144
  198.4 0.1 maximum_bitcast_fusion
  198.7 2.0 copy.31
  200.7 1.0 reduce_sum.65
  201.7 5.2 %all-to-all-done.5 = bf16[4,160,512]{2,1,0:T(8,128)(2,1)S(1)} async-done(((bf16[4,160,512]{2,1,0:T(8,128)(2,1)}), bf16[4,160,512]{2,1,0:T(8,128)(2,1)S(1)}, u32[]{:S(2)}, u32[]{:S(2)}) %all-to-all-start.5) | async-done | bytes 655392 | tf_op jit(solution)/shard_map/all_to_all | solution.py:144
  207.0 0.9 reshape.86
  (40 shorter events, 0.9 us)
Async XLA Ops:
  0.6 5.8 %copy-start = (bf16[128,5120]{1,0:T(8,128)(2,1)S(1)}, bf16[128,5120]{1,0:T(8,128)(2,1)}, u32[]{:S(2)}) copy-start(bf16[128,5120]{1,0:T(8,128)(2,1)} %param.8) | copy-start | bytes 3932164
  9.8 2.4 %collective-permute-start = (bf16[128,256]{1,0:T(8,128)(2,1)S(1)}, bf16[128,256]{1,0:T(8,128)(2,1)S(1)}, u32[]{:S(2)}, u32[]{:S(2)}) collective-permute-start(bf16[128,256]{1,0:T(8,128)(2,1)S(1)} %broadcast_select_fusion.2), channel_id=1, source_target_pairs={{0,4},{4,0},{1,5},{5,1},{2,6},{6,2},{3,7},{7,3},{8,12},{12,8},{9,1... | collective-permute-start | bytes 196616 | tf_op jit(solution)/shard_map/ppermute | solution.py:140
  37.3 19.2 %all-to-all-start = ((bf16[16,256,128]{2,1,0:T(8,128)(2,1)}), bf16[16,256,128]{2,1,0:T(8,128)(2,1)}, u32[]{:S(2)}, u32[]{:S(2)}) async-start(bf16[16,256,128]{2,1,0:T(8,128)(2,1)} %broadcast_in_dim.27), calls=%async_computation | async-start | bytes 2097152 | tf_op jit(solution)/shard_map/all_to_all | solution.py:144
  41.7 4.1 %copy-start.11 = (s32[32]{0:T(128)S(1)}, s32[32]{0:T(128)}, u32[]{:S(2)}) copy-start(s32[32]{0:T(128)} %param.15) | copy-start | bytes 388
  41.7 18.2 %copy-start.12 = (s32[32]{0:T(128)S(1)}, s32[32]{0:T(128)}, u32[]{:S(2)}) copy-start(s32[32]{0:T(128)} %param.13) | copy-start | bytes 388
  41.7 18.8 %copy-start.9 = (s32[32,8]{0,1:T(8,128)S(1)}, s32[32,8]{0,1:T(8,128)}, u32[]{:S(2)}) copy-start(s32[32,8]{0,1:T(8,128)} %param.14) | copy-start | bytes 3076
  42.5 19.1 %copy-start.4 = (bf16[8,128,2,256]{3,2,1,0:T(2,128)(2,1)S(1)}, bf16[8,128,2,256]{3,2,1,0:T(2,128)(2,1)}, u32[]{:S(2)}) copy-start(bf16[8,128,2,256]{3,2,1,0:T(2,128)(2,1)} %param.12) | copy-start | bytes 3145732
  43.8 20.6 %collective-permute-start.2 = (bf16[32,128,128]{2,1,0:T(8,128)(2,1)}, bf16[32,128,128]{2,1,0:T(8,128)(2,1)}, u32[]{:S(2)}, u32[]{:S(2)}) collective-permute-start(bf16[32,128,128]{2,1,0:T(8,128)(2,1)} %bitcast.5.near_ref), channel_id=1, source_target_pairs={{0,4},{4,0},{1,5},{5,1},{2,6},{6,2},{3,7},{7,3},{8,12},{12,8},{9,1... | collective-permute-start | bytes 3145736 | tf_op jit(solution)/shard_map/ppermute | solution.py:140
  56.6 25.6 %collective-permute-start.1 = (bf16[32,128,128]{2,1,0:T(8,128)(2,1)}, bf16[32,128,128]{2,1,0:T(8,128)(2,1)S(1)}, u32[]{:S(2)}, u32[]{:S(2)}) collective-permute-start(bf16[32,128,128]{2,1,0:T(8,128)(2,1)} %bitcast.1.near_ref), channel_id=1, source_target_pairs={{0,4},{4,0},{1,5},{5,1},{2,6},{6,2},{3,7},{7,3},{8,12},{12,8},{9,1... | collective-permute-start | bytes 3145736 | tf_op jit(solution)/shard_map/ppermute | solution.py:140
  82.1 19.1 %collective-permute-start.3 = (bf16[16,128,256]{2,1,0:T(8,128)(2,1)}, bf16[16,128,256]{2,1,0:T(8,128)(2,1)S(1)}, u32[]{:S(2)}, u32[]{:S(2)}) collective-permute-start(bf16[16,128,256]{2,1,0:T(8,128)(2,1)} %get-tuple-element.30), channel_id=1, source_target_pairs={{0,4},{4,0},{1,5},{5,1},{2,6},{6,2},{3,7},{7,3},{8,12},{12,8},{9,1... | collective-permute-start | bytes 3145736 | tf_op jit(solution)/shard_map/ppermute | solution.py:140
  82.2 1.0 copy-start.10
  83.2 18.0 %copy-start.2 = (bf16[16,128,256]{2,1,0:T(8,128)(2,1)S(1)}, bf16[16,128,256]{2,1,0:T(8,128)(2,1)}, u32[]{:S(2)}) copy-start(bf16[16,128,256]{2,1,0:T(8,128)(2,1)} %get-tuple-element.29) | copy-start | bytes 3145732
  101.1 3.0 %collective-permute-start.4 = (bf16[16,128,256]{2,1,0:T(8,128)(2,1)}, bf16[16,128,256]{2,1,0:T(8,128)(2,1)S(1)}, u32[]{:S(2)}, u32[]{:S(2)}) collective-permute-start(bf16[16,128,256]{2,1,0:T(8,128)(2,1)} %get-tuple-element.32), channel_id=1, source_target_pairs={{0,4},{4,0},{1,5},{5,1},{2,6},{6,2},{3,7},{7,3},{8,12},{12,8},{9,1... | collective-permute-start | bytes 3145736 | tf_op jit(solution)/shard_map/ppermute | solution.py:140
  101.2 2.8 %copy-start.3 = (bf16[16,128,256]{2,1,0:T(8,128)(2,1)S(1)}, bf16[16,128,256]{2,1,0:T(8,128)(2,1)}, u32[]{:S(2)}) copy-start(bf16[16,128,256]{2,1,0:T(8,128)(2,1)} %get-tuple-element.31) | copy-start | bytes 3145732
  149.3 24.8 %all-to-all-start.2 = ((bf16[8,128,640]{1,2,0:T(8,128)(2,1)}), bf16[8,128,640]{1,2,0:T(8,128)(2,1)S(1)}, u32[]{:S(2)}, u32[]{:S(2)}) async-start(bf16[8,128,640]{1,2,0:T(8,128)(2,1)} %bitcast.4), calls=%async_computation.2 | async-start | bytes 2621440 | tf_op jit(solution)/shard_map/all_to_all | solution.py:144
  165.3 14.2 %collective-permute-start.5 = (bf16[4,128,512]{2,1,0:T(8,128)(2,1)S(1)}, bf16[4,128,512]{2,1,0:T(8,128)(2,1)}, u32[]{:S(2)}, u32[]{:S(2)}) collective-permute-start(bf16[4,128,512]{2,1,0:T(8,128)(2,1)S(1)} %all_to_all.37), channel_id=1, source_target_pairs={{0,4},{4,0},{1,5},{5,1},{2,6},{6,2},{3,7},{7,3},{8,12},{12,8},{9,1... | collective-permute-start | bytes 1572872 | tf_op jit(solution)/shard_map/ppermute | solution.py:140
  174.1 20.8 %all-to-all-start.6 = ((bf16[4,128,1280]{2,1,0:T(8,128)(2,1)}), bf16[4,128,1280]{2,1,0:T(8,128)(2,1)S(1)}, u32[]{:S(2)}, u32[]{:S(2)}) async-start(bf16[4,128,1280]{2,1,0:T(8,128)(2,1)} %fusion), calls=%async_computation.6 | async-start | bytes 2621440 | tf_op jit(solution)/shard_map/all_to_all | solution.py:144
  179.5 1.5 copy-start.1
  181.0 17.4 %copy-start.5 = (bf16[8,128,128]{2,1,0:T(8,128)(2,1)S(1)}, bf16[8,128,128]{2,1,0:T(8,128)(2,1)}, u32[]{:S(2)}) copy-start(bf16[8,128,128]{2,1,0:T(8,128)(2,1)} %get-tuple-element.24) | copy-start | bytes 786436
  181.0 17.4 %copy-start.6 = (bf16[8,128,128]{2,1,0:T(8,128)(2,1)S(1)}, bf16[8,128,128]{2,1,0:T(8,128)(2,1)}, u32[]{:S(2)}) copy-start(bf16[8,128,128]{2,1,0:T(8,128)(2,1)} %get-tuple-element.26) | copy-start | bytes 786436
  181.0 17.4 %copy-start.7 = (bf16[8,128,128]{2,1,0:T(8,128)(2,1)S(1)}, bf16[8,128,128]{2,1,0:T(8,128)(2,1)}, u32[]{:S(2)}) copy-start(bf16[8,128,128]{2,1,0:T(8,128)(2,1)} %get-tuple-element.25) | copy-start | bytes 786436
  181.0 17.4 %copy-start.8 = (bf16[8,128,128]{2,1,0:T(8,128)(2,1)S(1)}, bf16[8,128,128]{2,1,0:T(8,128)(2,1)}, u32[]{:S(2)}) copy-start(bf16[8,128,128]{2,1,0:T(8,128)(2,1)} %get-tuple-element.27) | copy-start | bytes 786436
  194.9 12.0 %all-to-all-start.5 = ((bf16[4,160,512]{2,1,0:T(8,128)(2,1)}), bf16[4,160,512]{2,1,0:T(8,128)(2,1)S(1)}, u32[]{:S(2)}, u32[]{:S(2)}) async-start(bf16[4,160,512]{2,1,0:T(8,128)(2,1)} %bitcast.13), calls=%async_computation.5 | async-start | bytes 1310720 | tf_op jit(solution)/shard_map/all_to_all | solution.py:144

commit v2 on v1

v2 whole, which is shorter than its diff:
```python
import functools
import math

import jax
import jax.numpy as jnp
from jax import lax
from jax.experimental import pallas as pl
from jax.experimental.pallas import tpu as pltpu
from jax.sharding import Mesh, PartitionSpec as P

HD = 128
GROUP = 16
GROUPS = 8
BLOCKS = 4
SLOTS = 8
RESP = 128
REPEATS = 5
N_DP = 32
F32 = jnp.float32
BF16 = jnp.bfloat16
SCALE = 1.0 / math.sqrt(HD)
LOG2_SCALE = SCALE * math.log2(math.e)
NT = (((1,), (1,)), ((), ()))
NN = (((1,), (0,)), ((), ()))


def dot(a, b, dims):
    return lax.dot_general(a, b, dims, preferred_element_type=F32)


def attention_kernel(
    pack_counts, slot_groups, block_group, queries_hbm, grads_hbm, own_hbm, near, far,
    out_hbm, qgrad_hbm, own_grad_hbm, keep_hbm, send_hbm,
    queries, grads, out, qgrad, own, own_grad, keep, send, accum,
    expd_0, expd_1, inverse_0, inverse_1, order, filled, sems,
):
    core = lax.axis_index("c")
    me = (lax.axis_index("y") * 4 + lax.axis_index("z")) * 2 + core
    count = pack_counts[me]
    first = core == 0
    prefix_rows = BLOCKS * RESP
    states = ((expd_0, inverse_0), (expd_1, inverse_1))

    def loads(slot):
        return (
            pltpu.make_async_copy(queries_hbm.at[slot], queries.at[slot], sems.at[2, slot]),
            pltpu.make_async_copy(grads_hbm.at[slot], grads.at[slot], sems.at[3, slot]),
            pltpu.make_async_copy(own_hbm.at[slot], own.at[slot], sems.at[4, slot]),
        )

    def stores(slot):
        return (
            pltpu.make_async_copy(out.at[slot], out_hbm.at[slot], sems.at[0, slot]),
            pltpu.make_async_copy(qgrad.at[slot], qgrad_hbm.at[slot], sems.at[1, slot]),
            pltpu.make_async_copy(own_grad.at[slot], own_grad_hbm.at[slot], sems.at[5, slot]),
        )

    @pl.loop(0, jnp.minimum(count, 2))
    def _(slot):
        for copy in loads(slot):
            copy.start()

    for group in range(GROUPS):
        filled[group] = 0

    @pl.loop(0, N_DP)
    def _(block):
        group = block_group[block]
        order[group * BLOCKS + filled[group]] = block
        filled[group] = filled[group] + 1

    accum[...] = jnp.zeros_like(accum)

    @pl.loop(count, SLOTS)
    def _(slot):
        out[slot] = jnp.zeros(out.shape[1:], BF16)
        qgrad[slot] = jnp.zeros(qgrad.shape[1:], BF16)
        own_grad[slot] = jnp.zeros(own_grad.shape[1:], BF16)
        for copy in stores(slot):
            copy.start()

    key_pos = lax.broadcasted_iota(jnp.int32, (RESP, RESP), 0)
    query_pos = lax.broadcasted_iota(jnp.int32, (RESP, RESP), 1)

    def columns(part):
        return slice(part * HD, (part + 1) * HD)

    def blocks_of(slot):
        group = slot_groups[slot, me]
        return [order[group * BLOCKS + j] for j in range(BLOCKS)]

    def keys_values(slot, head):
        ids, cols = blocks_of(slot), columns(head)
        ours = jnp.concatenate([near[i, :, cols] for i in ids], 0)
        theirs = jnp.concatenate([far[i, :, cols] for i in ids], 0)
        keys, values = jnp.where(first, ours, theirs), jnp.where(first, theirs, ours)
        return (
            jnp.concatenate([keys, own[slot, :, cols]], 0),
            jnp.concatenate([values, own[slot, :, columns(2 + head)]], 0),
        )

    def query_rows(slot, head):
        return jnp.concatenate(
            [queries[slot, :, columns(head * REPEATS + r)] for r in range(REPEATS)], 0
        )

    def softmax(slot, head):
        expd_ref, inverse_ref = states[head]
        keys, _ = keys_values(slot, head)
        scores = dot(keys, query_rows(slot, head), NT)
        yield
        visible = jnp.concatenate([key_pos <= query_pos] * REPEATS, 1)
        scores = jnp.concatenate(
            [scores[:prefix_rows], jnp.where(visible, scores[prefix_rows:], -1e30)], 0
        )
        top = jnp.max(scores, 0, keepdims=True)
        yield
        expd = jnp.exp2((scores - top) * LOG2_SCALE)
        expd_ref[...] = expd.astype(BF16)
        yield
        inverse_ref[...] = 1.0 / jnp.sum(expd, 0, keepdims=True)

    def gradients(slot, head):
        expd_ref, inverse_ref = states[head]
        keys, values = keys_values(slot, head)
        expd, inverse = expd_ref[...], inverse_ref[...]
        attended = dot(values.T, expd, NN) * inverse
        scaled = jnp.concatenate(
            [grads[slot, :, columns(head * REPEATS + r)].T for r in range(REPEATS)], 1
        )
        scaled = (scaled.astype(F32) * inverse).astype(BF16)
        yield
        delta = jnp.sum(scaled.astype(F32) * attended, 0, keepdims=True)
        dprob = dot(values, scaled, NN)
        yield
        dscore = expd * (dprob - delta).astype(BF16)
        value_grads = dot(expd, scaled, NT)
        yield
        query_grad = dot(keys.T, dscore, NN) * SCALE
        key_grads = dot(dscore, query_rows(slot, head), NN) * SCALE
        yield
        for r in range(REPEATS):
            rows = slice(r * RESP, (r + 1) * RESP)
            cols = columns(head * REPEATS + r)
            out[slot, :, cols] = attended[:, rows].T.astype(BF16)
            qgrad[slot, :, cols] = query_grad[:, rows].T.astype(BF16)
        for j, i in enumerate(blocks_of(slot)):
            rows = slice(j * RESP, (j + 1) * RESP)
            accum[i, :, columns(head)] += key_grads[rows]
            accum[i, :, columns(2 + head)] += value_grads[rows]
        own_grad[slot, :, columns(head)] = key_grads[prefix_rows:].astype(BF16)
        own_grad[slot, :, columns(2 + head)] = value_grads[prefix_rows:].astype(BF16)

    def together(*parts):
        parts = list(parts)
        while parts:
            parts = [part for part in parts if next(part, part) is None]

    @pl.when(count > 0)
    def _():
        for copy in loads(0):
            copy.wait()
        together(softmax(0, 0))

    @pl.loop(0, count)
    def _(slot):
        later = jnp.minimum(slot + 1, count - 1)

        @pl.when(slot + 2 < count)
        def _():
            for copy in loads(slot + 2):
                copy.start()

        @pl.when(later > slot)
        def _():
            for copy in loads(later):
                copy.wait()

        together(gradients(slot, 0), softmax(slot, 1))
        together(gradients(slot, 1), softmax(later, 0))
        for copy in stores(slot):
            copy.start()

    halves = []
    for place, (half, half_hbm, mine) in enumerate(
        ((send, send_hbm, 1 - core), (keep, keep_hbm, core))
    ):
        for part in range(4):
            chips = pl.ds(4 * part, 4)
            for chip in range(4 * part, 4 * part + 4):
                half[chip] = accum[2 * chip + mine].astype(BF16)
            copy = pltpu.make_async_copy(
                half.at[chips], half_hbm.at[chips], sems.at[6 + place, part]
            )
            copy.start()
            halves.append(copy)

    @pl.loop(0, SLOTS)
    def _(slot):
        for copy in stores(slot):
            copy.wait()

    for copy in halves:
        copy.wait()


def after_kernel(*refs):
    del refs


def after(array, tokens, space):
    anywhere = pl.BlockSpec(memory_space=pl.ANY)
    spec = pl.BlockSpec(memory_space=space)
    return pl.pallas_call(
        after_kernel,
        in_specs=[spec] + [anywhere] * len(tokens),
        out_specs=spec,
        out_shape=space(array.shape, array.dtype),
        input_output_aliases={0: 0},
        compiler_params=pltpu.CompilerParams(vmem_limit_bytes=2**20),
        name="after",
    )(
        pltpu.with_memory_space_constraint(array, space),
        *tokens,
    )


def columns_kernel(hidden, columns):
    share = hidden.shape[1] // N_DP
    for part in range(8):
        for y in range(4):
            start = (8 * y + part) * share
            columns[part, y * share : (y + 1) * share] = hidden[:, start : start + share].T


def columns_of(hidden):
    rows, width = hidden.shape
    return pl.pallas_call(
        columns_kernel,
        out_shape=jax.ShapeDtypeStruct((8, width // 8, rows), BF16),
        compiler_params=pltpu.CompilerParams(vmem_limit_bytes=8 * 2**20),
        name="columns",
    )(hidden)


def total_kernel(parts, total, copies):
    summed = parts[0].astype(F32)
    for i in range(1, parts.shape[0]):
        summed = summed + parts[i].astype(F32)
    summed = summed.astype(BF16)
    total[...] = summed
    for i in range(copies.shape[0]):
        copies[i] = summed


def total_of(parts):
    shape = parts.shape[1:]
    return pl.pallas_call(
        total_kernel,
        out_shape=[
            jax.ShapeDtypeStruct(shape, BF16),
            jax.ShapeDtypeStruct((4,) + shape, BF16),
        ],
        compiler_params=pltpu.CompilerParams(vmem_limit_bytes=8 * 2**20),
        name="total",
    )(parts)


def term_kernel(hidden, line, other, *refs):
    *parts, terms = refs
    first = lax.axis_index("c") == 0
    total = None
    for z in range(4):
        ours, theirs = line[z], other[z]
        pair = jnp.concatenate(
            [jnp.where(first, ours, theirs), jnp.where(first, theirs, ours)], 0
        )
        both = jnp.concatenate([hidden[2 * z], hidden[2 * z + 1]], 1)
        part = dot(both, pair, NN)
        total = part if total is None else total + part
    terms[...] = total
    share = parts[0].shape[0]
    here = lax.axis_index("y")
    for step, part in enumerate(parts):
        start = pl.multiple_of(lax.rem(here + step, 4) * share, share)
        part[...] = terms[pl.ds(start, share)].astype(BF16)


def term_of(hidden, line, other):
    width, columns = hidden.shape[1], line.shape[2]
    return pl.pallas_call(
        term_kernel,
        out_shape=[jax.ShapeDtypeStruct((width // 4, columns), BF16)] * 4,
        scratch_shapes=[pltpu.VMEM((width, columns), F32)],
        compiler_params=pltpu.CompilerParams(vmem_limit_bytes=12 * 2**20),
        name="term",
    )(hidden, line, other)


def prompt_kernel(block, weight_hbm, terms, weight, sems):
    rows = terms.shape[2]
    copies = [
        pltpu.make_async_copy(
            weight_hbm.at[:, pl.ds(x * rows, rows)], weight.at[x], sems.at[x]
        )
        for x in range(4)
    ]
    for copy in copies:
        copy.start()
    for x, copy in enumerate(copies):
        copy.wait()
        terms[x] = (
            dot(block[:, : 2 * HD], weight[x, 0], NT)
            + dot(block[:, 2 * HD :], weight[x, 1], NT)
        ).astype(BF16)


def prompt_terms(block, weight):
    shape = (4, block.shape[0], weight.shape[1] // 4)
    return pl.pallas_call(
        prompt_kernel,
        out_shape=jax.ShapeDtypeStruct(shape, BF16),
        in_specs=[
            pl.BlockSpec(memory_space=pltpu.VMEM),
            pl.BlockSpec(memory_space=pl.ANY),
        ],
        scratch_shapes=[
            pltpu.VMEM((4, 2, shape[2], 2 * HD), BF16),
            pltpu.SemaphoreType.DMA((4,)),
        ],
        cost_estimate=pl.CostEstimate(
            flops=8 * shape[1] * shape[2] * 4 * HD, bytes_accessed=2**22, transcendentals=0
        ),
        compiler_params=pltpu.CompilerParams(vmem_limit_bytes=16 * 2**20),
        name="prompt",
    )(block, in_hbm(weight))


def sum_kernel(*refs):
    *parts, result = refs
    total = None
    for part in parts:
        values = [part[i] for i in range(part.shape[0])] if part.ndim == 3 else [part[...]]
        for value in values:
            value = value.astype(F32)
            total = value if total is None else total + value
    result[...] = total.astype(result.dtype)


def sum_of(parts, dtype):
    return pl.pallas_call(
        sum_kernel,
        out_shape=jax.ShapeDtypeStruct(parts[0].shape[-2:], dtype),
        compiler_params=pltpu.CompilerParams(vmem_limit_bytes=8 * 2**20),
        name="sum",
    )(*parts)


def attention(pack_counts, slot_groups, block_group, queries, out_grad, own, near, far):
    vmem = pl.BlockSpec(memory_space=pltpu.VMEM)
    smem = pl.BlockSpec(memory_space=pltpu.SMEM)
    anywhere = pl.BlockSpec(memory_space=pl.ANY)
    rows = BLOCKS * RESP + RESP
    shared = (N_DP // 2, RESP, 4 * HD)
    outer = [in_hbm(array) for array in (queries, out_grad, own)]
    inner = [pltpu.with_memory_space_constraint(array, pltpu.VMEM) for array in (near, far)]
    return pl.pallas_call(
        attention_kernel,
        in_specs=[smem] * 3 + [anywhere] * 3 + [vmem] * 2,
        out_specs=[anywhere] * 5,
        out_shape=[
            pltpu.HBM(queries.shape, BF16),
            pltpu.HBM(queries.shape, BF16),
            pltpu.HBM(own.shape, BF16),
            pltpu.HBM(shared, BF16),
            pltpu.HBM(shared, BF16),
        ],
        scratch_shapes=[pltpu.VMEM(queries.shape, BF16)] * 4
        + [pltpu.VMEM(own.shape, BF16)] * 2
        + [pltpu.VMEM(shared, BF16)] * 2
        + [
            pltpu.VMEM((N_DP, RESP, 4 * HD), F32),
            pltpu.VMEM((rows, REPEATS * RESP), BF16),
            pltpu.VMEM((rows, REPEATS * RESP), BF16),
            pltpu.VMEM((1, REPEATS * RESP), F32),
            pltpu.VMEM((1, REPEATS * RESP), F32),
            pltpu.SMEM((N_DP,), jnp.int32),
            pltpu.SMEM((GROUPS,), jnp.int32),
            pltpu.SemaphoreType.DMA((8, SLOTS)),
        ],
        cost_estimate=pl.CostEstimate(
            flops=6 * 2 * 2 * SLOTS * REPEATS * RESP * rows * HD,
            bytes_accessed=16 * 2**20,
            transcendentals=2 * SLOTS * REPEATS * RESP * rows,
        ),
        compiler_params=pltpu.CompilerParams(vmem_limit_bytes=40 * 2**20),
        name="attention",
    )(pack_counts, slot_groups.T, block_group, *outer, *inner)


def in_hbm(array):
    return pltpu.with_memory_space_constraint(array, pltpu.HBM)


def swap_cores(array):
    return lax.ppermute(array, "c", [(0, 1), (1, 0)])


def exchange(array, axes):
    return lax.all_to_all(array, axes, 0, 0, tiled=True)


def body(
    prompt_hidden, kv_weight, queries, out_grad, own_kv, pack_counts, slot_groups, block_group
):
    width = prompt_hidden.shape[1]
    core = lax.axis_index("c")
    first = core == 0

    projected = jnp.einsum(
        "pd,dkc->pkc", prompt_hidden, kv_weight, preferred_element_type=F32
    ).astype(BF16)

    keys, values = projected[:, 0], projected[:, 1]
    kept = jnp.where(first, keys, values)
    got = swap_cores(jnp.where(first, values, keys))
    piece = jnp.concatenate([jnp.where(first, kept, got), jnp.where(first, got, kept)], 0)
    piece = jnp.broadcast_to(piece[None], (16, 2 * RESP, 2 * HD))
    near = exchange(piece, ("y", "z")).reshape(N_DP, RESP, 2 * HD)

    own = own_kv.reshape(SLOTS, RESP, 4 * HD)
    columns = columns_of(prompt_hidden)
    relaid = kv_weight.transpose(1, 0, 2)
    near = after(near, (in_hbm(own), in_hbm(columns), in_hbm(relaid)), pltpu.VMEM)
    hidden_y = exchange(columns, ("z", "c"))

    outs, qgrads, own_grad, keep, send = attention(
        pack_counts, slot_groups, block_group, queries, out_grad, own, near, swap_cores(near)
    )
    send = after(send, (hidden_y,), pltpu.HBM)
    partial = (keep.astype(F32) + swap_cores(send).astype(F32)).astype(BF16)
    own_grad = own_grad.reshape(SLOTS, RESP, 2, 2 * HD)
    block_b, line = total_of(exchange(partial, ("y", "z")))
    block_b, own_grad = lax.optimization_barrier((block_b, own_grad))

    terms = prompt_terms(block_b, relaid)
    prompt_grad = sum_of([exchange(terms, "x")], BF16)

    line = after(exchange(line, "z"), (terms,), pltpu.VMEM)
    shares = term_of(hidden_y, line, swap_cores(line))
    moved = [
        lax.ppermute(shares[step], "y", [(i, (i + step) % 4) for i in range(4)])
        for step in (2, 1, 3)
    ]
    weight_grad = sum_of([shares[0], *moved], F32)
    weight_grad = weight_grad.reshape(width // N_DP, 2, 2 * HD)
    return (outs, qgrads, own_grad, weight_grad, prompt_grad)


def solution(mesh):
    grid = Mesh(mesh.devices.reshape(4, 4, 2, 4), ("y", "z", "c", "x"))
    dp = ("y", "z", "c")
    return jax.shard_map(
        body,
        mesh=grid,
        in_specs=(
            P(dp, None),
            P(None, None, "x"),
            P(dp, None, "x"),
            P(dp, None, "x"),
            P(dp, None, None, "x"),
            P(),
            P(),
            P(),
        ),
        out_specs=(
            P(dp, None, "x"),
            P(dp, None, "x"),
            P(dp, None, None, "x"),
            P(dp, None, "x"),
            P(dp, "x"),
        ),
        check_vma=False,
    )
```

time: 211 us -> 155 us (0.73); the launches traced: 208 us -> 155 us
  blocking collectives: 67.7 us -> 40.3 us
  Pallas kernels: 35.7 us -> 19 us
  local copies, waits for them, and re-layouts: 27.3 us -> 10.7 us
  starting transfers between devices: 25.9 us -> 36.5 us
  waiting for transfers between devices: 34.1 us -> 43.2 us
  matrix products: 10.4 us -> 3.75 us
  other arithmetic: 5.89 us -> 0.72 us
    all_to_all x3 -> x1, blocking collectives: 67.7 us -> 40.3 us  [exchange(): return lax.all_to_all(array, axes, 0, 0, tiled=True)]
    pallas_call x2 -> x10, Pallas kernels: 35.7 us -> 19 us  [the longest x1 7.08 us: attention(): pl.pallas_call(attention_kernel, in_specs=[smem] * 3 + [anywhere] * 3 + [...]
    another operation x1 -> x0, local copies, waits for them, and re-layouts: 9.19 us -> none  [body(): weight.reshape(4, width // 4, 4 * HD)]
    dot_general x3 -> x1, matrix products: 10.4 us -> 3.75 us  [body(): jnp.einsum('pd,dkc->pkc', prompt_hidden, kv_weight, preferred_element_typ...]
    ppermute x6 -> x4, starting transfers between devices: 7.24 us -> 13.2 us  [swap_cores(): return lax.ppermute(array, 'c', [(0, 1), (1, 0)])]
    unnamed x29 -> x15, local copies, waits for them, and re-layouts: 9.76 us -> 5.62 us
    ppermute x0 -> x3, starting transfers between devices: none -> 4.09 us  [body(): lax.ppermute(shares[step], 'y', [(i, (i + step) % 4) for i in range(4)])]
    ppermute x6 -> x4, waiting for transfers between devices: 3.13 us -> 6.83 us  [swap_cores(): return lax.ppermute(array, 'c', [(0, 1), (1, 0)])]
  transfers between devices with their start and end apart: 10 -> 11, of which waited for: 6 -> 9; matrix products, arithmetic and copies ran while one was open for 14% -> 5% of each run, Pallas kernels for 17% -> 11%
where the time goes in v2:
time: 155 us
  waiting for transfers between devices  43.2 us (28%)
  blocking collectives  40.3 us (26%)
  starting transfers between devices  36.5 us (24%)
  Pallas kernels  19 us (12%)
  local copies, waits for them, and re-layouts  10.7 us (7%)
  matrix products  3.75 us (2%)
    all_to_all x1, blocking collectives, exchange(): return lax.all_to_all(array, axes, 0, 0, tiled=True)  40.3 us
    all_to_all x4, waiting for transfers between devices, exchange(): return lax.all_to_all(array, axes, 0, 0, tiled=True)  33.2 us
    all_to_all x4, starting transfers between devices, exchange(): return lax.all_to_all(array, axes, 0, 0, tiled=True)  19.2 us
    ppermute x4, starting transfers between devices, swap_cores(): return lax.ppermute(array, 'c', [(0, 1), (1, 0)])  13.2 us
    pallas_call x1, Pallas kernels, attention(): pl.pallas_call(attention_kernel, in_specs=[smem] * 3 + [anywhere] * 3 + [...  7.08 us
    ppermute x4, waiting for transfers between devices, swap_cores(): return lax.ppermute(array, 'c', [(0, 1), (1, 0)])  6.83 us
    unnamed x15, local copies, waits for them, and re-layouts  5.62 us
    pallas_call x1, Pallas kernels, prompt_terms(): pl.pallas_call(prompt_kernel, out_shape=jax.ShapeDtypeStruct(shape, BF16)...  4.89 us
  transfers between devices with their start and end apart: 11, of which 9 were waited for; matrix products, arithmetic and copies ran while one was open for 5% of the time, Pallas kernels for 11%

profile of v2, /device:TPU:1, one launch (start us, length us, event | category | flops | bytes accessed | tf_op | source)
XLA Modules:
  0.0 154.9 jit_solution(7156171081312878736)
XLA Ops:
  0.6 3.8 %fusion.3 = bf16[128,2,256]{2,0,1:T(8,128)(2,1)S(1)} fusion(bf16[5120,2,256]{2,1,0:T(2,128)(2,1)} %param.9, bf16[128,5120]{1,0:T(8,128)(2,1)} %hidden.1), kind=kOutput, calls=%fused_computation.5 | convolution fusion | flops 671154176 | bytes 6684672 | tf_op jit(solution)/shard_map/pd,dkc->pkc/dot_general | solution.py:420
  4.4 1.5 collective-permute-start
  5.9 0.9 collective-permute-done
  6.9 1.5 broadcast_in_dim.2
  8.4 0.0 copy-start
  8.4 8.0 %all-to-all-start = ((bf16[16,256,256]{2,1,0:T(8,128)(2,1)}), bf16[16,256,256]{2,1,0:T(8,128)(2,1)S(1)}, u32[]{:S(2)}, u32[]{:S(2)}) async-start(bf16[16,256,256]{2,1,0:T(8,128)(2,1)} %broadcast_in_dim.2), calls=%async_computation | async-start | bytes 4194304 | tf_op jit(solution)/shard_map/all_to_all | solution.py:410
  16.4 0.0 copy-done
  16.4 3.3 %columns.1.refs_2_ = bf16[8,640,128]{2,1,0:T(8,128)(2,1)} custom-call(bf16[128,5120]{1,0:T(8,128)(2,1)S(1)} %copy-done), custom_call_target="tpu_custom_call" | custom-call | tf_op jit(solution)/shard_map/columns/pallas_call | solution.py:238
  19.7 0.0 copy-start.5
  19.7 5.6 %copy.23 = bf16[5120,2,256]{2,0,1:T(8,128)(2,1)} copy(bf16[5120,2,256]{2,1,0:T(2,128)(2,1)} %param.9) | data formatting | bytes 10485760 | tf_op args[1]
  25.3 0.0 copy-done.5
  25.3 1.5 reshape.27.refs_1_.own_hbm
  26.7 18.9 %all-to-all-done = bf16[16,256,256]{2,1,0:T(8,128)(2,1)S(1)} async-done(((bf16[16,256,256]{2,1,0:T(8,128)(2,1)}), bf16[16,256,256]{2,1,0:T(8,128)(2,1)S(1)}, u32[]{:S(2)}, u32[]{:S(2)}) %all-to-all-start) | async-done | bytes 2097184 | tf_op jit(solution)/shard_map/all_to_all | solution.py:410
  45.6 0.0 copy-start.1
  45.6 0.0 copy-start.2
  45.6 2.6 %collective-permute-start.1 = (bf16[32,128,256]{2,1,0:T(8,128)(2,1)S(1)}, bf16[32,128,256]{2,1,0:T(8,128)(2,1)}, u32[]{:S(2)}, u32[]{:S(2)}) collective-permute-start(bf16[32,128,256]{2,1,0:T(8,128)(2,1)S(1)} %after.3.near), channel_id=1, source_target_pairs={{0,4},{4,0},{1,5},{5,1},{2,6},{6,2},{3,7},{7,3},{8,12},{12,8},{9,1... | collective-permute-start | bytes 6291464 | tf_op jit(solution)/shard_map/ppermute | solution.py:406
  48.3 3.5 %all-to-all-start.1 = ((bf16[8,640,128]{2,1,0:T(8,128)(2,1)}), bf16[8,640,128]{2,1,0:T(8,128)(2,1)S(1)}, u32[]{:S(2)}, u32[]{:S(2)}) async-start(bf16[8,640,128]{2,1,0:T(8,128)(2,1)} %columns.1.refs_2_), calls=%async_computation.1 | async-start | bytes 2621440 | tf_op jit(solution)/shard_map/all_to_all | solution.py:410
  51.8 0.4 collective-permute-done.1.far
  52.2 0.0 copy-done.1
  52.2 0.0 copy-done.2
  52.2 0.0 copy-done.3
  52.2 7.1 %attention.1 = (bf16[8,128,1280]{2,1,0:T(8,128)(2,1)}, bf16[8,128,1280]{2,1,0:T(8,128)(2,1)}, bf16[8,128,512]{2,1,0:T(8,128)(2,1)}, bf16[16,128,512]{2,1,0:T(8,128)(2,1)}, bf16[16,128,512]{2,1,0:T(8,128)(2,1)}) custom-call(s32[32]{0:T(128)S(1)} %copy-done.2, s32[8,32]{1,0:T(8,128)S(1)} %bitcast.16, s32[32]{0:T(128)S(1)} %copy-done.3, ...), custom_call_target="tpu_custom_call" | custom-call | flops 10066329600 | bytes 16777216 | tf_op jit(solution)/shard_map/attention/pallas_call | solution.py:367
  59.3 10.4 %all-to-all-done.1.refs_1_.hidden = bf16[8,640,128]{2,1,0:T(8,128)(2,1)S(1)} async-done(((bf16[8,640,128]{2,1,0:T(8,128)(2,1)}), bf16[8,640,128]{2,1,0:T(8,128)(2,1)S(1)}, u32[]{:S(2)}, u32[]{:S(2)}) %all-to-all-start.1) | async-done | bytes 1310752 | tf_op jit(solution)/shard_map/all_to_all | solution.py:410
  69.7 5.3 %collective-permute-start.2 = (bf16[16,128,512]{2,1,0:T(8,128)(2,1)}, bf16[16,128,512]{2,1,0:T(8,128)(2,1)S(1)}, u32[]{:S(2)}, u32[]{:S(2)}) collective-permute-start(bf16[16,128,512]{2,1,0:T(8,128)(2,1)} %after.4), channel_id=1, source_target_pairs={{0,4},{4,0},{1,5},{5,1},{2,6},{6,2},{3,7},{7,3},{8,12},{12,8},{9,1... | collective-permute-start | bytes 6291464 | tf_op jit(solution)/shard_map/ppermute | solution.py:406
  75.0 4.0 %collective-permute-done.2 = bf16[16,128,512]{2,1,0:T(8,128)(2,1)S(1)} collective-permute-done((bf16[16,128,512]{2,1,0:T(8,128)(2,1)}, bf16[16,128,512]{2,1,0:T(8,128)(2,1)S(1)}, u32[]{:S(2)}, u32[]{:S(2)}) %collective-permute-start.2) | collective-permute-done | bytes 2097184 | tf_op jit(solution)/shard_map/ppermute | solution.py:406
  79.0 0.0 copy-done.4
  79.0 0.7 add_convert_fusion
  79.7 40.3 %all_to_all.25.parts = bf16[16,128,512]{2,1,0:T(8,128)(2,1)S(1)} all-to-all(bf16[16,128,512]{2,1,0:T(8,128)(2,1)S(1)} %add_convert_fusion), channel_id=1, replica_groups=mesh['y'=4,'z'=4,'c'=2,'x'=4] {'y','z'}, dimensions={0} | all-to-all | bytes 4194304 | tf_op jit(solution)/shard_map/all_to_all | solution.py:410
  120.0 1.1 total.1
  121.1 3.6 %all-to-all-start.3 = ((bf16[4,128,512]{2,1,0:T(8,128)(2,1)}), bf16[4,128,512]{2,1,0:T(8,128)(2,1)S(1)}, u32[]{:S(2)}, u32[]{:S(2)}) async-start(bf16[4,128,512]{2,1,0:T(8,128)(2,1)} %get-tuple-element.25), calls=%async_computation.3 | async-start | bytes 1048576 | tf_op jit(solution)/shard_map/all_to_all | solution.py:410
  124.8 0.0 copy-done.6
  124.8 1.1 reshape.29
  125.9 4.9 %prompt.1.refs_1_ = bf16[4,128,1280]{2,1,0:T(8,128)(2,1)} custom-call(bf16[128,512]{1,0:T(8,128)(2,1)S(1)} %get-tuple-element.26.block, bf16[2,5120,256]{2,1,0:T(8,128)(2,1)} %bitcast.18), custom_call_target="tpu_custom_call" | custom-call | flops 671088640 | bytes 4194304 | tf_op jit(solution)/shard_map/prompt/pallas_call | solution.py:320
  130.8 0.7 all-to-all-done.3.refs_0_
  131.5 4.0 %all-to-all-start.4 = ((bf16[4,128,1280]{2,1,0:T(8,128)(2,1)}), bf16[4,128,1280]{2,1,0:T(8,128)(2,1)S(1)}, u32[]{:S(2)}, u32[]{:S(2)}) async-start(bf16[4,128,1280]{2,1,0:T(8,128)(2,1)} %prompt.1.refs_1_), calls=%async_computation.4 | async-start | bytes 2621440 | tf_op jit(solution)/shard_map/all_to_all | solution.py:410
  135.5 3.7 %collective-permute-start.3 = (bf16[4,128,512]{2,1,0:T(8,128)(2,1)S(1)}, bf16[4,128,512]{2,1,0:T(8,128)(2,1)S(1)}, u32[]{:S(2)}, u32[]{:S(2)}) collective-permute-start(bf16[4,128,512]{2,1,0:T(8,128)(2,1)S(1)} %after.5.line), channel_id=1, source_target_pairs={{0,4},{4,0},{1,5},{5,1},{2,6},{6,2},{3,7},{7,3},{8,12},{12,8},{9,1... | collective-permute-start | bytes 1572872 | tf_op jit(solution)/shard_map/ppermute | solution.py:406
  139.3 1.5 collective-permute-done.3.other
  140.8 1.7 %term.1 = (bf16[160,512]{1,0:T(8,128)(2,1)S(1)}, bf16[160,512]{1,0:T(8,128)(2,1)}, bf16[160,512]{1,0:T(8,128)(2,1)}, bf16[160,512]{1,0:T(8,128)(2,1)S(1)}) custom-call(bf16[8,640,128]{2,1,0:T(8,128)(2,1)S(1)} %all-to-all-done.1.refs_1_.hidden, bf16[4,128,512]{2,1,0:T(8,128)(2,1)S(1)} %after.5.line, bf16[4,128,512]{2,1,0:T(8,128)(2,1)S(1)} %collective-permute-done.3.other), custom_call_target="tpu_custom_call" | custom-call | tf_op jit(solution)/shard_map/term/pallas_call | solution.py:291
  142.5 1.4 collective-permute-start.4
  143.9 0.7 collective-permute-start.5
  144.6 2.0 %collective-permute-start.6 = (bf16[160,512]{1,0:T(8,128)(2,1)S(1)}, bf16[160,512]{1,0:T(8,128)(2,1)S(1)}, u32[]{:S(2)}, u32[]{:S(2)}) collective-permute-start(bf16[160,512]{1,0:T(8,128)(2,1)S(1)} %get-tuple-element.30), channel_id=1, source_target_pairs={{0,96},{32,0},{64,32},{96,64},{1,97},{33,1},{65,33},{97,65},{2,98}... | collective-permute-start | bytes 491528 | tf_op jit(solution)/shard_map/ppermute | solution.py:452
  146.6 3.2 %all-to-all-done.4.refs_0_ = bf16[4,128,1280]{2,1,0:T(8,128)(2,1)S(1)} async-done(((bf16[4,128,1280]{2,1,0:T(8,128)(2,1)}), bf16[4,128,1280]{2,1,0:T(8,128)(2,1)S(1)}, u32[]{:S(2)}, u32[]{:S(2)}) %all-to-all-start.4) | async-done | bytes 1310752 | tf_op jit(solution)/shard_map/all_to_all | solution.py:410
  149.7 0.9 sum.3
  150.6 0.0 collective-permute-done.4.refs_1_
  150.6 3.2 %collective-permute-done.5.refs_2_ = bf16[160,512]{1,0:T(8,128)(2,1)S(1)} collective-permute-done((bf16[160,512]{1,0:T(8,128)(2,1)}, bf16[160,512]{1,0:T(8,128)(2,1)S(1)}, u32[]{:S(2)}, u32[]{:S(2)}) %collective-permute-start.5) | collective-permute-done | bytes 163872 | tf_op jit(solution)/shard_map/ppermute | solution.py:452
  153.8 0.0 collective-permute-done.6.refs_3_
  153.8 0.1 sum.2
  153.9 0.9 reshape.30
  (9 shorter events, 0.0 us)
Async XLA Ops:
  4.4 2.4 %collective-permute-start = (bf16[128,256]{1,0:T(8,128)(2,1)S(1)}, bf16[128,256]{1,0:T(8,128)(2,1)S(1)}, u32[]{:S(2)}, u32[]{:S(2)}) collective-permute-start(bf16[128,256]{1,0:T(8,128)(2,1)S(1)} %select_bitcast_fusion), channel_id=1, source_target_pairs={{0,4},{4,0},{1,5},{5,1},{2,6},{6,2},{3,7},{7,3},{8,12},{12,8},{9,1... | collective-permute-start | bytes 196616 | tf_op jit(solution)/shard_map/ppermute | solution.py:406
  8.4 8.0 %copy-start = (bf16[128,5120]{1,0:T(8,128)(2,1)S(1)}, bf16[128,5120]{1,0:T(8,128)(2,1)}, u32[]{:S(2)}) copy-start(bf16[128,5120]{1,0:T(8,128)(2,1)} %hidden.1) | copy-start | bytes 3932164
  8.4 37.2 %all-to-all-start = ((bf16[16,256,256]{2,1,0:T(8,128)(2,1)}), bf16[16,256,256]{2,1,0:T(8,128)(2,1)S(1)}, u32[]{:S(2)}, u32[]{:S(2)}) async-start(bf16[16,256,256]{2,1,0:T(8,128)(2,1)} %broadcast_in_dim.2), calls=%async_computation | async-start | bytes 4194304 | tf_op jit(solution)/shard_map/all_to_all | solution.py:410
  19.7 5.6 %copy-start.5 = (bf16[8,128,2,256]{3,2,1,0:T(2,128)(2,1)S(1)}, bf16[8,128,2,256]{3,2,1,0:T(2,128)(2,1)}, u32[]{:S(2)}) copy-start(bf16[8,128,2,256]{3,2,1,0:T(2,128)(2,1)} %param.12) | copy-start | bytes 3145732
  45.6 6.6 %copy-start.1 = (s32[32,8]{0,1:T(8,128)S(1)}, s32[32,8]{0,1:T(8,128)}, u32[]{:S(2)}) copy-start(s32[32,8]{0,1:T(8,128)} %param.14) | copy-start | bytes 3076
  45.6 6.6 %copy-start.2 = (s32[32]{0:T(128)S(1)}, s32[32]{0:T(128)}, u32[]{:S(2)}) copy-start(s32[32]{0:T(128)} %pack_counts.1) | copy-start | bytes 388
  45.6 6.6 %copy-start.3 = (s32[32]{0:T(128)S(1)}, s32[32]{0:T(128)}, u32[]{:S(2)}) copy-start(s32[32]{0:T(128)} %block_group.1) | copy-start | bytes 388
  45.6 6.5 %collective-permute-start.1 = (bf16[32,128,256]{2,1,0:T(8,128)(2,1)S(1)}, bf16[32,128,256]{2,1,0:T(8,128)(2,1)}, u32[]{:S(2)}, u32[]{:S(2)}) collective-permute-start(bf16[32,128,256]{2,1,0:T(8,128)(2,1)S(1)} %after.3.near), channel_id=1, source_target_pairs={{0,4},{4,0},{1,5},{5,1},{2,6},{6,2},{3,7},{7,3},{8,12},{12,8},{9,1... | collective-permute-start | bytes 6291464 | tf_op jit(solution)/shard_map/ppermute | solution.py:406
  48.3 21.4 %all-to-all-start.1 = ((bf16[8,640,128]{2,1,0:T(8,128)(2,1)}), bf16[8,640,128]{2,1,0:T(8,128)(2,1)S(1)}, u32[]{:S(2)}, u32[]{:S(2)}) async-start(bf16[8,640,128]{2,1,0:T(8,128)(2,1)} %columns.1.refs_2_), calls=%async_computation.1 | async-start | bytes 2621440 | tf_op jit(solution)/shard_map/all_to_all | solution.py:410
  69.7 9.3 %copy-start.4 = (bf16[16,128,512]{2,1,0:T(8,128)(2,1)S(1)}, bf16[16,128,512]{2,1,0:T(8,128)(2,1)}, u32[]{:S(2)}) copy-start(bf16[16,128,512]{2,1,0:T(8,128)(2,1)} %get-tuple-element.20) | copy-start | bytes 6291460
  69.7 9.3 %collective-permute-start.2 = (bf16[16,128,512]{2,1,0:T(8,128)(2,1)}, bf16[16,128,512]{2,1,0:T(8,128)(2,1)S(1)}, u32[]{:S(2)}, u32[]{:S(2)}) collective-permute-start(bf16[16,128,512]{2,1,0:T(8,128)(2,1)} %after.4), channel_id=1, source_target_pairs={{0,4},{4,0},{1,5},{5,1},{2,6},{6,2},{3,7},{7,3},{8,12},{12,8},{9,1... | collective-permute-start | bytes 6291464 | tf_op jit(solution)/shard_map/ppermute | solution.py:406
  120.0 4.7 %copy-start.6 = (bf16[8,128,512]{2,1,0:T(8,128)(2,1)S(1)}, bf16[8,128,512]{2,1,0:T(8,128)(2,1)}, u32[]{:S(2)}) copy-start(bf16[8,128,512]{2,1,0:T(8,128)(2,1)} %get-tuple-element.23) | copy-start | bytes 3145732
  121.1 10.4 %all-to-all-start.3 = ((bf16[4,128,512]{2,1,0:T(8,128)(2,1)}), bf16[4,128,512]{2,1,0:T(8,128)(2,1)S(1)}, u32[]{:S(2)}, u32[]{:S(2)}) async-start(bf16[4,128,512]{2,1,0:T(8,128)(2,1)} %get-tuple-element.25), calls=%async_computation.3 | async-start | bytes 1048576 | tf_op jit(solution)/shard_map/all_to_all | solution.py:410
  131.5 18.2 %all-to-all-start.4 = ((bf16[4,128,1280]{2,1,0:T(8,128)(2,1)}), bf16[4,128,1280]{2,1,0:T(8,128)(2,1)S(1)}, u32[]{:S(2)}, u32[]{:S(2)}) async-start(bf16[4,128,1280]{2,1,0:T(8,128)(2,1)} %prompt.1.refs_1_), calls=%async_computation.4 | async-start | bytes 2621440 | tf_op jit(solution)/shard_map/all_to_all | solution.py:410
  135.5 5.3 %collective-permute-start.3 = (bf16[4,128,512]{2,1,0:T(8,128)(2,1)S(1)}, bf16[4,128,512]{2,1,0:T(8,128)(2,1)S(1)}, u32[]{:S(2)}, u32[]{:S(2)}) collective-permute-start(bf16[4,128,512]{2,1,0:T(8,128)(2,1)S(1)} %after.5.line), channel_id=1, source_target_pairs={{0,4},{4,0},{1,5},{5,1},{2,6},{6,2},{3,7},{7,3},{8,12},{12,8},{9,1... | collective-permute-start | bytes 1572872 | tf_op jit(solution)/shard_map/ppermute | solution.py:406
  142.5 8.1 %collective-permute-start.4 = (bf16[160,512]{1,0:T(8,128)(2,1)}, bf16[160,512]{1,0:T(8,128)(2,1)S(1)}, u32[]{:S(2)}, u32[]{:S(2)}) collective-permute-start(bf16[160,512]{1,0:T(8,128)(2,1)} %get-tuple-element.28), channel_id=1, source_target_pairs={{0,64},{32,96},{64,0},{96,32},{1,65},{33,97},{65,1},{97,33},{2,66}... | collective-permute-start | bytes 491528 | tf_op jit(solution)/shard_map/ppermute | solution.py:452
  143.9 9.9 %collective-permute-start.5 = (bf16[160,512]{1,0:T(8,128)(2,1)}, bf16[160,512]{1,0:T(8,128)(2,1)S(1)}, u32[]{:S(2)}, u32[]{:S(2)}) collective-permute-start(bf16[160,512]{1,0:T(8,128)(2,1)} %get-tuple-element.29), channel_id=1, source_target_pairs={{0,32},{32,64},{64,96},{96,0},{1,33},{33,65},{65,97},{97,1},{2,34}... | collective-permute-start | bytes 491528 | tf_op jit(solution)/shard_map/ppermute | solution.py:452
  144.6 9.2 %collective-permute-start.6 = (bf16[160,512]{1,0:T(8,128)(2,1)S(1)}, bf16[160,512]{1,0:T(8,128)(2,1)S(1)}, u32[]{:S(2)}, u32[]{:S(2)}) collective-permute-start(bf16[160,512]{1,0:T(8,128)(2,1)S(1)} %get-tuple-element.30), channel_id=1, source_target_pairs={{0,96},{32,0},{64,32},{96,64},{1,97},{33,1},{65,33},{97,65},{2,98}... | collective-permute-start | bytes 491528 | tf_op jit(solution)/shard_map/ppermute | solution.py:452

commit v3 on v2

--- a/solution.py
+++ b/solution.py
@@ -225,6 +225,19 @@
     )
 
 
+def after_all(arrays, tokens):
+    anywhere = pl.BlockSpec(memory_space=pl.ANY)
+    return pl.pallas_call(
+        after_kernel,
+        in_specs=[anywhere] * (len(arrays) + len(tokens)),
+        out_specs=[anywhere] * len(arrays),
+        out_shape=[jax.ShapeDtypeStruct(array.shape, array.dtype) for array in arrays],
+        input_output_aliases={i: i for i in range(len(arrays))},
+        compiler_params=pltpu.CompilerParams(vmem_limit_bytes=2**20),
+        name="after",
+    )(*arrays, *tokens)
+
+
 def columns_kernel(hidden, columns):
     share = hidden.shape[1] // N_DP
     for part in range(8):
@@ -243,35 +256,14 @@
     )(hidden)
 
 
-def total_kernel(parts, total, copies):
-    summed = parts[0].astype(F32)
-    for i in range(1, parts.shape[0]):
-        summed = summed + parts[i].astype(F32)
-    summed = summed.astype(BF16)
-    total[...] = summed
-    for i in range(copies.shape[0]):
-        copies[i] = summed
-
-
-def total_of(parts):
-    shape = parts.shape[1:]
-    return pl.pallas_call(
-        total_kernel,
-        out_shape=[
-            jax.ShapeDtypeStruct(shape, BF16),
-            jax.ShapeDtypeStruct((4,) + shape, BF16),
-        ],
-        compiler_params=pltpu.CompilerParams(vmem_limit_bytes=8 * 2**20),
-        name="total",
-    )(parts)
-
-
-def term_kernel(hidden, line, other, *refs):
-    *parts, terms = refs
+def term_kernel(hidden, *refs):
+    lines, others, parts, terms = refs[:4], refs[4:8], refs[8:12], refs[12]
     first = lax.axis_index("c") == 0
+    here = lax.axis_index("z")
     total = None
-    for z in range(4):
-        ours, theirs = line[z], other[z]
+    for step, (line, other) in enumerate(zip(lines, others)):
+        z = lax.rem(here + 4 - step, 4)
+        ours, theirs = line[...], other[...]
         pair = jnp.concatenate(
             [jnp.where(first, ours, theirs), jnp.where(first, theirs, ours)], 0
         )
@@ -286,50 +278,57 @@
         part[...] = terms[pl.ds(start, share)].astype(BF16)
 
 
-def term_of(hidden, line, other):
-    width, columns = hidden.shape[1], line.shape[2]
+def term_of(hidden, lines, others):
+    width, columns = hidden.shape[1], lines[0].shape[1]
     return pl.pallas_call(
         term_kernel,
         out_shape=[jax.ShapeDtypeStruct((width // 4, columns), BF16)] * 4,
         scratch_shapes=[pltpu.VMEM((width, columns), F32)],
+        cost_estimate=pl.CostEstimate(
+            flops=2000000000, bytes_accessed=10000000, transcendentals=0
+        ),
         compiler_params=pltpu.CompilerParams(vmem_limit_bytes=12 * 2**20),
         name="term",
-    )(hidden, line, other)
-
-
-def prompt_kernel(block, weight_hbm, terms, weight, sems):
-    rows = terms.shape[2]
-    copies = [
-        pltpu.make_async_copy(
-            weight_hbm.at[:, pl.ds(x * rows, rows)], weight.at[x], sems.at[x]
-        )
-        for x in range(4)
-    ]
-    for copy in copies:
-        copy.start()
-    for x, copy in enumerate(copies):
+    )(hidden, *lines, *others)
+
+
+def prompt_kernel(block, weight_hbm, *refs):
+    *terms, weight, sems = refs
+    here = lax.axis_index("x")
+    rows = terms[0].shape[1]
+    steps = (2, 1, 3, 0)
+    copies = []
+    for step in steps:
+        start = pl.multiple_of(lax.rem(here + step, 4) * rows, rows)
+        copies.append(
+            pltpu.make_async_copy(
+                weight_hbm.at[:, pl.ds(start, rows)], weight.at[step], sems.at[step]
+            )
+        )
+        copies[-1].start()
+    for step, copy in zip(steps, copies):
         copy.wait()
-        terms[x] = (
-            dot(block[:, : 2 * HD], weight[x, 0], NT)
-            + dot(block[:, 2 * HD :], weight[x, 1], NT)
+        terms[step][...] = (
+            dot(block[:, : 2 * HD], weight[step, 0], NT)
+            + dot(block[:, 2 * HD :], weight[step, 1], NT)
         ).astype(BF16)
 
 
 def prompt_terms(block, weight):
-    shape = (4, block.shape[0], weight.shape[1] // 4)
+    shape = (block.shape[0], weight.shape[1] // 4)
     return pl.pallas_call(
         prompt_kernel,
-        out_shape=jax.ShapeDtypeStruct(shape, BF16),
+        out_shape=[jax.ShapeDtypeStruct(shape, BF16)] * 4,
         in_specs=[
             pl.BlockSpec(memory_space=pltpu.VMEM),
             pl.BlockSpec(memory_space=pl.ANY),
         ],
         scratch_shapes=[
-            pltpu.VMEM((4, 2, shape[2], 2 * HD), BF16),
+            pltpu.VMEM((4, 2, shape[1], 2 * HD), BF16),
             pltpu.SemaphoreType.DMA((4,)),
         ],
         cost_estimate=pl.CostEstimate(
-            flops=8 * shape[1] * shape[2] * 4 * HD, bytes_accessed=2**22, transcendentals=0
+            flops=8 * shape[0] * shape[1] * 4 * HD, bytes_accessed=2**22, transcendentals=0
         ),
         compiler_params=pltpu.CompilerParams(vmem_limit_bytes=16 * 2**20),
         name="prompt",
@@ -440,18 +439,17 @@
     send = after(send, (hidden_y,), pltpu.HBM)
     partial = (keep.astype(F32) + swap_cores(send).astype(F32)).astype(BF16)
     own_grad = own_grad.reshape(SLOTS, RESP, 2, 2 * HD)
-    block_b, line = total_of(exchange(partial, ("y", "z")))
-    block_b, own_grad = lax.optimization_barrier((block_b, own_grad))
+    block_b = sum_of([exchange(partial, ("y", "z"))], BF16)
+
+    def ring(array, axis, step):
+        return lax.ppermute(array, axis, [(i, (i + step) % 4) for i in range(4)])
 
     terms = prompt_terms(block_b, relaid)
-    prompt_grad = sum_of([exchange(terms, "x")], BF16)
-
-    line = after(exchange(line, "z"), (terms,), pltpu.VMEM)
-    shares = term_of(hidden_y, line, swap_cores(line))
-    moved = [
-        lax.ppermute(shares[step], "y", [(i, (i + step) % 4) for i in range(4)])
-        for step in (2, 1, 3)
-    ]
+    prompt_grad = sum_of([terms[0], *[ring(terms[step], "x", step) for step in (2, 1, 3)]], BF16)
+
+    lines = [block_b] + [ring(block_b, "z", step) for step in (1, 2, 3)]
+    shares = term_of(hidden_y, lines, [swap_cores(line) for line in lines])
+    moved = [ring(shares[step], "y", step) for step in (2, 1, 3)]
     weight_grad = sum_of([shares[0], *moved], F32)
     weight_grad = weight_grad.reshape(width // N_DP, 2, 2 * HD)
     return (outs, qgrads, own_grad, weight_grad, prompt_grad)

time: 155 us -> 149 us (0.961)
  Pallas kernels: 19 us -> 35.8 us
  waiting for transfers between devices: 43.2 us -> 29 us
  blocking collectives: 40.3 us -> 31.8 us
  starting transfers between devices: 36.5 us -> 34.4 us
    pallas_call x1, Pallas kernels: 7.08 us -> 25.5 us  [attention(): pl.pallas_call(attention_kernel, in_specs=[smem] * 3 + [anywhere] * 3 + [...]
    all_to_all x4 -> x2, waiting for transfers between devices: 33.2 us -> 18.9 us  [exchange(): return lax.all_to_all(array, axes, 0, 0, tiled=True)]
    all_to_all x1, blocking collectives: 40.3 us -> 31.8 us  [exchange(): return lax.all_to_all(array, axes, 0, 0, tiled=True)]
    all_to_all x4 -> x2, starting transfers between devices: 19.2 us -> 11.5 us  [exchange(): return lax.all_to_all(array, axes, 0, 0, tiled=True)]
    ppermute x3 -> x9, starting transfers between devices: 4.09 us -> 11.7 us  [ring(): return lax.ppermute(array, axis, [(i, (i + step) % 4) for i in range(4)])]
    ppermute x4 -> x7, starting transfers between devices: 13.2 us -> 11.2 us  [swap_cores(): return lax.ppermute(array, 'c', [(0, 1), (1, 0)])]
    pallas_call x2 -> x1, Pallas kernels: 5.97 us -> 4.05 us  [prompt_terms(): pl.pallas_call(prompt_kernel, out_shape=[jax.ShapeDtypeStruct(shape, BF16...]
    ppermute x3 -> x9, waiting for transfers between devices: 3.21 us -> 4.4 us  [ring(): return lax.ppermute(array, axis, [(i, (i + step) % 4) for i in range(4)])]
  transfers between devices with their start and end apart: 11 -> 18, of which waited for: 9 -> 8; matrix products, arithmetic and copies ran while one was open for 5% -> 6% of each run, Pallas kernels for 11% -> 24%
where the time goes in v3:
time: 149 us; the launch traced here: 148 us
  Pallas kernels  35.8 us (24%)
  starting transfers between devices  34.4 us (23%)
  blocking collectives  31.8 us (21%)
  waiting for transfers between devices  29 us (19%)
  local copies, waits for them, and re-layouts  11.7 us (8%)
  matrix products  3.75 us (3%)
    all_to_all x1, blocking collectives, exchange(): return lax.all_to_all(array, axes, 0, 0, tiled=True)  31.8 us
    pallas_call x1, Pallas kernels, attention(): pl.pallas_call(attention_kernel, in_specs=[smem] * 3 + [anywhere] * 3 + [...  25.5 us
    all_to_all x2, waiting for transfers between devices, exchange(): return lax.all_to_all(array, axes, 0, 0, tiled=True)  18.9 us
    ppermute x9, starting transfers between devices, ring(): return lax.ppermute(array, axis, [(i, (i + step) % 4) for i in range(4)])  11.7 us
    all_to_all x2, starting transfers between devices, exchange(): return lax.all_to_all(array, axes, 0, 0, tiled=True)  11.5 us
    ppermute x7, starting transfers between devices, swap_cores(): return lax.ppermute(array, 'c', [(0, 1), (1, 0)])  11.2 us
    ppermute x7, waiting for transfers between devices, swap_cores(): return lax.ppermute(array, 'c', [(0, 1), (1, 0)])  5.73 us
    unnamed x13, local copies, waits for them, and re-layouts  5.6 us
  transfers between devices with their start and end apart: 18, of which 8 were waited for; matrix products, arithmetic and copies ran while one was open for 6% of the time, Pallas kernels for 24%

profile of v3, /device:TPU:1, one launch (start us, length us, event | category | flops | bytes accessed | tf_op | source)
XLA Modules:
  0.0 148.0 jit_solution(7842407001879314619)
XLA Ops:
  0.6 3.8 %fusion.3 = bf16[128,2,256]{2,0,1:T(8,128)(2,1)S(1)} fusion(bf16[5120,2,256]{2,1,0:T(2,128)(2,1)} %param.9, bf16[128,5120]{1,0:T(8,128)(2,1)} %hidden.1), kind=kOutput, calls=%fused_computation.5 | convolution fusion | flops 671154176 | bytes 6684672 | tf_op jit(solution)/shard_map/pd,dkc->pkc/dot_general | solution.py:419
  4.4 1.5 %collective-permute-start = (bf16[128,256]{1,0:T(8,128)(2,1)S(1)}, bf16[128,256]{1,0:T(8,128)(2,1)S(1)}, u32[]{:S(2)}, u32[]{:S(2)}) collective-permute-start(bf16[128,256]{1,0:T(8,128)(2,1)S(1)} %select_bitcast_fusion), channel_id=1, source_target_pairs={{0,4},{4,0},{1,5},{5,1},{2,6},{6,2},{3,7},{7,3},{8,12},{12,8},{9,1... | collective-permute-start | bytes 196616 | tf_op jit(solution)/shard_map/ppermute | solution.py:405
  5.9 0.9 collective-permute-done
  6.9 1.5 %broadcast_in_dim.2 = bf16[16,256,256]{2,1,0:T(8,128)(2,1)} broadcast(bf16[256,256]{1,0:T(8,128)(2,1)S(1)} %pad_maximum_fusion), dimensions={1,2} | broadcast | bytes 2228224 | tf_op jit(solution)/shard_map/broadcast_in_dim | solution.py:427
  8.4 8.0 %all-to-all-start = ((bf16[16,256,256]{2,1,0:T(8,128)(2,1)}), bf16[16,256,256]{2,1,0:T(8,128)(2,1)S(1)}, u32[]{:S(2)}, u32[]{:S(2)}) async-start(bf16[16,256,256]{2,1,0:T(8,128)(2,1)} %broadcast_in_dim.2), calls=%async_computation | async-start | bytes 4194304 | tf_op jit(solution)/shard_map/all_to_all | solution.py:409
  16.4 3.3 %columns.1.refs_2_ = bf16[8,640,128]{2,1,0:T(8,128)(2,1)} custom-call(bf16[128,5120]{1,0:T(8,128)(2,1)S(1)} %copy-done), custom_call_target="tpu_custom_call" | custom-call | tf_op jit(solution)/shard_map/columns/pallas_call | solution.py:251
  19.7 5.6 %copy.22 = bf16[5120,2,256]{2,0,1:T(8,128)(2,1)} copy(bf16[5120,2,256]{2,1,0:T(2,128)(2,1)} %param.9) | data formatting | bytes 10485760 | tf_op args[1]
  25.3 1.5 reshape.27.refs_1_.own_hbm
  26.7 18.9 %all-to-all-done = bf16[16,256,256]{2,1,0:T(8,128)(2,1)S(1)} async-done(((bf16[16,256,256]{2,1,0:T(8,128)(2,1)}), bf16[16,256,256]{2,1,0:T(8,128)(2,1)S(1)}, u32[]{:S(2)}, u32[]{:S(2)}) %all-to-all-start) | async-done | bytes 2097184 | tf_op jit(solution)/shard_map/all_to_all | solution.py:409
  45.6 2.6 %collective-permute-start.1 = (bf16[32,128,256]{2,1,0:T(8,128)(2,1)S(1)}, bf16[32,128,256]{2,1,0:T(8,128)(2,1)}, u32[]{:S(2)}, u32[]{:S(2)}) collective-permute-start(bf16[32,128,256]{2,1,0:T(8,128)(2,1)S(1)} %after.2.near), channel_id=1, source_target_pairs={{0,4},{4,0},{1,5},{5,1},{2,6},{6,2},{3,7},{7,3},{8,12},{12,8},{9,1... | collective-permute-start | bytes 6291464 | tf_op jit(solution)/shard_map/ppermute | solution.py:405
  48.3 3.5 %all-to-all-start.1 = ((bf16[8,640,128]{2,1,0:T(8,128)(2,1)}), bf16[8,640,128]{2,1,0:T(8,128)(2,1)S(1)}, u32[]{:S(2)}, u32[]{:S(2)}) async-start(bf16[8,640,128]{2,1,0:T(8,128)(2,1)} %columns.1.refs_2_), calls=%async_computation.1 | async-start | bytes 2621440 | tf_op jit(solution)/shard_map/all_to_all | solution.py:409
  51.8 0.4 collective-permute-done.1.far
  52.2 25.5 %attention.1 = (bf16[8,128,1280]{2,1,0:T(8,128)(2,1)}, bf16[8,128,1280]{2,1,0:T(8,128)(2,1)}, bf16[8,128,512]{2,1,0:T(8,128)(2,1)}, bf16[16,128,512]{2,1,0:T(8,128)(2,1)}, bf16[16,128,512]{2,1,0:T(8,128)(2,1)}) custom-call(s32[32]{0:T(128)S(1)} %copy-done.2, s32[8,32]{1,0:T(8,128)S(1)} %bitcast.16, s32[32]{0:T(128)S(1)} %copy-done.3, ...), custom_call_target="tpu_custom_call" | custom-call | flops 10066329600 | bytes 16777216 | tf_op jit(solution)/shard_map/attention/pallas_call | solution.py:366
  77.7 0.0 all-to-all-done.1.refs_1_.hidden
  77.7 3.7 %collective-permute-start.2 = (bf16[16,128,512]{2,1,0:T(8,128)(2,1)}, bf16[16,128,512]{2,1,0:T(8,128)(2,1)S(1)}, u32[]{:S(2)}, u32[]{:S(2)}) collective-permute-start(bf16[16,128,512]{2,1,0:T(8,128)(2,1)} %after.3), channel_id=1, source_target_pairs={{0,4},{4,0},{1,5},{5,1},{2,6},{6,2},{3,7},{7,3},{8,12},{12,8},{9,1... | collective-permute-start | bytes 6291464 | tf_op jit(solution)/shard_map/ppermute | solution.py:405
  81.4 4.0 %collective-permute-done.2 = bf16[16,128,512]{2,1,0:T(8,128)(2,1)S(1)} collective-permute-done((bf16[16,128,512]{2,1,0:T(8,128)(2,1)}, bf16[16,128,512]{2,1,0:T(8,128)(2,1)S(1)}, u32[]{:S(2)}, u32[]{:S(2)}) %collective-permute-start.2) | collective-permute-done | bytes 2097184 | tf_op jit(solution)/shard_map/ppermute | solution.py:405
  85.4 0.7 add_convert_fusion
  86.1 31.8 %all_to_all.15.refs_0_ = bf16[16,128,512]{2,1,0:T(8,128)(2,1)S(1)} all-to-all(bf16[16,128,512]{2,1,0:T(8,128)(2,1)S(1)} %add_convert_fusion), channel_id=1, replica_groups=mesh['y'=4,'z'=4,'c'=2,'x'=4] {'y','z'}, dimensions={0} | all-to-all | bytes 4194304 | tf_op jit(solution)/shard_map/all_to_all | solution.py:409
  117.9 0.3 sum.3.refs_0_.block
  118.2 1.5 %collective-permute-start.5 = (bf16[128,512]{1,0:T(8,128)(2,1)S(1)}, bf16[128,512]{1,0:T(8,128)(2,1)S(1)}, u32[]{:S(2)}, u32[]{:S(2)}) collective-permute-start(bf16[128,512]{1,0:T(8,128)(2,1)S(1)} %sum.3.refs_0_.block), channel_id=1, source_target_pairs={{0,24},{8,0},{16,8},{24,16},{1,25},{9,1},{17,9},{25,17},{2,26},{10... | collective-permute-start | bytes 393224 | tf_op jit(solution)/shard_map/ppermute | solution.py:445
  119.6 1.0 collective-permute-start.4
  120.6 0.0 collective-permute-start.3
  120.6 4.1 %prompt.1 = (bf16[128,1280]{1,0:T(8,128)(2,1)S(1)}, bf16[128,1280]{1,0:T(8,128)(2,1)}, bf16[128,1280]{1,0:T(8,128)(2,1)S(1)}, bf16[128,1280]{1,0:T(8,128)(2,1)}) custom-call(bf16[128,512]{1,0:T(8,128)(2,1)S(1)} %sum.3.refs_0_.block, bf16[2,5120,256]{2,1,0:T(8,128)(2,1)} %bitcast.18), custom_call_target="tpu_custom_call" | custom-call | flops 671088640 | bytes 4194304 | tf_op jit(solution)/shard_map/prompt/pallas_call | solution.py:319
  124.7 2.8 %collective-permute-start.13 = (bf16[128,1280]{1,0:T(8,128)(2,1)S(1)}, bf16[128,1280]{1,0:T(8,128)(2,1)S(1)}, u32[]{:S(2)}, u32[]{:S(2)}) collective-permute-start(bf16[128,1280]{1,0:T(8,128)(2,1)S(1)} %get-tuple-element.28), channel_id=1, source_target_pairs={{0,2},{1,3},{2,0},{3,1},{4,6},{5,7},{6,4},{7,5},{8,10},{9,11},{10,... | collective-permute-start | bytes 983048 | tf_op jit(solution)/shard_map/ppermute | solution.py:445
  127.5 2.8 %collective-permute-start.6 = (bf16[128,512]{1,0:T(8,128)(2,1)S(1)}, bf16[128,512]{1,0:T(8,128)(2,1)S(1)}, u32[]{:S(2)}, u32[]{:S(2)}) collective-permute-start(bf16[128,512]{1,0:T(8,128)(2,1)S(1)} %sum.3.refs_0_.block), channel_id=1, source_target_pairs={{0,4},{4,0},{1,5},{5,1},{2,6},{6,2},{3,7},{7,3},{8,12},{12,8},{9,1... | collective-permute-start | bytes 393224 | tf_op jit(solution)/shard_map/ppermute | solution.py:405
  130.3 0.0 collective-permute-done.5.refs_3_
  130.3 0.0 collective-permute-start.9
  130.3 0.0 collective-permute-done.4.refs_2_
  130.3 0.5 collective-permute-start.8
  130.8 0.0 collective-permute-done.3.refs_1_
  130.8 0.1 collective-permute-start.7
  130.9 0.4 collective-permute-done.6.refs_4_
  131.3 0.3 collective-permute-start.14
  131.6 0.1 collective-permute-done.9.refs_7_
  131.7 2.3 %collective-permute-start.15 = (bf16[128,1280]{1,0:T(8,128)(2,1)}, bf16[128,1280]{1,0:T(8,128)(2,1)S(1)}, u32[]{:S(2)}, u32[]{:S(2)}) collective-permute-start(bf16[128,1280]{1,0:T(8,128)(2,1)} %get-tuple-element.30), channel_id=1, source_target_pairs={{0,3},{1,0},{2,1},{3,2},{4,7},{5,4},{6,5},{7,6},{8,11},{9,8},{10,9... | collective-permute-start | bytes 983048 | tf_op jit(solution)/shard_map/ppermute | solution.py:445
  134.0 0.0 collective-permute-done.8.refs_6_
  134.0 1.7 %term.1 = (bf16[160,512]{1,0:T(8,128)(2,1)S(1)}, bf16[160,512]{1,0:T(8,128)(2,1)}, bf16[160,512]{1,0:T(8,128)(2,1)}, bf16[160,512]{1,0:T(8,128)(2,1)}) custom-call(bf16[8,640,128]{2,1,0:T(8,128)(2,1)S(1)} %all-to-all-done.1.refs_1_.hidden, bf16[128,512]{1,0:T(8,128)(2,1)S(1)} %sum.3.refs_0_.block, bf16[128,512]{1,0:T(8,128)(2,1)S(1)} %collective-permute-done.3.refs_1_, ...), custom_call_target="tpu_custom_call" | custom-call | flops 2000000000 | bytes 10000000 | tf_op jit(solution)/shard_map/term/pallas_call | solution.py:283
  135.7 1.1 collective-permute-start.10
  136.9 0.2 collective-permute-start.11
  137.1 0.0 collective-permute-done.13.refs_1_
  137.1 2.5 %collective-permute-start.12 = (bf16[160,512]{1,0:T(8,128)(2,1)}, bf16[160,512]{1,0:T(8,128)(2,1)S(1)}, u32[]{:S(2)}, u32[]{:S(2)}) collective-permute-start(bf16[160,512]{1,0:T(8,128)(2,1)} %get-tuple-element.26), channel_id=1, source_target_pairs={{0,96},{32,0},{64,32},{96,64},{1,97},{33,1},{65,33},{97,65},{2,98}... | collective-permute-start | bytes 491528 | tf_op jit(solution)/shard_map/ppermute | solution.py:445
  139.5 2.1 %reshape.29 = bf16[8,128,2,256]{3,2,1,0:T(2,128)(2,1)} reshape(bf16[8,128,512]{2,1,0:T(8,128)(2,1)} %get-tuple-element.20) | data formatting | bytes 2097152 | tf_op jit(solution)/shard_map/reshape | solution.py:441
  141.7 1.1 collective-permute-done.14.refs_2_
  142.8 0.9 sum.5
  143.7 3.3 %collective-permute-done.11.refs_2_ = bf16[160,512]{1,0:T(8,128)(2,1)S(1)} collective-permute-done((bf16[160,512]{1,0:T(8,128)(2,1)}, bf16[160,512]{1,0:T(8,128)(2,1)S(1)}, u32[]{:S(2)}, u32[]{:S(2)}) %collective-permute-start.11) | collective-permute-done | bytes 163872 | tf_op jit(solution)/shard_map/ppermute | solution.py:445
  147.0 0.0 collective-permute-done.12.refs_3_
  147.0 0.1 sum.4
  147.0 0.9 reshape.30
  (20 shorter events, 0.1 us)
Async XLA Ops:
  4.4 2.4 %collective-permute-start = (bf16[128,256]{1,0:T(8,128)(2,1)S(1)}, bf16[128,256]{1,0:T(8,128)(2,1)S(1)}, u32[]{:S(2)}, u32[]{:S(2)}) collective-permute-start(bf16[128,256]{1,0:T(8,128)(2,1)S(1)} %select_bitcast_fusion), channel_id=1, source_target_pairs={{0,4},{4,0},{1,5},{5,1},{2,6},{6,2},{3,7},{7,3},{8,12},{12,8},{9,1... | collective-permute-start | bytes 196616 | tf_op jit(solution)/shard_map/ppermute | solution.py:405
  8.4 8.0 %copy-start = (bf16[128,5120]{1,0:T(8,128)(2,1)S(1)}, bf16[128,5120]{1,0:T(8,128)(2,1)}, u32[]{:S(2)}) copy-start(bf16[128,5120]{1,0:T(8,128)(2,1)} %hidden.1) | copy-start | bytes 3932164
  8.4 37.2 %all-to-all-start = ((bf16[16,256,256]{2,1,0:T(8,128)(2,1)}), bf16[16,256,256]{2,1,0:T(8,128)(2,1)S(1)}, u32[]{:S(2)}, u32[]{:S(2)}) async-start(bf16[16,256,256]{2,1,0:T(8,128)(2,1)} %broadcast_in_dim.2), calls=%async_computation | async-start | bytes 4194304 | tf_op jit(solution)/shard_map/all_to_all | solution.py:409
  19.7 5.6 %copy-start.5 = (bf16[8,128,2,256]{3,2,1,0:T(2,128)(2,1)S(1)}, bf16[8,128,2,256]{3,2,1,0:T(2,128)(2,1)}, u32[]{:S(2)}) copy-start(bf16[8,128,2,256]{3,2,1,0:T(2,128)(2,1)} %param.12) | copy-start | bytes 3145732
  45.6 6.6 %copy-start.1 = (s32[32,8]{0,1:T(8,128)S(1)}, s32[32,8]{0,1:T(8,128)}, u32[]{:S(2)}) copy-start(s32[32,8]{0,1:T(8,128)} %param.14) | copy-start | bytes 3076
  45.6 6.6 %copy-start.2 = (s32[32]{0:T(128)S(1)}, s32[32]{0:T(128)}, u32[]{:S(2)}) copy-start(s32[32]{0:T(128)} %pack_counts.1) | copy-start | bytes 388
  45.6 6.6 %copy-start.3 = (s32[32]{0:T(128)S(1)}, s32[32]{0:T(128)}, u32[]{:S(2)}) copy-start(s32[32]{0:T(128)} %block_group.1) | copy-start | bytes 388
  45.6 6.5 %collective-permute-start.1 = (bf16[32,128,256]{2,1,0:T(8,128)(2,1)S(1)}, bf16[32,128,256]{2,1,0:T(8,128)(2,1)}, u32[]{:S(2)}, u32[]{:S(2)}) collective-permute-start(bf16[32,128,256]{2,1,0:T(8,128)(2,1)S(1)} %after.2.near), channel_id=1, source_target_pairs={{0,4},{4,0},{1,5},{5,1},{2,6},{6,2},{3,7},{7,3},{8,12},{12,8},{9,1... | collective-permute-start | bytes 6291464 | tf_op jit(solution)/shard_map/ppermute | solution.py:405
  48.3 29.4 %all-to-all-start.1 = ((bf16[8,640,128]{2,1,0:T(8,128)(2,1)}), bf16[8,640,128]{2,1,0:T(8,128)(2,1)S(1)}, u32[]{:S(2)}, u32[]{:S(2)}) async-start(bf16[8,640,128]{2,1,0:T(8,128)(2,1)} %columns.1.refs_2_), calls=%async_computation.1 | async-start | bytes 2621440 | tf_op jit(solution)/shard_map/all_to_all | solution.py:409
  77.7 7.7 %copy-start.4 = (bf16[16,128,512]{2,1,0:T(8,128)(2,1)S(1)}, bf16[16,128,512]{2,1,0:T(8,128)(2,1)}, u32[]{:S(2)}) copy-start(bf16[16,128,512]{2,1,0:T(8,128)(2,1)} %get-tuple-element.21) | copy-start | bytes 6291460
  77.7 7.7 %collective-permute-start.2 = (bf16[16,128,512]{2,1,0:T(8,128)(2,1)}, bf16[16,128,512]{2,1,0:T(8,128)(2,1)S(1)}, u32[]{:S(2)}, u32[]{:S(2)}) collective-permute-start(bf16[16,128,512]{2,1,0:T(8,128)(2,1)} %after.3), channel_id=1, source_target_pairs={{0,4},{4,0},{1,5},{5,1},{2,6},{6,2},{3,7},{7,3},{8,12},{12,8},{9,1... | collective-permute-start | bytes 6291464 | tf_op jit(solution)/shard_map/ppermute | solution.py:405
  118.2 12.2 %collective-permute-start.5 = (bf16[128,512]{1,0:T(8,128)(2,1)S(1)}, bf16[128,512]{1,0:T(8,128)(2,1)S(1)}, u32[]{:S(2)}, u32[]{:S(2)}) collective-permute-start(bf16[128,512]{1,0:T(8,128)(2,1)S(1)} %sum.3.refs_0_.block), channel_id=1, source_target_pairs={{0,24},{8,0},{16,8},{24,16},{1,25},{9,1},{17,9},{25,17},{2,26},{10... | collective-permute-start | bytes 393224 | tf_op jit(solution)/shard_map/ppermute | solution.py:445
  119.6 10.7 %collective-permute-start.4 = (bf16[128,512]{1,0:T(8,128)(2,1)S(1)}, bf16[128,512]{1,0:T(8,128)(2,1)S(1)}, u32[]{:S(2)}, u32[]{:S(2)}) collective-permute-start(bf16[128,512]{1,0:T(8,128)(2,1)S(1)} %sum.3.refs_0_.block), channel_id=1, source_target_pairs={{0,16},{8,24},{16,0},{24,8},{1,17},{9,25},{17,1},{25,9},{2,18},{10... | collective-permute-start | bytes 393224 | tf_op jit(solution)/shard_map/ppermute | solution.py:445
  120.6 10.2 %collective-permute-start.3 = (bf16[128,512]{1,0:T(8,128)(2,1)S(1)}, bf16[128,512]{1,0:T(8,128)(2,1)S(1)}, u32[]{:S(2)}, u32[]{:S(2)}) collective-permute-start(bf16[128,512]{1,0:T(8,128)(2,1)S(1)} %sum.3.refs_0_.block), channel_id=1, source_target_pairs={{0,8},{8,16},{16,24},{24,0},{1,9},{9,17},{17,25},{25,1},{2,10},{10... | collective-permute-start | bytes 393224 | tf_op jit(solution)/shard_map/ppermute | solution.py:445
  124.7 12.4 %collective-permute-start.13 = (bf16[128,1280]{1,0:T(8,128)(2,1)S(1)}, bf16[128,1280]{1,0:T(8,128)(2,1)S(1)}, u32[]{:S(2)}, u32[]{:S(2)}) collective-permute-start(bf16[128,1280]{1,0:T(8,128)(2,1)S(1)} %get-tuple-element.28), channel_id=1, source_target_pairs={{0,2},{1,3},{2,0},{3,1},{4,6},{5,7},{6,4},{7,5},{8,10},{9,11},{10,... | collective-permute-start | bytes 983048 | tf_op jit(solution)/shard_map/ppermute | solution.py:445
  127.5 3.8 %collective-permute-start.6 = (bf16[128,512]{1,0:T(8,128)(2,1)S(1)}, bf16[128,512]{1,0:T(8,128)(2,1)S(1)}, u32[]{:S(2)}, u32[]{:S(2)}) collective-permute-start(bf16[128,512]{1,0:T(8,128)(2,1)S(1)} %sum.3.refs_0_.block), channel_id=1, source_target_pairs={{0,4},{4,0},{1,5},{5,1},{2,6},{6,2},{3,7},{7,3},{8,12},{12,8},{9,1... | collective-permute-start | bytes 393224 | tf_op jit(solution)/shard_map/ppermute | solution.py:405
  130.3 1.3 collective-permute-start.9
  130.3 3.7 %collective-permute-start.8 = (bf16[128,512]{1,0:T(8,128)(2,1)S(1)}, bf16[128,512]{1,0:T(8,128)(2,1)S(1)}, u32[]{:S(2)}, u32[]{:S(2)}) collective-permute-start(bf16[128,512]{1,0:T(8,128)(2,1)S(1)} %collective-permute-done.4.refs_2_), channel_id=1, source_target_pairs={{0,4},{4,0},{1,5},{5,1},{2,6},{6,2},{3,7},{7,3},{8,12},{12,8},{9,1... | collective-permute-start | bytes 393224 | tf_op jit(solution)/shard_map/ppermute | solution.py:405
  130.8 3.2 %collective-permute-start.7 = (bf16[128,512]{1,0:T(8,128)(2,1)S(1)}, bf16[128,512]{1,0:T(8,128)(2,1)S(1)}, u32[]{:S(2)}, u32[]{:S(2)}) collective-permute-start(bf16[128,512]{1,0:T(8,128)(2,1)S(1)} %collective-permute-done.3.refs_1_), channel_id=1, source_target_pairs={{0,4},{4,0},{1,5},{5,1},{2,6},{6,2},{3,7},{7,3},{8,12},{12,8},{9,1... | collective-permute-start | bytes 393224 | tf_op jit(solution)/shard_map/ppermute | solution.py:405
  131.3 11.5 %collective-permute-start.14 = (bf16[128,1280]{1,0:T(8,128)(2,1)}, bf16[128,1280]{1,0:T(8,128)(2,1)S(1)}, u32[]{:S(2)}, u32[]{:S(2)}) collective-permute-start(bf16[128,1280]{1,0:T(8,128)(2,1)} %get-tuple-element.29), channel_id=1, source_target_pairs={{0,1},{1,2},{2,3},{3,0},{4,5},{5,6},{6,7},{7,4},{8,9},{9,10},{10,1... | collective-permute-start | bytes 983048 | tf_op jit(solution)/shard_map/ppermute | solution.py:445
  131.7 11.1 %collective-permute-start.15 = (bf16[128,1280]{1,0:T(8,128)(2,1)}, bf16[128,1280]{1,0:T(8,128)(2,1)S(1)}, u32[]{:S(2)}, u32[]{:S(2)}) collective-permute-start(bf16[128,1280]{1,0:T(8,128)(2,1)} %get-tuple-element.30), channel_id=1, source_target_pairs={{0,3},{1,0},{2,1},{3,2},{4,7},{5,4},{6,5},{7,6},{8,11},{9,8},{10,9... | collective-permute-start | bytes 983048 | tf_op jit(solution)/shard_map/ppermute | solution.py:445
  135.7 8.0 %collective-permute-start.10 = (bf16[160,512]{1,0:T(8,128)(2,1)}, bf16[160,512]{1,0:T(8,128)(2,1)S(1)}, u32[]{:S(2)}, u32[]{:S(2)}) collective-permute-start(bf16[160,512]{1,0:T(8,128)(2,1)} %get-tuple-element.24), channel_id=1, source_target_pairs={{0,64},{32,96},{64,0},{96,32},{1,65},{33,97},{65,1},{97,33},{2,66}... | collective-permute-start | bytes 491528 | tf_op jit(solution)/shard_map/ppermute | solution.py:445
  136.9 10.1 %collective-permute-start.11 = (bf16[160,512]{1,0:T(8,128)(2,1)}, bf16[160,512]{1,0:T(8,128)(2,1)S(1)}, u32[]{:S(2)}, u32[]{:S(2)}) collective-permute-start(bf16[160,512]{1,0:T(8,128)(2,1)} %get-tuple-element.25), channel_id=1, source_target_pairs={{0,32},{32,64},{64,96},{96,0},{1,33},{33,65},{65,97},{97,1},{2,34}... | collective-permute-start | bytes 491528 | tf_op jit(solution)/shard_map/ppermute | solution.py:445
  137.1 9.9 %collective-permute-start.12 = (bf16[160,512]{1,0:T(8,128)(2,1)}, bf16[160,512]{1,0:T(8,128)(2,1)S(1)}, u32[]{:S(2)}, u32[]{:S(2)}) collective-permute-start(bf16[160,512]{1,0:T(8,128)(2,1)} %get-tuple-element.26), channel_id=1, source_target_pairs={{0,96},{32,0},{64,32},{96,64},{1,97},{33,1},{65,33},{97,65},{2,98}... | collective-permute-start | bytes 491528 | tf_op jit(solution)/shard_map/ppermute | solution.py:445

commit v4 on v3

--- a/solution.py
+++ b/solution.py
@@ -30,8 +30,8 @@
 
 def attention_kernel(
     pack_counts, slot_groups, block_group, queries_hbm, grads_hbm, own_hbm, near, far,
-    out_hbm, qgrad_hbm, own_grad_hbm, keep_hbm, send_hbm,
-    queries, grads, out, qgrad, own, own_grad, keep, send, accum,
+    out_hbm, qgrad_hbm, own_grad_hbm, send_k_hbm, send_v_hbm, keep_k_hbm, keep_v_hbm,
+    queries, grads, out, qgrad, own, own_grad, send_k, send_v, keep_k, keep_v, accum,
     expd_0, expd_1, inverse_0, inverse_1, order, filled, sems,
 ):
     core = lax.axis_index("c")
@@ -183,12 +183,18 @@
 
     halves = []
     for place, (half, half_hbm, mine) in enumerate(
-        ((send, send_hbm, 1 - core), (keep, keep_hbm, core))
+        (
+            (send_k, send_k_hbm, 1 - core),
+            (send_v, send_v_hbm, 1 - core),
+            (keep_k, keep_k_hbm, core),
+            (keep_v, keep_v_hbm, core),
+        )
     ):
+        cols = slice(place % 2 * 2 * HD, (place % 2 + 1) * 2 * HD)
         for part in range(4):
             chips = pl.ds(4 * part, 4)
             for chip in range(4 * part, 4 * part + 4):
-                half[chip] = accum[2 * chip + mine].astype(BF16)
+                half[chip] = accum[2 * chip + mine, :, cols].astype(BF16)
             copy = pltpu.make_async_copy(
                 half.at[chips], half_hbm.at[chips], sems.at[6 + place, part]
             )
@@ -254,6 +260,61 @@
         compiler_params=pltpu.CompilerParams(vmem_limit_bytes=8 * 2**20),
         name="columns",
     )(hidden)
+
+
+def split_kernel(axis, keep, got, *parts):
+    here = lax.axis_index(axis)
+    for step, part in enumerate(parts):
+        place = lax.rem(here + step, 4)
+        for i in range(4):
+            chip = place * 4 + i if axis == "y" else i * 4 + place
+            part[i] = (keep[chip].astype(F32) + got[chip].astype(F32)).astype(BF16)
+
+
+def split_sum(keep, got, axis):
+    shape = (4,) + keep.shape[1:]
+    return pl.pallas_call(
+        functools.partial(split_kernel, axis),
+        out_shape=[jax.ShapeDtypeStruct(shape, BF16)] * 4,
+        compiler_params=pltpu.CompilerParams(vmem_limit_bytes=12 * 2**20),
+        name="split",
+    )(keep, got)
+
+
+def reduce_kernel(axis, *refs):
+    here = lax.axis_index(axis)
+    for step in range(4):
+        place = lax.rem(here + step, 4)
+        total = refs[0][place].astype(F32)
+        for ref in refs[1:4]:
+            total = total + ref[place].astype(F32)
+        refs[4 + step][...] = total.astype(BF16)
+
+
+def reduce_of(parts, axis):
+    return pl.pallas_call(
+        functools.partial(reduce_kernel, axis),
+        out_shape=[jax.ShapeDtypeStruct(parts[0].shape[1:], BF16)] * 4,
+        compiler_params=pltpu.CompilerParams(vmem_limit_bytes=8 * 2**20),
+        name="reduce",
+    )(*parts)
+
+
+def block_kernel(*refs):
+    for half in range(2):
+        total = refs[4 * half][...].astype(F32)
+        for ref in refs[4 * half + 1 : 4 * half + 4]:
+            total = total + ref[...].astype(F32)
+        refs[8][:, half * 2 * HD : (half + 1) * 2 * HD] = total.astype(BF16)
+
+
+def block_of(keys, values):
+    return pl.pallas_call(
+        block_kernel,
+        out_shape=jax.ShapeDtypeStruct((keys[0].shape[0], 4 * HD), BF16),
+        compiler_params=pltpu.CompilerParams(vmem_limit_bytes=8 * 2**20),
+        name="block",
+    )(*keys, *values)
 
 
 def term_kernel(hidden, *refs):
@@ -360,23 +421,22 @@
     smem = pl.BlockSpec(memory_space=pltpu.SMEM)
     anywhere = pl.BlockSpec(memory_space=pl.ANY)
     rows = BLOCKS * RESP + RESP
-    shared = (N_DP // 2, RESP, 4 * HD)
+    shared = (N_DP // 2, RESP, 2 * HD)
     outer = [in_hbm(array) for array in (queries, out_grad, own)]
     inner = [pltpu.with_memory_space_constraint(array, pltpu.VMEM) for array in (near, far)]
     return pl.pallas_call(
         attention_kernel,
         in_specs=[smem] * 3 + [anywhere] * 3 + [vmem] * 2,
-        out_specs=[anywhere] * 5,
+        out_specs=[anywhere] * 7,
         out_shape=[
             pltpu.HBM(queries.shape, BF16),
             pltpu.HBM(queries.shape, BF16),
             pltpu.HBM(own.shape, BF16),
-            pltpu.HBM(shared, BF16),
-            pltpu.HBM(shared, BF16),
+            *[pltpu.HBM(shared, BF16) for _ in range(4)],
         ],
         scratch_shapes=[pltpu.VMEM(queries.shape, BF16)] * 4
         + [pltpu.VMEM(own.shape, BF16)] * 2
-        + [pltpu.VMEM(shared, BF16)] * 2
+        + [pltpu.VMEM(shared, BF16)] * 4
         + [
             pltpu.VMEM((N_DP, RESP, 4 * HD), F32),
             pltpu.VMEM((rows, REPEATS * RESP), BF16),
@@ -385,7 +445,7 @@
             pltpu.VMEM((1, REPEATS * RESP), F32),
             pltpu.SMEM((N_DP,), jnp.int32),
             pltpu.SMEM((GROUPS,), jnp.int32),
-            pltpu.SemaphoreType.DMA((8, SLOTS)),
+            pltpu.SemaphoreType.DMA((10, SLOTS)),
         ],
         cost_estimate=pl.CostEstimate(
             flops=6 * 2 * 2 * SLOTS * REPEATS * RESP * rows * HD,
@@ -433,16 +493,23 @@
     near = after(near, (in_hbm(own), in_hbm(columns), in_hbm(relaid)), pltpu.VMEM)
     hidden_y = exchange(columns, ("z", "c"))
 
-    outs, qgrads, own_grad, keep, send = attention(
+    outs, qgrads, own_grad, send_k, send_v, keep_k, keep_v = attention(
         pack_counts, slot_groups, block_group, queries, out_grad, own, near, swap_cores(near)
     )
-    send = after(send, (hidden_y,), pltpu.HBM)
-    partial = (keep.astype(F32) + swap_cores(send).astype(F32)).astype(BF16)
     own_grad = own_grad.reshape(SLOTS, RESP, 2, 2 * HD)
-    block_b = sum_of([exchange(partial, ("y", "z"))], BF16)
 
     def ring(array, axis, step):
         return lax.ppermute(array, axis, [(i, (i + step) % 4) for i in range(4)])
+
+    def deal(parts, axis):
+        return [parts[0]] + [ring(parts[step], axis, step) for step in (1, 2, 3)]
+
+    send_k = after(send_k, (hidden_y,), pltpu.HBM)
+    keys = deal(split_sum(keep_k, swap_cores(send_k), "y"), "y")
+    values = deal(split_sum(keep_v, swap_cores(send_v), "z"), "z")
+    keys = deal(reduce_of(keys, "z"), "z")
+    values = deal(reduce_of(values, "y"), "y")
+    block_b = block_of(keys, values)
 
     terms = prompt_terms(block_b, relaid)
     prompt_grad = sum_of([terms[0], *[ring(terms[step], "x", step) for step in (2, 1, 3)]], BF16)

time: 149 us -> 149 us (level)
  blocking collectives: 31.8 us -> 0 us
  waiting for transfers between devices: 29 us -> 45.2 us
  starting transfers between devices: 34.4 us -> 41.6 us
  Pallas kernels: 35.8 us -> 42.9 us
    all_to_all x1 -> x0, blocking collectives: 31.8 us -> none  [exchange(): return lax.all_to_all(array, axes, 0, 0, tiled=True)]
    ppermute x9 -> x21, waiting for transfers between devices: 4.4 us -> 22.8 us  [ring(): return lax.ppermute(array, axis, [(i, (i + step) % 4) for i in range(4)])]
    ppermute x9 -> x21, starting transfers between devices: 11.7 us -> 20.2 us  [ring(): return lax.ppermute(array, axis, [(i, (i + step) % 4) for i in range(4)])]
    pallas_call x1, Pallas kernels: 25.5 us -> 32 us  [attention(): pl.pallas_call(attention_kernel, in_specs=[smem] * 3 + [anywhere] * 3 + [...]
    ppermute x7 -> x8, waiting for transfers between devices: 5.73 us -> 3.5 us  [swap_cores(): return lax.ppermute(array, 'c', [(0, 1), (1, 0)])]
    ppermute x7 -> x8, starting transfers between devices: 11.2 us -> 9.94 us  [swap_cores(): return lax.ppermute(array, 'c', [(0, 1), (1, 0)])]
    unnamed x13 -> x17, local copies, waits for them, and re-layouts: 5.6 us -> 6.69 us
  transfers between devices with their start and end apart: 18 -> 31, of which waited for: 8 -> 14; matrix products, arithmetic and copies ran while one was open for 6% -> 6% of each run, Pallas kernels for 24% -> 29%
where the time goes in v4:
time: 149 us; the launch traced here: 147 us
  waiting for transfers between devices  45.2 us (30%)
  Pallas kernels  42.9 us (29%)
  starting transfers between devices  41.6 us (28%)
  local copies, waits for them, and re-layouts  12.7 us (9%)
  matrix products  3.75 us (3%)
    pallas_call x1, Pallas kernels, attention(): pl.pallas_call(attention_kernel, in_specs=[smem] * 3 + [anywhere] * 3 + [...  32 us
    ppermute x21, waiting for transfers between devices, ring(): return lax.ppermute(array, axis, [(i, (i + step) % 4) for i in range(4)])  22.8 us
    ppermute x21, starting transfers between devices, ring(): return lax.ppermute(array, axis, [(i, (i + step) % 4) for i in range(4)])  20.2 us
    all_to_all x2, waiting for transfers between devices, exchange(): return lax.all_to_all(array, axes, 0, 0, tiled=True)  18.9 us
    all_to_all x2, starting transfers between devices, exchange(): return lax.all_to_all(array, axes, 0, 0, tiled=True)  11.5 us
    ppermute x8, starting transfers between devices, swap_cores(): return lax.ppermute(array, 'c', [(0, 1), (1, 0)])  9.94 us
    unnamed x17, local copies, waits for them, and re-layouts  6.69 us
    pallas_call x1, Pallas kernels, prompt_terms(): pl.pallas_call(prompt_kernel, out_shape=[jax.ShapeDtypeStruct(shape, BF16...  4.05 us
  transfers between devices with their start and end apart: 31, of which 14 were waited for; matrix products, arithmetic and copies ran while one was open for 6% of the time, Pallas kernels for 29%

profile of v4, /device:TPU:1, one launch (start us, length us, event | category | flops | bytes accessed | tf_op | source)
XLA Modules:
  0.0 147.1 jit_solution(1798896742193715956)
XLA Ops:
  0.6 3.8 %fusion.3 = bf16[128,2,256]{2,0,1:T(8,128)(2,1)S(1)} fusion(bf16[5120,2,256]{2,1,0:T(2,128)(2,1)} %param.9, bf16[128,5120]{1,0:T(8,128)(2,1)} %hidden.1), kind=kOutput, calls=%fused_computation.4 | convolution fusion | flops 671154176 | bytes 6684672 | tf_op jit(solution)/shard_map/pd,dkc->pkc/dot_general | solution.py:479
  4.4 1.5 %collective-permute-start = (bf16[128,256]{1,0:T(8,128)(2,1)S(1)}, bf16[128,256]{1,0:T(8,128)(2,1)S(1)}, u32[]{:S(2)}, u32[]{:S(2)}) collective-permute-start(bf16[128,256]{1,0:T(8,128)(2,1)S(1)} %select_bitcast_fusion), channel_id=1, source_target_pairs={{0,4},{4,0},{1,5},{5,1},{2,6},{6,2},{3,7},{7,3},{8,12},{12,8},{9,1... | collective-permute-start | bytes 196616 | tf_op jit(solution)/shard_map/ppermute | solution.py:465
  5.9 0.9 collective-permute-done
  6.9 1.5 %broadcast_in_dim.2 = bf16[16,256,256]{2,1,0:T(8,128)(2,1)} broadcast(bf16[256,256]{1,0:T(8,128)(2,1)S(1)} %pad_maximum_fusion), dimensions={1,2} | broadcast | bytes 2228224 | tf_op jit(solution)/shard_map/broadcast_in_dim | solution.py:487
  8.4 8.0 %all-to-all-start = ((bf16[16,256,256]{2,1,0:T(8,128)(2,1)}), bf16[16,256,256]{2,1,0:T(8,128)(2,1)S(1)}, u32[]{:S(2)}, u32[]{:S(2)}) async-start(bf16[16,256,256]{2,1,0:T(8,128)(2,1)} %broadcast_in_dim.2), calls=%async_computation | async-start | bytes 4194304 | tf_op jit(solution)/shard_map/all_to_all | solution.py:469
  16.4 3.3 %columns.1.refs_2_ = bf16[8,640,128]{2,1,0:T(8,128)(2,1)} custom-call(bf16[128,5120]{1,0:T(8,128)(2,1)S(1)} %copy-done), custom_call_target="tpu_custom_call" | custom-call | tf_op jit(solution)/shard_map/columns/pallas_call | solution.py:257
  19.7 5.6 %copy.22 = bf16[5120,2,256]{2,0,1:T(8,128)(2,1)} copy(bf16[5120,2,256]{2,1,0:T(2,128)(2,1)} %param.9) | data formatting | bytes 10485760 | tf_op args[1]
  25.3 1.5 reshape.27.refs_1_.own_hbm
  26.7 18.9 %all-to-all-done = bf16[16,256,256]{2,1,0:T(8,128)(2,1)S(1)} async-done(((bf16[16,256,256]{2,1,0:T(8,128)(2,1)}), bf16[16,256,256]{2,1,0:T(8,128)(2,1)S(1)}, u32[]{:S(2)}, u32[]{:S(2)}) %all-to-all-start) | async-done | bytes 2097184 | tf_op jit(solution)/shard_map/all_to_all | solution.py:469
  45.6 2.6 %collective-permute-start.1 = (bf16[32,128,256]{2,1,0:T(8,128)(2,1)S(1)}, bf16[32,128,256]{2,1,0:T(8,128)(2,1)}, u32[]{:S(2)}, u32[]{:S(2)}) collective-permute-start(bf16[32,128,256]{2,1,0:T(8,128)(2,1)S(1)} %after.2.near), channel_id=1, source_target_pairs={{0,4},{4,0},{1,5},{5,1},{2,6},{6,2},{3,7},{7,3},{8,12},{12,8},{9,1... | collective-permute-start | bytes 6291464 | tf_op jit(solution)/shard_map/ppermute | solution.py:465
  48.3 3.5 %all-to-all-start.1 = ((bf16[8,640,128]{2,1,0:T(8,128)(2,1)}), bf16[8,640,128]{2,1,0:T(8,128)(2,1)S(1)}, u32[]{:S(2)}, u32[]{:S(2)}) async-start(bf16[8,640,128]{2,1,0:T(8,128)(2,1)} %columns.1.refs_2_), calls=%async_computation.1 | async-start | bytes 2621440 | tf_op jit(solution)/shard_map/all_to_all | solution.py:469
  51.8 0.4 collective-permute-done.1.far
  52.2 32.0 %attention.1 = (bf16[8,128,1280]{2,1,0:T(8,128)(2,1)}, bf16[8,128,1280]{2,1,0:T(8,128)(2,1)}, bf16[8,128,512]{2,1,0:T(8,128)(2,1)}, bf16[16,128,256]{2,1,0:T(8,1...) custom-call(s32[32]{0:T(128)S(1)} %copy-done.4, ...), custom_call_target="tpu_custom_call" | custom-call | flops 10066329600 | bytes 16777216 | tf_op jit(solution)/shard_map/attention/pallas_call | solution.py:427
  84.4 1.1 copy-done.7
  85.4 1.8 %collective-permute-done.2.got = bf16[16,128,256]{2,1,0:T(8,128)(2,1)S(1)} collective-permute-done((bf16[16,128,256]{2,1,0:T(8,128)(2,1)}, bf16[16,128,256]{2,1,0:T(8,128)(2,1)S(1)}, u32[]{:S(2)}, u32[]{:S(2)}) %collective-permute-start.2) | collective-permute-done | bytes 1048608 | tf_op jit(solution)/shard_map/ppermute | solution.py:465
  87.2 0.2 split.2
  87.6 2.6 %collective-permute-start.5 = (bf16[4,128,256]{2,1,0:T(8,128)(2,1)S(1)}, bf16[4,128,256]{2,1,0:T(8,128)(2,1)S(1)}, u32[]{:S(2)}, u32[]{:S(2)}) collective-permute-start(bf16[4,128,256]{2,1,0:T(8,128)(2,1)S(1)} %get-tuple-element.44), channel_id=1, source_target_pairs={{0,96},{32,0},{64,32},{96,64},{1,97},{33,1},{65,33},{97,65},{2,98}... | collective-permute-start | bytes 786440 | tf_op jit(solution)/shard_map/ppermute | solution.py:502
  90.2 0.2 split.3
  90.5 0.3 collective-permute-start.11
  90.8 11.4 %collective-permute-done.3.refs_1_ = bf16[4,128,256]{2,1,0:T(8,128)(2,1)S(1)} collective-permute-done((bf16[4,128,256]{2,1,0:T(8,128)(2,1)S(1)}, bf16[4,128,256]{2,1,0:T(8,128)(2,1)S(1)}, u32[]{:S(2)}, u32[]{:S(2)}) %collective-permute-start.3) | collective-permute-done | bytes 262176 | tf_op jit(solution)/shard_map/ppermute | solution.py:502
  102.2 0.2 collective-permute-done.5.refs_3_
  102.6 1.3 collective-permute-start.6
  103.9 0.6 collective-permute-done.10.refs_1_
  104.5 1.9 %collective-permute-start.8 = (bf16[128,256]{1,0:T(8,128)(2,1)S(1)}, bf16[128,256]{1,0:T(8,128)(2,1)S(1)}, u32[]{:S(2)}, u32[]{:S(2)}) collective-permute-start(bf16[128,256]{1,0:T(8,128)(2,1)S(1)} %get-tuple-element.48), channel_id=1, source_target_pairs={{0,24},{8,0},{16,8},{24,16},{1,25},{9,1},{17,9},{25,17},{2,26},{10... | collective-permute-start | bytes 196616 | tf_op jit(solution)/shard_map/ppermute | solution.py:502
  106.4 2.8 %collective-permute-done.12.refs_3_ = bf16[4,128,256]{2,1,0:T(8,128)(2,1)S(1)} collective-permute-done((bf16[4,128,256]{2,1,0:T(8,128)(2,1)S(1)}, bf16[4,128,256]{2,1,0:T(8,128)(2,1)S(1)}, u32[]{:S(2)}, u32[]{:S(2)}) %collective-permute-start.12) | collective-permute-done | bytes 262176 | tf_op jit(solution)/shard_map/ppermute | solution.py:502
  109.4 0.4 collective-permute-start.14
  109.8 2.2 %collective-permute-start.15 = (bf16[128,256]{1,0:T(8,128)(2,1)S(1)}, bf16[128,256]{1,0:T(8,128)(2,1)S(1)}, u32[]{:S(2)}, u32[]{:S(2)}) collective-permute-start(bf16[128,256]{1,0:T(8,128)(2,1)S(1)} %get-tuple-element.58), channel_id=1, source_target_pairs={{0,96},{32,0},{64,32},{96,64},{1,97},{33,1},{65,33},{97,65},{2,98}... | collective-permute-start | bytes 196616 | tf_op jit(solution)/shard_map/ppermute | solution.py:502
  112.0 1.9 %collective-permute-done.13.refs_5_ = bf16[128,256]{1,0:T(8,128)(2,1)S(1)} collective-permute-done((bf16[128,256]{1,0:T(8,128)(2,1)S(1)}, bf16[128,256]{1,0:T(8,128)(2,1)S(1)}, u32[]{:S(2)}, u32[]{:S(2)}) %collective-permute-start.13) | collective-permute-done | bytes 65568 | tf_op jit(solution)/shard_map/ppermute | solution.py:502
  114.0 0.4 collective-permute-done.14.refs_6_
  114.4 0.5 collective-permute-done.15.refs_7_
  115.0 1.6 %collective-permute-start.18 = (bf16[128,512]{1,0:T(8,128)(2,1)S(1)}, bf16[128,512]{1,0:T(8,128)(2,1)S(1)}, u32[]{:S(2)}, u32[]{:S(2)}) collective-permute-start(bf16[128,512]{1,0:T(8,128)(2,1)S(1)} %block.1.refs_0_), channel_id=1, source_target_pairs={{0,24},{8,0},{16,8},{24,16},{1,25},{9,1},{17,9},{25,17},{2,26},{10... | collective-permute-start | bytes 393224 | tf_op jit(solution)/shard_map/ppermute | solution.py:502
  116.6 0.7 collective-permute-start.16
  117.3 4.0 %prompt.1 = (bf16[128,1280]{1,0:T(8,128)(2,1)S(1)}, bf16[128,1280]{1,0:T(8,128)(2,1)}, bf16[128,1280]{1,0:T(8,128)(2,1)S(1)}, bf16[128,1280]{1,0:T(8,128)(2,1)}) custom-call(bf16[128,512]{1,0:T(8,128)(2,1)S(1)} %block.1.refs_0_, bf16[2,5120,256]{2,1,0:T(8,128)(2,1)} %bitcast.18), custom_call_target="tpu_custom_call" | custom-call | flops 671088640 | bytes 4194304 | tf_op jit(solution)/shard_map/prompt/pallas_call | solution.py:380
  121.4 2.8 %collective-permute-start.26 = (bf16[128,1280]{1,0:T(8,128)(2,1)S(1)}, bf16[128,1280]{1,0:T(8,128)(2,1)S(1)}, u32[]{:S(2)}, u32[]{:S(2)}) collective-permute-start(bf16[128,1280]{1,0:T(8,128)(2,1)S(1)} %get-tuple-element.64), channel_id=1, source_target_pairs={{0,2},{1,3},{2,0},{3,1},{4,6},{5,7},{6,4},{7,5},{8,10},{9,11},{10,... | collective-permute-start | bytes 983048 | tf_op jit(solution)/shard_map/ppermute | solution.py:502
  124.2 5.1 %collective-permute-start.19 = (bf16[128,512]{1,0:T(8,128)(2,1)S(1)}, bf16[128,512]{1,0:T(8,128)(2,1)S(1)}, u32[]{:S(2)}, u32[]{:S(2)}) collective-permute-start(bf16[128,512]{1,0:T(8,128)(2,1)S(1)} %block.1.refs_0_), channel_id=1, source_target_pairs={{0,4},{4,0},{1,5},{5,1},{2,6},{6,2},{3,7},{7,3},{8,12},{12,8},{9,1... | collective-permute-start | bytes 393224 | tf_op jit(solution)/shard_map/ppermute | solution.py:465
  129.3 0.5 collective-permute-start.21
  129.9 0.4 collective-permute-done.19.refs_4_
  130.3 0.3 collective-permute-start.27
  130.7 2.3 %collective-permute-start.28 = (bf16[128,1280]{1,0:T(8,128)(2,1)}, bf16[128,1280]{1,0:T(8,128)(2,1)S(1)}, u32[]{:S(2)}, u32[]{:S(2)}) collective-permute-start(bf16[128,1280]{1,0:T(8,128)(2,1)} %get-tuple-element.66), channel_id=1, source_target_pairs={{0,3},{1,0},{2,1},{3,2},{4,7},{5,4},{6,5},{7,6},{8,11},{9,8},{10,9... | collective-permute-start | bytes 983048 | tf_op jit(solution)/shard_map/ppermute | solution.py:502
  133.0 1.7 %term.1 = (bf16[160,512]{1,0:T(8,128)(2,1)S(1)}, bf16[160,512]{1,0:T(8,128)(2,1)}, bf16[160,512]{1,0:T(8,128)(2,1)}, bf16[160,512]{1,0:T(8,128)(2,1)}) custom-call(bf16[8,640,128]{2,1,0:T(8,128)(2,1)S(1)} %all-to-all-done.1.refs_1_.hidden, bf16[128,512]{1,0:T(8,128)(2,1)S(1)} %block.1.refs_0_, bf16[128,512]{1,0:T(8,128)(2,1)S(1)} %collective-permute-done.16.refs_1_, ...), custom_call_target="tpu_custom_call" | custom-call | flops 2000000000 | bytes 10000000 | tf_op jit(solution)/shard_map/term/pallas_call | solution.py:344
  134.7 0.8 collective-permute-start.23
  135.5 1.9 %collective-permute-start.24 = (bf16[160,512]{1,0:T(8,128)(2,1)}, bf16[160,512]{1,0:T(8,128)(2,1)S(1)}, u32[]{:S(2)}, u32[]{:S(2)}) collective-permute-start(bf16[160,512]{1,0:T(8,128)(2,1)} %get-tuple-element.61), channel_id=1, source_target_pairs={{0,32},{32,64},{64,96},{96,0},{1,33},{33,65},{65,97},{97,1},{2,34}... | collective-permute-start | bytes 491528 | tf_op jit(solution)/shard_map/ppermute | solution.py:502
  137.4 0.8 collective-permute-start.25
  138.2 2.1 %reshape.29 = bf16[8,128,2,256]{3,2,1,0:T(2,128)(2,1)} reshape(bf16[8,128,512]{2,1,0:T(8,128)(2,1)} %get-tuple-element.38) | data formatting | bytes 2097152 | tf_op jit(solution)/shard_map/reshape | solution.py:499
  140.3 0.8 collective-permute-done.27.refs_2_
  141.1 0.9 sum.3
  142.0 4.1 %collective-permute-done.24.refs_2_ = bf16[160,512]{1,0:T(8,128)(2,1)S(1)} collective-permute-done((bf16[160,512]{1,0:T(8,128)(2,1)}, bf16[160,512]{1,0:T(8,128)(2,1)S(1)}, u32[]{:S(2)}, u32[]{:S(2)}) %collective-permute-start.24) | collective-permute-done | bytes 163872 | tf_op jit(solution)/shard_map/ppermute | solution.py:502
  146.2 0.9 reshape.30
  (52 shorter events, 1.1 us)
Async XLA Ops:
  4.4 2.4 %collective-permute-start = (bf16[128,256]{1,0:T(8,128)(2,1)S(1)}, bf16[128,256]{1,0:T(8,128)(2,1)S(1)}, u32[]{:S(2)}, u32[]{:S(2)}) collective-permute-start(bf16[128,256]{1,0:T(8,128)(2,1)S(1)} %select_bitcast_fusion), channel_id=1, source_target_pairs={{0,4},{4,0},{1,5},{5,1},{2,6},{6,2},{3,7},{7,3},{8,12},{12,8},{9,1... | collective-permute-start | bytes 196616 | tf_op jit(solution)/shard_map/ppermute | solution.py:465
  8.4 8.0 %copy-start = (bf16[128,5120]{1,0:T(8,128)(2,1)S(1)}, bf16[128,5120]{1,0:T(8,128)(2,1)}, u32[]{:S(2)}) copy-start(bf16[128,5120]{1,0:T(8,128)(2,1)} %hidden.1) | copy-start | bytes 3932164
  8.4 37.2 %all-to-all-start = ((bf16[16,256,256]{2,1,0:T(8,128)(2,1)}), bf16[16,256,256]{2,1,0:T(8,128)(2,1)S(1)}, u32[]{:S(2)}, u32[]{:S(2)}) async-start(bf16[16,256,256]{2,1,0:T(8,128)(2,1)} %broadcast_in_dim.2), calls=%async_computation | async-start | bytes 4194304 | tf_op jit(solution)/shard_map/all_to_all | solution.py:469
  19.7 5.6 %copy-start.6 = (bf16[8,128,2,256]{3,2,1,0:T(2,128)(2,1)S(1)}, bf16[8,128,2,256]{3,2,1,0:T(2,128)(2,1)}, u32[]{:S(2)}) copy-start(bf16[8,128,2,256]{3,2,1,0:T(2,128)(2,1)} %param.12) | copy-start | bytes 3145732
  45.6 6.6 %copy-start.3 = (s32[32,8]{0,1:T(8,128)S(1)}, s32[32,8]{0,1:T(8,128)}, u32[]{:S(2)}) copy-start(s32[32,8]{0,1:T(8,128)} %param.14) | copy-start | bytes 3076
  45.6 6.6 %copy-start.4 = (s32[32]{0:T(128)S(1)}, s32[32]{0:T(128)}, u32[]{:S(2)}) copy-start(s32[32]{0:T(128)} %pack_counts.1) | copy-start | bytes 388
  45.6 6.6 %copy-start.5 = (s32[32]{0:T(128)S(1)}, s32[32]{0:T(128)}, u32[]{:S(2)}) copy-start(s32[32]{0:T(128)} %block_group.1) | copy-start | bytes 388
  45.6 6.5 %collective-permute-start.1 = (bf16[32,128,256]{2,1,0:T(8,128)(2,1)S(1)}, bf16[32,128,256]{2,1,0:T(8,128)(2,1)}, u32[]{:S(2)}, u32[]{:S(2)}) collective-permute-start(bf16[32,128,256]{2,1,0:T(8,128)(2,1)S(1)} %after.2.near), channel_id=1, source_target_pairs={{0,4},{4,0},{1,5},{5,1},{2,6},{6,2},{3,7},{7,3},{8,12},{12,8},{9,1... | collective-permute-start | bytes 6291464 | tf_op jit(solution)/shard_map/ppermute | solution.py:465
  48.3 36.0 %all-to-all-start.1 = ((bf16[8,640,128]{2,1,0:T(8,128)(2,1)}), bf16[8,640,128]{2,1,0:T(8,128)(2,1)S(1)}, u32[]{:S(2)}, u32[]{:S(2)}) async-start(bf16[8,640,128]{2,1,0:T(8,128)(2,1)} %columns.1.refs_2_), calls=%async_computation.1 | async-start | bytes 2621440 | tf_op jit(solution)/shard_map/all_to_all | solution.py:469
  84.2 1.2 copy-start.7
  84.2 3.0 %copy-start.2 = (bf16[16,128,256]{2,1,0:T(8,128)(2,1)S(1)}, bf16[16,128,256]{2,1,0:T(8,128)(2,1)}, u32[]{:S(2)}) copy-start(bf16[16,128,256]{2,1,0:T(8,128)(2,1)} %get-tuple-element.39.keep) | copy-start | bytes 3145732
  84.2 6.0 %copy-start.1 = (bf16[16,128,256]{2,1,0:T(8,128)(2,1)S(1)}, bf16[16,128,256]{2,1,0:T(8,128)(2,1)}, u32[]{:S(2)}) copy-start(bf16[16,128,256]{2,1,0:T(8,128)(2,1)} %get-tuple-element.49.keep) | copy-start | bytes 3145732
  84.3 3.0 %collective-permute-start.2 = (bf16[16,128,256]{2,1,0:T(8,128)(2,1)}, bf16[16,128,256]{2,1,0:T(8,128)(2,1)S(1)}, u32[]{:S(2)}, u32[]{:S(2)}) collective-permute-start(bf16[16,128,256]{2,1,0:T(8,128)(2,1)} %after.3), channel_id=1, source_target_pairs={{0,4},{4,0},{1,5},{5,1},{2,6},{6,2},{3,7},{7,3},{8,12},{12,8},{9,1... | collective-permute-start | bytes 3145736 | tf_op jit(solution)/shard_map/ppermute | solution.py:465
  85.4 4.8 %collective-permute-start.9 = (bf16[16,128,256]{2,1,0:T(8,128)(2,1)S(1)}, bf16[16,128,256]{2,1,0:T(8,128)(2,1)S(1)}, u32[]{:S(2)}, u32[]{:S(2)}) collective-permute-start(bf16[16,128,256]{2,1,0:T(8,128)(2,1)S(1)} %copy-done.7), channel_id=1, source_target_pairs={{0,4},{4,0},{1,5},{5,1},{2,6},{6,2},{3,7},{7,3},{8,12},{12,8},{9,1... | collective-permute-start | bytes 3145736 | tf_op jit(solution)/shard_map/ppermute | solution.py:465
  87.5 14.7 %collective-permute-start.3 = (bf16[4,128,256]{2,1,0:T(8,128)(2,1)S(1)}, bf16[4,128,256]{2,1,0:T(8,128)(2,1)S(1)}, u32[]{:S(2)}, u32[]{:S(2)}) collective-permute-start(bf16[4,128,256]{2,1,0:T(8,128)(2,1)S(1)} %get-tuple-element.42), channel_id=1, source_target_pairs={{0,32},{32,64},{64,96},{96,0},{1,33},{33,65},{65,97},{97,1},{2,34}... | collective-permute-start | bytes 786440 | tf_op jit(solution)/shard_map/ppermute | solution.py:502
  87.5 14.7 %collective-permute-start.4 = (bf16[4,128,256]{2,1,0:T(8,128)(2,1)S(1)}, bf16[4,128,256]{2,1,0:T(8,128)(2,1)S(1)}, u32[]{:S(2)}, u32[]{:S(2)}) collective-permute-start(bf16[4,128,256]{2,1,0:T(8,128)(2,1)S(1)} %get-tuple-element.43), channel_id=1, source_target_pairs={{0,64},{32,96},{64,0},{96,32},{1,65},{33,97},{65,1},{97,33},{2,66}... | collective-permute-start | bytes 786440 | tf_op jit(solution)/shard_map/ppermute | solution.py:502
  87.6 14.8 %collective-permute-start.5 = (bf16[4,128,256]{2,1,0:T(8,128)(2,1)S(1)}, bf16[4,128,256]{2,1,0:T(8,128)(2,1)S(1)}, u32[]{:S(2)}, u32[]{:S(2)}) collective-permute-start(bf16[4,128,256]{2,1,0:T(8,128)(2,1)S(1)} %get-tuple-element.44), channel_id=1, source_target_pairs={{0,96},{32,0},{64,32},{96,64},{1,97},{33,1},{65,33},{97,65},{2,98}... | collective-permute-start | bytes 786440 | tf_op jit(solution)/shard_map/ppermute | solution.py:502
  90.5 14.0 %collective-permute-start.10 = (bf16[4,128,256]{2,1,0:T(8,128)(2,1)S(1)}, bf16[4,128,256]{2,1,0:T(8,128)(2,1)S(1)}, u32[]{:S(2)}, u32[]{:S(2)}) collective-permute-start(bf16[4,128,256]{2,1,0:T(8,128)(2,1)S(1)} %get-tuple-element.52), channel_id=1, source_target_pairs={{0,8},{8,16},{16,24},{24,0},{1,9},{9,17},{17,25},{25,1},{2,10},{10... | collective-permute-start | bytes 786440 | tf_op jit(solution)/shard_map/ppermute | solution.py:502
  90.5 15.8 %collective-permute-start.11 = (bf16[4,128,256]{2,1,0:T(8,128)(2,1)S(1)}, bf16[4,128,256]{2,1,0:T(8,128)(2,1)S(1)}, u32[]{:S(2)}, u32[]{:S(2)}) collective-permute-start(bf16[4,128,256]{2,1,0:T(8,128)(2,1)S(1)} %get-tuple-element.53), channel_id=1, source_target_pairs={{0,16},{8,24},{16,0},{24,8},{1,17},{9,25},{17,1},{25,9},{2,18},{10... | collective-permute-start | bytes 786440 | tf_op jit(solution)/shard_map/ppermute | solution.py:502
  102.2 6.9 %collective-permute-start.12 = (bf16[4,128,256]{2,1,0:T(8,128)(2,1)S(1)}, bf16[4,128,256]{2,1,0:T(8,128)(2,1)S(1)}, u32[]{:S(2)}, u32[]{:S(2)}) collective-permute-start(bf16[4,128,256]{2,1,0:T(8,128)(2,1)S(1)} %get-tuple-element.54), channel_id=1, source_target_pairs={{0,24},{8,0},{16,8},{24,16},{1,25},{9,1},{17,9},{25,17},{2,26},{10... | collective-permute-start | bytes 786440 | tf_op jit(solution)/shard_map/ppermute | solution.py:502
  102.6 7.2 %collective-permute-start.6 = (bf16[128,256]{1,0:T(8,128)(2,1)S(1)}, bf16[128,256]{1,0:T(8,128)(2,1)S(1)}, u32[]{:S(2)}, u32[]{:S(2)}) collective-permute-start(bf16[128,256]{1,0:T(8,128)(2,1)S(1)} %get-tuple-element.46), channel_id=1, source_target_pairs={{0,8},{8,16},{16,24},{24,0},{1,9},{9,17},{17,25},{25,1},{2,10},{10... | collective-permute-start | bytes 196616 | tf_op jit(solution)/shard_map/ppermute | solution.py:502
  103.9 8.2 %collective-permute-start.7 = (bf16[128,256]{1,0:T(8,128)(2,1)S(1)}, bf16[128,256]{1,0:T(8,128)(2,1)S(1)}, u32[]{:S(2)}, u32[]{:S(2)}) collective-permute-start(bf16[128,256]{1,0:T(8,128)(2,1)S(1)} %get-tuple-element.47), channel_id=1, source_target_pairs={{0,16},{8,24},{16,0},{24,8},{1,17},{9,25},{17,1},{25,9},{2,18},{10... | collective-permute-start | bytes 196616 | tf_op jit(solution)/shard_map/ppermute | solution.py:502
  104.5 7.6 %collective-permute-start.8 = (bf16[128,256]{1,0:T(8,128)(2,1)S(1)}, bf16[128,256]{1,0:T(8,128)(2,1)S(1)}, u32[]{:S(2)}, u32[]{:S(2)}) collective-permute-start(bf16[128,256]{1,0:T(8,128)(2,1)S(1)} %get-tuple-element.48), channel_id=1, source_target_pairs={{0,24},{8,0},{16,8},{24,16},{1,25},{9,1},{17,9},{25,17},{2,26},{10... | collective-permute-start | bytes 196616 | tf_op jit(solution)/shard_map/ppermute | solution.py:502
  109.3 4.7 %collective-permute-start.13 = (bf16[128,256]{1,0:T(8,128)(2,1)S(1)}, bf16[128,256]{1,0:T(8,128)(2,1)S(1)}, u32[]{:S(2)}, u32[]{:S(2)}) collective-permute-start(bf16[128,256]{1,0:T(8,128)(2,1)S(1)} %get-tuple-element.56), channel_id=1, source_target_pairs={{0,32},{32,64},{64,96},{96,0},{1,33},{33,65},{65,97},{97,1},{2,34}... | collective-permute-start | bytes 196616 | tf_op jit(solution)/shard_map/ppermute | solution.py:502
  109.4 5.1 %collective-permute-start.14 = (bf16[128,256]{1,0:T(8,128)(2,1)S(1)}, bf16[128,256]{1,0:T(8,128)(2,1)S(1)}, u32[]{:S(2)}, u32[]{:S(2)}) collective-permute-start(bf16[128,256]{1,0:T(8,128)(2,1)S(1)} %get-tuple-element.57), channel_id=1, source_target_pairs={{0,64},{32,96},{64,0},{96,32},{1,65},{33,97},{65,1},{97,33},{2,66}... | collective-permute-start | bytes 196616 | tf_op jit(solution)/shard_map/ppermute | solution.py:502
  109.8 5.2 %collective-permute-start.15 = (bf16[128,256]{1,0:T(8,128)(2,1)S(1)}, bf16[128,256]{1,0:T(8,128)(2,1)S(1)}, u32[]{:S(2)}, u32[]{:S(2)}) collective-permute-start(bf16[128,256]{1,0:T(8,128)(2,1)S(1)} %get-tuple-element.58), channel_id=1, source_target_pairs={{0,96},{32,0},{64,32},{96,64},{1,97},{33,1},{65,33},{97,65},{2,98}... | collective-permute-start | bytes 196616 | tf_op jit(solution)/shard_map/ppermute | solution.py:502
  115.0 14.3 %collective-permute-start.18 = (bf16[128,512]{1,0:T(8,128)(2,1)S(1)}, bf16[128,512]{1,0:T(8,128)(2,1)S(1)}, u32[]{:S(2)}, u32[]{:S(2)}) collective-permute-start(bf16[128,512]{1,0:T(8,128)(2,1)S(1)} %block.1.refs_0_), channel_id=1, source_target_pairs={{0,24},{8,0},{16,8},{24,16},{1,25},{9,1},{17,9},{25,17},{2,26},{10... | collective-permute-start | bytes 393224 | tf_op jit(solution)/shard_map/ppermute | solution.py:502
  116.6 12.7 %collective-permute-start.17 = (bf16[128,512]{1,0:T(8,128)(2,1)S(1)}, bf16[128,512]{1,0:T(8,128)(2,1)S(1)}, u32[]{:S(2)}, u32[]{:S(2)}) collective-permute-start(bf16[128,512]{1,0:T(8,128)(2,1)S(1)} %block.1.refs_0_), channel_id=1, source_target_pairs={{0,16},{8,24},{16,0},{24,8},{1,17},{9,25},{17,1},{25,9},{2,18},{10... | collective-permute-start | bytes 393224 | tf_op jit(solution)/shard_map/ppermute | solution.py:502
  116.6 13.2 %collective-permute-start.16 = (bf16[128,512]{1,0:T(8,128)(2,1)S(1)}, bf16[128,512]{1,0:T(8,128)(2,1)S(1)}, u32[]{:S(2)}, u32[]{:S(2)}) collective-permute-start(bf16[128,512]{1,0:T(8,128)(2,1)S(1)} %block.1.refs_0_), channel_id=1, source_target_pairs={{0,8},{8,16},{16,24},{24,0},{1,9},{9,17},{17,25},{25,1},{2,10},{10... | collective-permute-start | bytes 393224 | tf_op jit(solution)/shard_map/ppermute | solution.py:502
  121.4 16.1 %collective-permute-start.26 = (bf16[128,1280]{1,0:T(8,128)(2,1)S(1)}, bf16[128,1280]{1,0:T(8,128)(2,1)S(1)}, u32[]{:S(2)}, u32[]{:S(2)}) collective-permute-start(bf16[128,1280]{1,0:T(8,128)(2,1)S(1)} %get-tuple-element.64), channel_id=1, source_target_pairs={{0,2},{1,3},{2,0},{3,1},{4,6},{5,7},{6,4},{7,5},{8,10},{9,11},{10,... | collective-permute-start | bytes 983048 | tf_op jit(solution)/shard_map/ppermute | solution.py:502
  124.2 6.1 %collective-permute-start.19 = (bf16[128,512]{1,0:T(8,128)(2,1)S(1)}, bf16[128,512]{1,0:T(8,128)(2,1)S(1)}, u32[]{:S(2)}, u32[]{:S(2)}) collective-permute-start(bf16[128,512]{1,0:T(8,128)(2,1)S(1)} %block.1.refs_0_), channel_id=1, source_target_pairs={{0,4},{4,0},{1,5},{5,1},{2,6},{6,2},{3,7},{7,3},{8,12},{12,8},{9,1... | collective-permute-start | bytes 393224 | tf_op jit(solution)/shard_map/ppermute | solution.py:465
  129.3 1.3 collective-permute-start.22
  129.3 3.7 %collective-permute-start.21 = (bf16[128,512]{1,0:T(8,128)(2,1)S(1)}, bf16[128,512]{1,0:T(8,128)(2,1)S(1)}, u32[]{:S(2)}, u32[]{:S(2)}) collective-permute-start(bf16[128,512]{1,0:T(8,128)(2,1)S(1)} %collective-permute-done.17.refs_2_), channel_id=1, source_target_pairs={{0,4},{4,0},{1,5},{5,1},{2,6},{6,2},{3,7},{7,3},{8,12},{12,8},{9,1... | collective-permute-start | bytes 393224 | tf_op jit(solution)/shard_map/ppermute | solution.py:465
  129.8 3.2 %collective-permute-start.20 = (bf16[128,512]{1,0:T(8,128)(2,1)S(1)}, bf16[128,512]{1,0:T(8,128)(2,1)S(1)}, u32[]{:S(2)}, u32[]{:S(2)}) collective-permute-start(bf16[128,512]{1,0:T(8,128)(2,1)S(1)} %collective-permute-done.16.refs_1_), channel_id=1, source_target_pairs={{0,4},{4,0},{1,5},{5,1},{2,6},{6,2},{3,7},{7,3},{8,12},{12,8},{9,1... | collective-permute-start | bytes 393224 | tf_op jit(solution)/shard_map/ppermute | solution.py:465
  130.3 10.8 %collective-permute-start.27 = (bf16[128,1280]{1,0:T(8,128)(2,1)}, bf16[128,1280]{1,0:T(8,128)(2,1)S(1)}, u32[]{:S(2)}, u32[]{:S(2)}) collective-permute-start(bf16[128,1280]{1,0:T(8,128)(2,1)} %get-tuple-element.65), channel_id=1, source_target_pairs={{0,1},{1,2},{2,3},{3,0},{4,5},{5,6},{6,7},{7,4},{8,9},{9,10},{10,1... | collective-permute-start | bytes 983048 | tf_op jit(solution)/shard_map/ppermute | solution.py:502
  130.7 10.4 %collective-permute-start.28 = (bf16[128,1280]{1,0:T(8,128)(2,1)}, bf16[128,1280]{1,0:T(8,128)(2,1)S(1)}, u32[]{:S(2)}, u32[]{:S(2)}) collective-permute-start(bf16[128,1280]{1,0:T(8,128)(2,1)} %get-tuple-element.66), channel_id=1, source_target_pairs={{0,3},{1,0},{2,1},{3,2},{4,7},{5,4},{6,5},{7,6},{8,11},{9,8},{10,9... | collective-permute-start | bytes 983048 | tf_op jit(solution)/shard_map/ppermute | solution.py:502
  134.7 7.2 %collective-permute-start.23 = (bf16[160,512]{1,0:T(8,128)(2,1)}, bf16[160,512]{1,0:T(8,128)(2,1)S(1)}, u32[]{:S(2)}, u32[]{:S(2)}) collective-permute-start(bf16[160,512]{1,0:T(8,128)(2,1)} %get-tuple-element.60), channel_id=1, source_target_pairs={{0,64},{32,96},{64,0},{96,32},{1,65},{33,97},{65,1},{97,33},{2,66}... | collective-permute-start | bytes 491528 | tf_op jit(solution)/shard_map/ppermute | solution.py:502
  135.5 10.6 %collective-permute-start.24 = (bf16[160,512]{1,0:T(8,128)(2,1)}, bf16[160,512]{1,0:T(8,128)(2,1)S(1)}, u32[]{:S(2)}, u32[]{:S(2)}) collective-permute-start(bf16[160,512]{1,0:T(8,128)(2,1)} %get-tuple-element.61), channel_id=1, source_target_pairs={{0,32},{32,64},{64,96},{96,0},{1,33},{33,65},{65,97},{97,1},{2,34}... | collective-permute-start | bytes 491528 | tf_op jit(solution)/shard_map/ppermute | solution.py:502
  137.4 8.7 %collective-permute-start.25 = (bf16[160,512]{1,0:T(8,128)(2,1)}, bf16[160,512]{1,0:T(8,128)(2,1)S(1)}, u32[]{:S(2)}, u32[]{:S(2)}) collective-permute-start(bf16[160,512]{1,0:T(8,128)(2,1)} %get-tuple-element.62), channel_id=1, source_target_pairs={{0,96},{32,0},{64,32},{96,64},{1,97},{33,1},{65,33},{97,65},{2,98}... | collective-permute-start | bytes 491528 | tf_op jit(solution)/shard_map/ppermute | solution.py:502

commit v5 on v4

--- a/solution.py
+++ b/solution.py
@@ -353,25 +353,32 @@
     )(hidden, *lines, *others)
 
 
-def prompt_kernel(block, weight_hbm, *refs):
-    *terms, weight, sems = refs
+def hold_kernel(source, target, sem):
+    copy = pltpu.make_async_copy(source, target, sem)
+    copy.start()
+    copy.wait()
+
+
+def hold(array):
+    return pl.pallas_call(
+        hold_kernel,
+        in_specs=[pl.BlockSpec(memory_space=pl.ANY)],
+        out_specs=pl.BlockSpec(memory_space=pltpu.VMEM),
+        out_shape=pltpu.VMEM(array.shape, BF16),
+        scratch_shapes=[pltpu.SemaphoreType.DMA],
+        compiler_params=pltpu.CompilerParams(vmem_limit_bytes=2**20),
+        name="hold",
+    )(in_hbm(array))
+
+
+def prompt_kernel(block, weight, *terms):
     here = lax.axis_index("x")
     rows = terms[0].shape[1]
-    steps = (2, 1, 3, 0)
-    copies = []
-    for step in steps:
+    for step in (2, 1, 3, 0):
         start = pl.multiple_of(lax.rem(here + step, 4) * rows, rows)
-        copies.append(
-            pltpu.make_async_copy(
-                weight_hbm.at[:, pl.ds(start, rows)], weight.at[step], sems.at[step]
-            )
-        )
-        copies[-1].start()
-    for step, copy in zip(steps, copies):
-        copy.wait()
         terms[step][...] = (
-            dot(block[:, : 2 * HD], weight[step, 0], NT)
-            + dot(block[:, 2 * HD :], weight[step, 1], NT)
+            dot(block[:, : 2 * HD], weight[0, pl.ds(start, rows)], NT)
+            + dot(block[:, 2 * HD :], weight[1, pl.ds(start, rows)], NT)
         ).astype(BF16)
 
 
@@ -380,20 +387,13 @@
     return pl.pallas_call(
         prompt_kernel,
         out_shape=[jax.ShapeDtypeStruct(shape, BF16)] * 4,
-        in_specs=[
-            pl.BlockSpec(memory_space=pltpu.VMEM),
-            pl.BlockSpec(memory_space=pl.ANY),
-        ],
-        scratch_shapes=[
-            pltpu.VMEM((4, 2, shape[1], 2 * HD), BF16),
-            pltpu.SemaphoreType.DMA((4,)),
-        ],
+        in_specs=[pl.BlockSpec(memory_space=pltpu.VMEM)] * 2,
         cost_estimate=pl.CostEstimate(
             flops=8 * shape[0] * shape[1] * 4 * HD, bytes_accessed=2**22, transcendentals=0
         ),
         compiler_params=pltpu.CompilerParams(vmem_limit_bytes=16 * 2**20),
         name="prompt",
-    )(block, in_hbm(weight))
+    )(block, pltpu.with_memory_space_constraint(weight, pltpu.VMEM))
 
 
 def sum_kernel(*refs):
@@ -507,6 +507,8 @@
     send_k = after(send_k, (hidden_y,), pltpu.HBM)
     keys = deal(split_sum(keep_k, swap_cores(send_k), "y"), "y")
     values = deal(split_sum(keep_v, swap_cores(send_v), "z"), "z")
+    relaid = hold(after(relaid, (in_hbm(send_k),), pltpu.HBM))
+    values[2] = after_all([values[2]], [relaid])[0]
     keys = deal(reduce_of(keys, "z"), "z")
     values = deal(reduce_of(values, "y"), "y")
     block_b = block_of(keys, values)

time: 149 us -> 146 us (0.980)
  waiting for transfers between devices: 45.2 us -> 41.5 us
    ppermute x21, waiting for transfers between devices: 22.8 us -> 19.1 us  [ring(): return lax.ppermute(array, axis, [(i, (i + step) % 4) for i in range(4)])]
    pallas_call x0 -> x2, Pallas kernels: none -> 2.49 us  [the longest x1 2.49 us: hold(): pl.pallas_call(hold_kernel, in_specs=[pl.BlockSpec(memory_space=pl.ANY)],...]
    ppermute x21, starting transfers between devices: 20.2 us -> 22.5 us  [ring(): return lax.ppermute(array, axis, [(i, (i + step) % 4) for i in range(4)])]
    pallas_call x1, Pallas kernels: 4.05 us -> 2.24 us  [prompt_terms(): pl.pallas_call(prompt_kernel, out_shape=[jax.ShapeDtypeStruct(shape, BF16...]
  transfers between devices with their start and end apart: 31 -> 31, of which waited for: 14 -> 12; matrix products, arithmetic and copies ran while one was open for 6% -> 6% of each run, Pallas kernels for 29% -> 30%
where the time goes in v5:
time: 146 us; the launch traced here: 145 us
  Pallas kernels  43.6 us (30%)
  starting transfers between devices  42.9 us (29%)
  waiting for transfers between devices  41.5 us (28%)
  local copies, waits for them, and re-layouts  12.7 us (9%)
  matrix products  3.75 us (3%)
    pallas_call x1, Pallas kernels, attention(): pl.pallas_call(attention_kernel, in_specs=[smem] * 3 + [anywhere] * 3 + [...  32 us
    ppermute x21, starting transfers between devices, ring(): return lax.ppermute(array, axis, [(i, (i + step) % 4) for i in range(4)])  22.5 us
    ppermute x21, waiting for transfers between devices, ring(): return lax.ppermute(array, axis, [(i, (i + step) % 4) for i in range(4)])  19.1 us
    all_to_all x2, waiting for transfers between devices, exchange(): return lax.all_to_all(array, axes, 0, 0, tiled=True)  18.9 us
    all_to_all x2, starting transfers between devices, exchange(): return lax.all_to_all(array, axes, 0, 0, tiled=True)  11.5 us
    ppermute x8, starting transfers between devices, swap_cores(): return lax.ppermute(array, 'c', [(0, 1), (1, 0)])  8.95 us
    unnamed x17, local copies, waits for them, and re-layouts  6.69 us
    dot_general x1, matrix products, body(): jnp.einsum('pd,dkc->pkc', prompt_hidden, kv_weight, preferred_element_typ...  3.75 us
  transfers between devices with their start and end apart: 31, of which 12 were waited for; matrix products, arithmetic and copies ran while one was open for 6% of the time, Pallas kernels for 30%

profile of v5, /device:TPU:1, one launch (start us, length us, event | category | flops | bytes accessed | tf_op | source)
XLA Modules:
  0.0 145.4 jit_solution(171080506365833041)
XLA Ops:
  0.6 3.8 %fusion.3 = bf16[128,2,256]{2,0,1:T(8,128)(2,1)S(1)} fusion(bf16[5120,2,256]{2,1,0:T(2,128)(2,1)} %param.9, bf16[128,5120]{1,0:T(8,128)(2,1)} %hidden.1), kind=kOutput, calls=%fused_computation.4 | convolution fusion | flops 671154176 | bytes 6684672 | tf_op jit(solution)/shard_map/pd,dkc->pkc/dot_general | solution.py:479
  4.4 1.5 %collective-permute-start = (bf16[128,256]{1,0:T(8,128)(2,1)S(1)}, bf16[128,256]{1,0:T(8,128)(2,1)S(1)}, u32[]{:S(2)}, u32[]{:S(2)}) collective-permute-start(bf16[128,256]{1,0:T(8,128)(2,1)S(1)} %select_bitcast_fusion), channel_id=1, source_target_pairs={{0,4},{4,0},{1,5},{5,1},{2,6},{6,2},{3,7},{7,3},{8,12},{12,8},{9,1... | collective-permute-start | bytes 196616 | tf_op jit(solution)/shard_map/ppermute | solution.py:465
  5.9 0.9 collective-permute-done
  6.9 1.5 %broadcast_in_dim.2 = bf16[16,256,256]{2,1,0:T(8,128)(2,1)} broadcast(bf16[256,256]{1,0:T(8,128)(2,1)S(1)} %pad_maximum_fusion), dimensions={1,2} | broadcast | bytes 2228224 | tf_op jit(solution)/shard_map/broadcast_in_dim | solution.py:487
  8.4 8.0 %all-to-all-start = ((bf16[16,256,256]{2,1,0:T(8,128)(2,1)}), bf16[16,256,256]{2,1,0:T(8,128)(2,1)S(1)}, u32[]{:S(2)}, u32[]{:S(2)}) async-start(bf16[16,256,256]{2,1,0:T(8,128)(2,1)} %broadcast_in_dim.2), calls=%async_computation | async-start | bytes 4194304 | tf_op jit(solution)/shard_map/all_to_all | solution.py:469
  16.4 3.3 %columns.1.refs_2_ = bf16[8,640,128]{2,1,0:T(8,128)(2,1)} custom-call(bf16[128,5120]{1,0:T(8,128)(2,1)S(1)} %copy-done), custom_call_target="tpu_custom_call" | custom-call | tf_op jit(solution)/shard_map/columns/pallas_call | solution.py:257
  19.7 5.6 %copy.24 = bf16[5120,2,256]{2,0,1:T(8,128)(2,1)} copy(bf16[5120,2,256]{2,1,0:T(2,128)(2,1)} %param.9) | data formatting | bytes 10485760 | tf_op args[1]
  25.3 1.5 %reshape.27.refs_1_.own_hbm = bf16[8,128,512]{2,1,0:T(8,128)(2,1)} reshape(bf16[8,128,2,256]{3,2,1,0:T(2,128)(2,1)S(1)} %copy-done.6) | data formatting | bytes 2097152 | tf_op jit(solution)/shard_map/reshape | solution.py:490
  26.7 18.9 %all-to-all-done = bf16[16,256,256]{2,1,0:T(8,128)(2,1)S(1)} async-done(((bf16[16,256,256]{2,1,0:T(8,128)(2,1)}), bf16[16,256,256]{2,1,0:T(8,128)(2,1)S(1)}, u32[]{:S(2)}, u32[]{:S(2)}) %all-to-all-start) | async-done | bytes 2097184 | tf_op jit(solution)/shard_map/all_to_all | solution.py:469
  45.6 2.6 %collective-permute-start.1 = (bf16[32,128,256]{2,1,0:T(8,128)(2,1)S(1)}, bf16[32,128,256]{2,1,0:T(8,128)(2,1)}, u32[]{:S(2)}, u32[]{:S(2)}) collective-permute-start(bf16[32,128,256]{2,1,0:T(8,128)(2,1)S(1)} %after.4.near), channel_id=1, source_target_pairs={{0,4},{4,0},{1,5},{5,1},{2,6},{6,2},{3,7},{7,3},{8,12},{12,8},{9,1... | collective-permute-start | bytes 6291464 | tf_op jit(solution)/shard_map/ppermute | solution.py:465
  48.3 3.5 %all-to-all-start.1 = ((bf16[8,640,128]{2,1,0:T(8,128)(2,1)}), bf16[8,640,128]{2,1,0:T(8,128)(2,1)S(1)}, u32[]{:S(2)}, u32[]{:S(2)}) async-start(bf16[8,640,128]{2,1,0:T(8,128)(2,1)} %columns.1.refs_2_), calls=%async_computation.1 | async-start | bytes 2621440 | tf_op jit(solution)/shard_map/all_to_all | solution.py:469
  51.8 0.4 collective-permute-done.1.far
  52.2 32.0 %attention.1 = (bf16[8,128,1280]{2,1,0:T(8,128)(2,1)}, bf16[8,128,1280]{2,1,0:T(8,128)(2,1)}, bf16[8,128,512]{2,1,0:T(8,128)(2,1)}, bf16[16,128,256]{2,1,0:T(8,1...) custom-call(s32[32]{0:T(128)S(1)} %copy-done.4, ...), custom_call_target="tpu_custom_call" | custom-call | flops 10066329600 | bytes 16777216 | tf_op jit(solution)/shard_map/attention/pallas_call | solution.py:427
  84.4 1.1 copy-done.7
  85.4 1.8 %collective-permute-done.2.got = bf16[16,128,256]{2,1,0:T(8,128)(2,1)S(1)} collective-permute-done((bf16[16,128,256]{2,1,0:T(8,128)(2,1)}, bf16[16,128,256]{2,1,0:T(8,128)(2,1)S(1)}, u32[]{:S(2)}, u32[]{:S(2)}) %collective-permute-start.2) | collective-permute-done | bytes 1048608 | tf_op jit(solution)/shard_map/ppermute | solution.py:465
  87.2 0.2 split.2
  87.6 2.6 %collective-permute-start.5 = (bf16[4,128,256]{2,1,0:T(8,128)(2,1)S(1)}, bf16[4,128,256]{2,1,0:T(8,128)(2,1)S(1)}, u32[]{:S(2)}, u32[]{:S(2)}) collective-permute-start(bf16[4,128,256]{2,1,0:T(8,128)(2,1)S(1)} %get-tuple-element.44), channel_id=1, source_target_pairs={{0,96},{32,0},{64,32},{96,64},{1,97},{33,1},{65,33},{97,65},{2,98}... | collective-permute-start | bytes 786440 | tf_op jit(solution)/shard_map/ppermute | solution.py:502
  90.2 0.2 split.3
  90.5 0.3 collective-permute-start.10
  90.8 11.4 %collective-permute-done.3.refs_1_ = bf16[4,128,256]{2,1,0:T(8,128)(2,1)S(1)} collective-permute-done((bf16[4,128,256]{2,1,0:T(8,128)(2,1)S(1)}, bf16[4,128,256]{2,1,0:T(8,128)(2,1)S(1)}, u32[]{:S(2)}, u32[]{:S(2)}) %collective-permute-start.3) | collective-permute-done | bytes 262176 | tf_op jit(solution)/shard_map/ppermute | solution.py:502
  102.3 0.2 collective-permute-done.5.refs_3_
  102.4 0.1 reduce.2
  102.6 1.4 collective-permute-start.6
  103.9 2.5 %hold.1.refs_1_.weight = bf16[2,5120,256]{2,1,0:T(8,128)(2,1)S(1)} custom-call(bf16[2,5120,256]{2,1,0:T(8,128)(2,1)} %after.6.source), custom_call_target="tpu_custom_call" | custom-call | tf_op jit(solution)/shard_map/hold/pallas_call | solution.py:363
  106.5 2.4 %collective-permute-start.8 = (bf16[128,256]{1,0:T(8,128)(2,1)S(1)}, bf16[128,256]{1,0:T(8,128)(2,1)S(1)}, u32[]{:S(2)}, u32[]{:S(2)}) collective-permute-start(bf16[128,256]{1,0:T(8,128)(2,1)S(1)} %get-tuple-element.48), channel_id=1, source_target_pairs={{0,24},{8,0},{16,8},{24,16},{1,25},{9,1},{17,9},{25,17},{2,26},{10... | collective-permute-start | bytes 196616 | tf_op jit(solution)/shard_map/ppermute | solution.py:502
  108.9 0.3 collective-permute-done.12.refs_3_
  109.5 2.5 %collective-permute-start.14 = (bf16[128,256]{1,0:T(8,128)(2,1)S(1)}, bf16[128,256]{1,0:T(8,128)(2,1)S(1)}, u32[]{:S(2)}, u32[]{:S(2)}) collective-permute-start(bf16[128,256]{1,0:T(8,128)(2,1)S(1)} %get-tuple-element.57), channel_id=1, source_target_pairs={{0,64},{32,96},{64,0},{96,32},{1,65},{33,97},{65,1},{97,33},{2,66}... | collective-permute-start | bytes 196616 | tf_op jit(solution)/shard_map/ppermute | solution.py:502
  111.9 0.2 collective-permute-start.15
  112.1 2.3 %collective-permute-done.13.refs_5_ = bf16[128,256]{1,0:T(8,128)(2,1)S(1)} collective-permute-done((bf16[128,256]{1,0:T(8,128)(2,1)S(1)}, bf16[128,256]{1,0:T(8,128)(2,1)S(1)}, u32[]{:S(2)}, u32[]{:S(2)}) %collective-permute-start.13) | collective-permute-done | bytes 65568 | tf_op jit(solution)/shard_map/ppermute | solution.py:502
  114.5 0.6 collective-permute-done.15.refs_7_
  115.1 1.9 %collective-permute-start.18 = (bf16[128,512]{1,0:T(8,128)(2,1)S(1)}, bf16[128,512]{1,0:T(8,128)(2,1)S(1)}, u32[]{:S(2)}, u32[]{:S(2)}) collective-permute-start(bf16[128,512]{1,0:T(8,128)(2,1)S(1)} %block.1.refs_0_), channel_id=1, source_target_pairs={{0,24},{8,0},{16,8},{24,16},{1,25},{9,1},{17,9},{25,17},{2,26},{10... | collective-permute-start | bytes 393224 | tf_op jit(solution)/shard_map/ppermute | solution.py:502
  117.0 0.8 collective-permute-start.17
  117.9 0.8 collective-permute-start.16
  118.6 2.2 %prompt.1 = (bf16[128,1280]{1,0:T(8,128)(2,1)S(1)}, bf16[128,1280]{1,0:T(8,128)(2,1)}, bf16[128,1280]{1,0:T(8,128)(2,1)S(1)}, bf16[128,1280]{1,0:T(8,128)(2,1)}) custom-call(bf16[128,512]{1,0:T(8,128)(2,1)S(1)} %block.1.refs_0_, bf16[2,5120,256]{2,1,0:T(8,128)(2,1)S(1)} %hold.1.refs_1_.weight), custom_call_target="tpu_custom_call" | custom-call | flops 671088640 | bytes 4194304 | tf_op jit(solution)/shard_map/prompt/pallas_call | solution.py:387
  120.9 2.8 %collective-permute-start.26 = (bf16[128,1280]{1,0:T(8,128)(2,1)S(1)}, bf16[128,1280]{1,0:T(8,128)(2,1)S(1)}, u32[]{:S(2)}, u32[]{:S(2)}) collective-permute-start(bf16[128,1280]{1,0:T(8,128)(2,1)S(1)} %get-tuple-element.64), channel_id=1, source_target_pairs={{0,2},{1,3},{2,0},{3,1},{4,6},{5,7},{6,4},{7,5},{8,10},{9,11},{10,... | collective-permute-start | bytes 983048 | tf_op jit(solution)/shard_map/ppermute | solution.py:502
  123.6 4.1 %collective-permute-start.19 = (bf16[128,512]{1,0:T(8,128)(2,1)S(1)}, bf16[128,512]{1,0:T(8,128)(2,1)S(1)}, u32[]{:S(2)}, u32[]{:S(2)}) collective-permute-start(bf16[128,512]{1,0:T(8,128)(2,1)S(1)} %block.1.refs_0_), channel_id=1, source_target_pairs={{0,4},{4,0},{1,5},{5,1},{2,6},{6,2},{3,7},{7,3},{8,12},{12,8},{9,1... | collective-permute-start | bytes 393224 | tf_op jit(solution)/shard_map/ppermute | solution.py:465
  127.8 0.5 collective-permute-start.21
  128.4 0.4 collective-permute-done.19.refs_4_
  128.8 0.3 collective-permute-start.27
  129.1 2.3 %collective-permute-start.28 = (bf16[128,1280]{1,0:T(8,128)(2,1)}, bf16[128,1280]{1,0:T(8,128)(2,1)S(1)}, u32[]{:S(2)}, u32[]{:S(2)}) collective-permute-start(bf16[128,1280]{1,0:T(8,128)(2,1)} %get-tuple-element.66), channel_id=1, source_target_pairs={{0,3},{1,0},{2,1},{3,2},{4,7},{5,4},{6,5},{7,6},{8,11},{9,8},{10,9... | collective-permute-start | bytes 983048 | tf_op jit(solution)/shard_map/ppermute | solution.py:502
  131.4 1.7 %term.1 = (bf16[160,512]{1,0:T(8,128)(2,1)S(1)}, bf16[160,512]{1,0:T(8,128)(2,1)}, bf16[160,512]{1,0:T(8,128)(2,1)}, bf16[160,512]{1,0:T(8,128)(2,1)}) custom-call(bf16[8,640,128]{2,1,0:T(8,128)(2,1)S(1)} %all-to-all-done.1.refs_1_.hidden, bf16[128,512]{1,0:T(8,128)(2,1)S(1)} %block.1.refs_0_, bf16[128,512]{1,0:T(8,128)(2,1)S(1)} %collective-permute-done.16.refs_1_, ...), custom_call_target="tpu_custom_call" | custom-call | flops 2000000000 | bytes 10000000 | tf_op jit(solution)/shard_map/term/pallas_call | solution.py:344
  133.2 1.2 collective-permute-start.23
  134.4 0.7 collective-permute-start.24
  135.1 2.0 %collective-permute-start.25 = (bf16[160,512]{1,0:T(8,128)(2,1)}, bf16[160,512]{1,0:T(8,128)(2,1)S(1)}, u32[]{:S(2)}, u32[]{:S(2)}) collective-permute-start(bf16[160,512]{1,0:T(8,128)(2,1)} %get-tuple-element.62), channel_id=1, source_target_pairs={{0,96},{32,0},{64,32},{96,64},{1,97},{33,1},{65,33},{97,65},{2,98}... | collective-permute-start | bytes 491528 | tf_op jit(solution)/shard_map/ppermute | solution.py:502
  137.1 2.1 %reshape.29 = bf16[8,128,2,256]{3,2,1,0:T(2,128)(2,1)} reshape(bf16[8,128,512]{2,1,0:T(8,128)(2,1)} %get-tuple-element.38) | data formatting | bytes 2097152 | tf_op jit(solution)/shard_map/reshape | solution.py:499
  139.2 0.9 sum.3
  140.1 4.3 %collective-permute-done.24.refs_2_ = bf16[160,512]{1,0:T(8,128)(2,1)S(1)} collective-permute-done((bf16[160,512]{1,0:T(8,128)(2,1)}, bf16[160,512]{1,0:T(8,128)(2,1)S(1)}, u32[]{:S(2)}, u32[]{:S(2)}) %collective-permute-start.24) | collective-permute-done | bytes 163872 | tf_op jit(solution)/shard_map/ppermute | solution.py:502
  144.5 0.9 reshape.30
  (55 shorter events, 1.0 us)
Async XLA Ops:
  4.4 2.4 %collective-permute-start = (bf16[128,256]{1,0:T(8,128)(2,1)S(1)}, bf16[128,256]{1,0:T(8,128)(2,1)S(1)}, u32[]{:S(2)}, u32[]{:S(2)}) collective-permute-start(bf16[128,256]{1,0:T(8,128)(2,1)S(1)} %select_bitcast_fusion), channel_id=1, source_target_pairs={{0,4},{4,0},{1,5},{5,1},{2,6},{6,2},{3,7},{7,3},{8,12},{12,8},{9,1... | collective-permute-start | bytes 196616 | tf_op jit(solution)/shard_map/ppermute | solution.py:465
  8.4 8.0 %copy-start = (bf16[128,5120]{1,0:T(8,128)(2,1)S(1)}, bf16[128,5120]{1,0:T(8,128)(2,1)}, u32[]{:S(2)}) copy-start(bf16[128,5120]{1,0:T(8,128)(2,1)} %hidden.1) | copy-start | bytes 3932164
  8.4 37.2 %all-to-all-start = ((bf16[16,256,256]{2,1,0:T(8,128)(2,1)}), bf16[16,256,256]{2,1,0:T(8,128)(2,1)S(1)}, u32[]{:S(2)}, u32[]{:S(2)}) async-start(bf16[16,256,256]{2,1,0:T(8,128)(2,1)} %broadcast_in_dim.2), calls=%async_computation | async-start | bytes 4194304 | tf_op jit(solution)/shard_map/all_to_all | solution.py:469
  19.7 5.6 %copy-start.6 = (bf16[8,128,2,256]{3,2,1,0:T(2,128)(2,1)S(1)}, bf16[8,128,2,256]{3,2,1,0:T(2,128)(2,1)}, u32[]{:S(2)}) copy-start(bf16[8,128,2,256]{3,2,1,0:T(2,128)(2,1)} %param.12) | copy-start | bytes 3145732
  45.6 6.6 %copy-start.3 = (s32[32,8]{0,1:T(8,128)S(1)}, s32[32,8]{0,1:T(8,128)}, u32[]{:S(2)}) copy-start(s32[32,8]{0,1:T(8,128)} %param.14) | copy-start | bytes 3076
  45.6 6.6 %copy-start.4 = (s32[32]{0:T(128)S(1)}, s32[32]{0:T(128)}, u32[]{:S(2)}) copy-start(s32[32]{0:T(128)} %pack_counts.1) | copy-start | bytes 388
  45.6 6.6 %copy-start.5 = (s32[32]{0:T(128)S(1)}, s32[32]{0:T(128)}, u32[]{:S(2)}) copy-start(s32[32]{0:T(128)} %block_group.1) | copy-start | bytes 388
  45.6 6.5 %collective-permute-start.1 = (bf16[32,128,256]{2,1,0:T(8,128)(2,1)S(1)}, bf16[32,128,256]{2,1,0:T(8,128)(2,1)}, u32[]{:S(2)}, u32[]{:S(2)}) collective-permute-start(bf16[32,128,256]{2,1,0:T(8,128)(2,1)S(1)} %after.4.near), channel_id=1, source_target_pairs={{0,4},{4,0},{1,5},{5,1},{2,6},{6,2},{3,7},{7,3},{8,12},{12,8},{9,1... | collective-permute-start | bytes 6291464 | tf_op jit(solution)/shard_map/ppermute | solution.py:465
  48.3 36.0 %all-to-all-start.1 = ((bf16[8,640,128]{2,1,0:T(8,128)(2,1)}), bf16[8,640,128]{2,1,0:T(8,128)(2,1)S(1)}, u32[]{:S(2)}, u32[]{:S(2)}) async-start(bf16[8,640,128]{2,1,0:T(8,128)(2,1)} %columns.1.refs_2_), calls=%async_computation.1 | async-start | bytes 2621440 | tf_op jit(solution)/shard_map/all_to_all | solution.py:469
  84.2 1.2 copy-start.7
  84.2 3.0 %copy-start.2 = (bf16[16,128,256]{2,1,0:T(8,128)(2,1)S(1)}, bf16[16,128,256]{2,1,0:T(8,128)(2,1)}, u32[]{:S(2)}) copy-start(bf16[16,128,256]{2,1,0:T(8,128)(2,1)} %get-tuple-element.39.keep) | copy-start | bytes 3145732
  84.2 6.0 %copy-start.1 = (bf16[16,128,256]{2,1,0:T(8,128)(2,1)S(1)}, bf16[16,128,256]{2,1,0:T(8,128)(2,1)}, u32[]{:S(2)}) copy-start(bf16[16,128,256]{2,1,0:T(8,128)(2,1)} %get-tuple-element.49.keep) | copy-start | bytes 3145732
  84.3 3.0 %collective-permute-start.2 = (bf16[16,128,256]{2,1,0:T(8,128)(2,1)}, bf16[16,128,256]{2,1,0:T(8,128)(2,1)S(1)}, u32[]{:S(2)}, u32[]{:S(2)}) collective-permute-start(bf16[16,128,256]{2,1,0:T(8,128)(2,1)} %after.5.refs_1_), channel_id=1, source_target_pairs={{0,4},{4,0},{1,5},{5,1},{2,6},{6,2},{3,7},{7,3},{8,12},{12,8},{9,1... | collective-permute-start | bytes 3145736 | tf_op jit(solution)/shard_map/ppermute | solution.py:465
  85.4 4.8 %collective-permute-start.9 = (bf16[16,128,256]{2,1,0:T(8,128)(2,1)S(1)}, bf16[16,128,256]{2,1,0:T(8,128)(2,1)S(1)}, u32[]{:S(2)}, u32[]{:S(2)}) collective-permute-start(bf16[16,128,256]{2,1,0:T(8,128)(2,1)S(1)} %copy-done.7), channel_id=1, source_target_pairs={{0,4},{4,0},{1,5},{5,1},{2,6},{6,2},{3,7},{7,3},{8,12},{12,8},{9,1... | collective-permute-start | bytes 3145736 | tf_op jit(solution)/shard_map/ppermute | solution.py:465
  87.5 14.8 %collective-permute-start.3 = (bf16[4,128,256]{2,1,0:T(8,128)(2,1)S(1)}, bf16[4,128,256]{2,1,0:T(8,128)(2,1)S(1)}, u32[]{:S(2)}, u32[]{:S(2)}) collective-permute-start(bf16[4,128,256]{2,1,0:T(8,128)(2,1)S(1)} %get-tuple-element.42), channel_id=1, source_target_pairs={{0,32},{32,64},{64,96},{96,0},{1,33},{33,65},{65,97},{97,1},{2,34}... | collective-permute-start | bytes 786440 | tf_op jit(solution)/shard_map/ppermute | solution.py:502
  87.5 14.7 %collective-permute-start.4 = (bf16[4,128,256]{2,1,0:T(8,128)(2,1)S(1)}, bf16[4,128,256]{2,1,0:T(8,128)(2,1)S(1)}, u32[]{:S(2)}, u32[]{:S(2)}) collective-permute-start(bf16[4,128,256]{2,1,0:T(8,128)(2,1)S(1)} %get-tuple-element.43), channel_id=1, source_target_pairs={{0,64},{32,96},{64,0},{96,32},{1,65},{33,97},{65,1},{97,33},{2,66}... | collective-permute-start | bytes 786440 | tf_op jit(solution)/shard_map/ppermute | solution.py:502
  87.6 14.8 %collective-permute-start.5 = (bf16[4,128,256]{2,1,0:T(8,128)(2,1)S(1)}, bf16[4,128,256]{2,1,0:T(8,128)(2,1)S(1)}, u32[]{:S(2)}, u32[]{:S(2)}) collective-permute-start(bf16[4,128,256]{2,1,0:T(8,128)(2,1)S(1)} %get-tuple-element.44), channel_id=1, source_target_pairs={{0,96},{32,0},{64,32},{96,64},{1,97},{33,1},{65,33},{97,65},{2,98}... | collective-permute-start | bytes 786440 | tf_op jit(solution)/shard_map/ppermute | solution.py:502
  90.5 16.1 %collective-permute-start.11 = (bf16[4,128,256]{2,1,0:T(8,128)(2,1)S(1)}, bf16[4,128,256]{2,1,0:T(8,128)(2,1)S(1)}, u32[]{:S(2)}, u32[]{:S(2)}) collective-permute-start(bf16[4,128,256]{2,1,0:T(8,128)(2,1)S(1)} %get-tuple-element.53), channel_id=1, source_target_pairs={{0,16},{8,24},{16,0},{24,8},{1,17},{9,25},{17,1},{25,9},{2,18},{10... | collective-permute-start | bytes 786440 | tf_op jit(solution)/shard_map/ppermute | solution.py:502
  90.5 18.4 %collective-permute-start.10 = (bf16[4,128,256]{2,1,0:T(8,128)(2,1)S(1)}, bf16[4,128,256]{2,1,0:T(8,128)(2,1)S(1)}, u32[]{:S(2)}, u32[]{:S(2)}) collective-permute-start(bf16[4,128,256]{2,1,0:T(8,128)(2,1)S(1)} %get-tuple-element.52), channel_id=1, source_target_pairs={{0,8},{8,16},{16,24},{24,0},{1,9},{9,17},{17,25},{25,1},{2,10},{10... | collective-permute-start | bytes 786440 | tf_op jit(solution)/shard_map/ppermute | solution.py:502
  102.2 7.0 %collective-permute-start.12 = (bf16[4,128,256]{2,1,0:T(8,128)(2,1)S(1)}, bf16[4,128,256]{2,1,0:T(8,128)(2,1)S(1)}, u32[]{:S(2)}, u32[]{:S(2)}) collective-permute-start(bf16[4,128,256]{2,1,0:T(8,128)(2,1)S(1)} %get-tuple-element.54), channel_id=1, source_target_pairs={{0,24},{8,0},{16,8},{24,16},{1,25},{9,1},{17,9},{25,17},{2,26},{10... | collective-permute-start | bytes 786440 | tf_op jit(solution)/shard_map/ppermute | solution.py:502
  102.6 9.4 %collective-permute-start.6 = (bf16[128,256]{1,0:T(8,128)(2,1)S(1)}, bf16[128,256]{1,0:T(8,128)(2,1)S(1)}, u32[]{:S(2)}, u32[]{:S(2)}) collective-permute-start(bf16[128,256]{1,0:T(8,128)(2,1)S(1)} %get-tuple-element.46), channel_id=1, source_target_pairs={{0,8},{8,16},{16,24},{24,0},{1,9},{9,17},{17,25},{25,1},{2,10},{10... | collective-permute-start | bytes 196616 | tf_op jit(solution)/shard_map/ppermute | solution.py:502
  106.4 5.7 %collective-permute-start.7 = (bf16[128,256]{1,0:T(8,128)(2,1)S(1)}, bf16[128,256]{1,0:T(8,128)(2,1)S(1)}, u32[]{:S(2)}, u32[]{:S(2)}) collective-permute-start(bf16[128,256]{1,0:T(8,128)(2,1)S(1)} %get-tuple-element.47), channel_id=1, source_target_pairs={{0,16},{8,24},{16,0},{24,8},{1,17},{9,25},{17,1},{25,9},{2,18},{10... | collective-permute-start | bytes 196616 | tf_op jit(solution)/shard_map/ppermute | solution.py:502
  106.5 5.6 %collective-permute-start.8 = (bf16[128,256]{1,0:T(8,128)(2,1)S(1)}, bf16[128,256]{1,0:T(8,128)(2,1)S(1)}, u32[]{:S(2)}, u32[]{:S(2)}) collective-permute-start(bf16[128,256]{1,0:T(8,128)(2,1)S(1)} %get-tuple-element.48), channel_id=1, source_target_pairs={{0,24},{8,0},{16,8},{24,16},{1,25},{9,1},{17,9},{25,17},{2,26},{10... | collective-permute-start | bytes 196616 | tf_op jit(solution)/shard_map/ppermute | solution.py:502
  109.4 5.1 %collective-permute-start.13 = (bf16[128,256]{1,0:T(8,128)(2,1)S(1)}, bf16[128,256]{1,0:T(8,128)(2,1)S(1)}, u32[]{:S(2)}, u32[]{:S(2)}) collective-permute-start(bf16[128,256]{1,0:T(8,128)(2,1)S(1)} %get-tuple-element.56), channel_id=1, source_target_pairs={{0,32},{32,64},{64,96},{96,0},{1,33},{33,65},{65,97},{97,1},{2,34}... | collective-permute-start | bytes 196616 | tf_op jit(solution)/shard_map/ppermute | solution.py:502
  109.5 5.0 %collective-permute-start.14 = (bf16[128,256]{1,0:T(8,128)(2,1)S(1)}, bf16[128,256]{1,0:T(8,128)(2,1)S(1)}, u32[]{:S(2)}, u32[]{:S(2)}) collective-permute-start(bf16[128,256]{1,0:T(8,128)(2,1)S(1)} %get-tuple-element.57), channel_id=1, source_target_pairs={{0,64},{32,96},{64,0},{96,32},{1,65},{33,97},{65,1},{97,33},{2,66}... | collective-permute-start | bytes 196616 | tf_op jit(solution)/shard_map/ppermute | solution.py:502
  111.9 3.1 %collective-permute-start.15 = (bf16[128,256]{1,0:T(8,128)(2,1)S(1)}, bf16[128,256]{1,0:T(8,128)(2,1)S(1)}, u32[]{:S(2)}, u32[]{:S(2)}) collective-permute-start(bf16[128,256]{1,0:T(8,128)(2,1)S(1)} %get-tuple-element.58), channel_id=1, source_target_pairs={{0,96},{32,0},{64,32},{96,64},{1,97},{33,1},{65,33},{97,65},{2,98}... | collective-permute-start | bytes 196616 | tf_op jit(solution)/shard_map/ppermute | solution.py:502
  115.1 12.6 %collective-permute-start.18 = (bf16[128,512]{1,0:T(8,128)(2,1)S(1)}, bf16[128,512]{1,0:T(8,128)(2,1)S(1)}, u32[]{:S(2)}, u32[]{:S(2)}) collective-permute-start(bf16[128,512]{1,0:T(8,128)(2,1)S(1)} %block.1.refs_0_), channel_id=1, source_target_pairs={{0,24},{8,0},{16,8},{24,16},{1,25},{9,1},{17,9},{25,17},{2,26},{10... | collective-permute-start | bytes 393224 | tf_op jit(solution)/shard_map/ppermute | solution.py:502
  117.0 10.8 %collective-permute-start.17 = (bf16[128,512]{1,0:T(8,128)(2,1)S(1)}, bf16[128,512]{1,0:T(8,128)(2,1)S(1)}, u32[]{:S(2)}, u32[]{:S(2)}) collective-permute-start(bf16[128,512]{1,0:T(8,128)(2,1)S(1)} %block.1.refs_0_), channel_id=1, source_target_pairs={{0,16},{8,24},{16,0},{24,8},{1,17},{9,25},{17,1},{25,9},{2,18},{10... | collective-permute-start | bytes 393224 | tf_op jit(solution)/shard_map/ppermute | solution.py:502
  117.9 10.4 %collective-permute-start.16 = (bf16[128,512]{1,0:T(8,128)(2,1)S(1)}, bf16[128,512]{1,0:T(8,128)(2,1)S(1)}, u32[]{:S(2)}, u32[]{:S(2)}) collective-permute-start(bf16[128,512]{1,0:T(8,128)(2,1)S(1)} %block.1.refs_0_), channel_id=1, source_target_pairs={{0,8},{8,16},{16,24},{24,0},{1,9},{9,17},{17,25},{25,1},{2,10},{10... | collective-permute-start | bytes 393224 | tf_op jit(solution)/shard_map/ppermute | solution.py:502
  120.9 14.3 %collective-permute-start.26 = (bf16[128,1280]{1,0:T(8,128)(2,1)S(1)}, bf16[128,1280]{1,0:T(8,128)(2,1)S(1)}, u32[]{:S(2)}, u32[]{:S(2)}) collective-permute-start(bf16[128,1280]{1,0:T(8,128)(2,1)S(1)} %get-tuple-element.64), channel_id=1, source_target_pairs={{0,2},{1,3},{2,0},{3,1},{4,6},{5,7},{6,4},{7,5},{8,10},{9,11},{10,... | collective-permute-start | bytes 983048 | tf_op jit(solution)/shard_map/ppermute | solution.py:502
  123.6 5.1 %collective-permute-start.19 = (bf16[128,512]{1,0:T(8,128)(2,1)S(1)}, bf16[128,512]{1,0:T(8,128)(2,1)S(1)}, u32[]{:S(2)}, u32[]{:S(2)}) collective-permute-start(bf16[128,512]{1,0:T(8,128)(2,1)S(1)} %block.1.refs_0_), channel_id=1, source_target_pairs={{0,4},{4,0},{1,5},{5,1},{2,6},{6,2},{3,7},{7,3},{8,12},{12,8},{9,1... | collective-permute-start | bytes 393224 | tf_op jit(solution)/shard_map/ppermute | solution.py:465
  127.8 1.3 collective-permute-start.22
  127.8 3.7 %collective-permute-start.21 = (bf16[128,512]{1,0:T(8,128)(2,1)S(1)}, bf16[128,512]{1,0:T(8,128)(2,1)S(1)}, u32[]{:S(2)}, u32[]{:S(2)}) collective-permute-start(bf16[128,512]{1,0:T(8,128)(2,1)S(1)} %collective-permute-done.17.refs_2_), channel_id=1, source_target_pairs={{0,4},{4,0},{1,5},{5,1},{2,6},{6,2},{3,7},{7,3},{8,12},{12,8},{9,1... | collective-permute-start | bytes 393224 | tf_op jit(solution)/shard_map/ppermute | solution.py:465
  128.3 3.2 %collective-permute-start.20 = (bf16[128,512]{1,0:T(8,128)(2,1)S(1)}, bf16[128,512]{1,0:T(8,128)(2,1)S(1)}, u32[]{:S(2)}, u32[]{:S(2)}) collective-permute-start(bf16[128,512]{1,0:T(8,128)(2,1)S(1)} %collective-permute-done.16.refs_1_), channel_id=1, source_target_pairs={{0,4},{4,0},{1,5},{5,1},{2,6},{6,2},{3,7},{7,3},{8,12},{12,8},{9,1... | collective-permute-start | bytes 393224 | tf_op jit(solution)/shard_map/ppermute | solution.py:465
  128.8 10.5 %collective-permute-start.27 = (bf16[128,1280]{1,0:T(8,128)(2,1)}, bf16[128,1280]{1,0:T(8,128)(2,1)S(1)}, u32[]{:S(2)}, u32[]{:S(2)}) collective-permute-start(bf16[128,1280]{1,0:T(8,128)(2,1)} %get-tuple-element.65), channel_id=1, source_target_pairs={{0,1},{1,2},{2,3},{3,0},{4,5},{5,6},{6,7},{7,4},{8,9},{9,10},{10,1... | collective-permute-start | bytes 983048 | tf_op jit(solution)/shard_map/ppermute | solution.py:502
  129.1 10.1 %collective-permute-start.28 = (bf16[128,1280]{1,0:T(8,128)(2,1)}, bf16[128,1280]{1,0:T(8,128)(2,1)S(1)}, u32[]{:S(2)}, u32[]{:S(2)}) collective-permute-start(bf16[128,1280]{1,0:T(8,128)(2,1)} %get-tuple-element.66), channel_id=1, source_target_pairs={{0,3},{1,0},{2,1},{3,2},{4,7},{5,4},{6,5},{7,6},{8,11},{9,8},{10,9... | collective-permute-start | bytes 983048 | tf_op jit(solution)/shard_map/ppermute | solution.py:502
  133.2 6.9 %collective-permute-start.23 = (bf16[160,512]{1,0:T(8,128)(2,1)}, bf16[160,512]{1,0:T(8,128)(2,1)S(1)}, u32[]{:S(2)}, u32[]{:S(2)}) collective-permute-start(bf16[160,512]{1,0:T(8,128)(2,1)} %get-tuple-element.60), channel_id=1, source_target_pairs={{0,64},{32,96},{64,0},{96,32},{1,65},{33,97},{65,1},{97,33},{2,66}... | collective-permute-start | bytes 491528 | tf_op jit(solution)/shard_map/ppermute | solution.py:502
  134.4 10.0 %collective-permute-start.24 = (bf16[160,512]{1,0:T(8,128)(2,1)}, bf16[160,512]{1,0:T(8,128)(2,1)S(1)}, u32[]{:S(2)}, u32[]{:S(2)}) collective-permute-start(bf16[160,512]{1,0:T(8,128)(2,1)} %get-tuple-element.61), channel_id=1, source_target_pairs={{0,32},{32,64},{64,96},{96,0},{1,33},{33,65},{65,97},{97,1},{2,34}... | collective-permute-start | bytes 491528 | tf_op jit(solution)/shard_map/ppermute | solution.py:502
  135.1 9.3 %collective-permute-start.25 = (bf16[160,512]{1,0:T(8,128)(2,1)}, bf16[160,512]{1,0:T(8,128)(2,1)S(1)}, u32[]{:S(2)}, u32[]{:S(2)}) collective-permute-start(bf16[160,512]{1,0:T(8,128)(2,1)} %get-tuple-element.62), channel_id=1, source_target_pairs={{0,96},{32,0},{64,32},{96,64},{1,97},{33,1},{65,33},{97,65},{2,98}... | collective-permute-start | bytes 491528 | tf_op jit(solution)/shard_map/ppermute | solution.py:502

commit v6 on v5

--- a/solution.py
+++ b/solution.py
@@ -176,8 +176,10 @@
             for copy in loads(later):
                 copy.wait()
 
-        together(gradients(slot, 0), softmax(slot, 1))
-        together(gradients(slot, 1), softmax(later, 0))
+        together(softmax(slot, 1))
+        together(gradients(slot, 0))
+        together(softmax(later, 0))
+        together(gradients(slot, 1))
         for copy in stores(slot):
             copy.start()
 

time: 146 us -> 145 us (level); the launches traced: 145 us -> 143 us
  Pallas kernels: 43.6 us -> 18.8 us
  starting transfers between devices: 42.9 us -> 64.6 us
  waiting for transfers between devices: 41.5 us -> 43 us
    pallas_call x1, Pallas kernels: 32 us -> 7.22 us  [attention(): pl.pallas_call(attention_kernel, in_specs=[smem] * 3 + [anywhere] * 3 + [...]
    ppermute x21, starting transfers between devices: 22.5 us -> 43.4 us  [ring(): return lax.ppermute(array, axis, [(i, (i + step) % 4) for i in range(4)])]
    all_to_all x2, waiting for transfers between devices: 18.9 us -> 29.1 us  [exchange(): return lax.all_to_all(array, axes, 0, 0, tiled=True)]
    ppermute x21, waiting for transfers between devices: 19.1 us -> 9.46 us  [ring(): return lax.ppermute(array, axis, [(i, (i + step) % 4) for i in range(4)])]
  transfers between devices with their start and end apart: 31 -> 31, of which waited for: 12 -> 10; matrix products, arithmetic and copies ran while one was open for 6% -> 6% of each run, Pallas kernels for 30% -> 13%
where the time goes in v6:
time: 145 us; the launch traced here: 143 us
  starting transfers between devices  64.6 us (45%)
  waiting for transfers between devices  43 us (30%)
  Pallas kernels  18.8 us (13%)
  local copies, waits for them, and re-layouts  11.7 us (8%)
  matrix products  3.75 us (3%)
    ppermute x21, starting transfers between devices, ring(): return lax.ppermute(array, axis, [(i, (i + step) % 4) for i in range(4)])  43.4 us
    all_to_all x2, waiting for transfers between devices, exchange(): return lax.all_to_all(array, axes, 0, 0, tiled=True)  29.1 us
    all_to_all x2, starting transfers between devices, exchange(): return lax.all_to_all(array, axes, 0, 0, tiled=True)  11.5 us
    ppermute x8, starting transfers between devices, swap_cores(): return lax.ppermute(array, 'c', [(0, 1), (1, 0)])  9.68 us
    ppermute x21, waiting for transfers between devices, ring(): return lax.ppermute(array, axis, [(i, (i + step) % 4) for i in range(4)])  9.46 us
    pallas_call x1, Pallas kernels, attention(): pl.pallas_call(attention_kernel, in_specs=[smem] * 3 + [anywhere] * 3 + [...  7.22 us
    unnamed x17, local copies, waits for them, and re-layouts  5.61 us
    ppermute x8, waiting for transfers between devices, swap_cores(): return lax.ppermute(array, 'c', [(0, 1), (1, 0)])  4.37 us
  transfers between devices with their start and end apart: 31, of which 10 were waited for; matrix products, arithmetic and copies ran while one was open for 6% of the time, Pallas kernels for 13%

profile of v6, /device:TPU:1, one launch (start us, length us, event | category | flops | bytes accessed | tf_op | source)
XLA Modules:
  0.0 142.6 jit_solution(4972072864303645337)
XLA Ops:
  0.6 3.8 %fusion.3 = bf16[128,2,256]{2,0,1:T(8,128)(2,1)S(1)} fusion(bf16[5120,2,256]{2,1,0:T(2,128)(2,1)} %param.9, bf16[128,5120]{1,0:T(8,128)(2,1)} %hidden.1), kind=kOutput, calls=%fused_computation.4 | convolution fusion | flops 671154176 | bytes 6684672 | tf_op jit(solution)/shard_map/pd,dkc->pkc/dot_general | solution.py:481
  4.4 1.5 %collective-permute-start = (bf16[128,256]{1,0:T(8,128)(2,1)S(1)}, bf16[128,256]{1,0:T(8,128)(2,1)S(1)}, u32[]{:S(2)}, u32[]{:S(2)}) collective-permute-start(bf16[128,256]{1,0:T(8,128)(2,1)S(1)} %select_bitcast_fusion), channel_id=1, source_target_pairs={{0,4},{4,0},{1,5},{5,1},{2,6},{6,2},{3,7},{7,3},{8,12},{12,8},{9,1... | collective-permute-start | bytes 196616 | tf_op jit(solution)/shard_map/ppermute | solution.py:467
  5.9 0.9 collective-permute-done
  6.9 1.5 %broadcast_in_dim.2 = bf16[16,256,256]{2,1,0:T(8,128)(2,1)} broadcast(bf16[256,256]{1,0:T(8,128)(2,1)S(1)} %pad_maximum_fusion), dimensions={1,2} | broadcast | bytes 2228224 | tf_op jit(solution)/shard_map/broadcast_in_dim | solution.py:489
  8.4 8.0 %all-to-all-start = ((bf16[16,256,256]{2,1,0:T(8,128)(2,1)}), bf16[16,256,256]{2,1,0:T(8,128)(2,1)S(1)}, u32[]{:S(2)}, u32[]{:S(2)}) async-start(bf16[16,256,256]{2,1,0:T(8,128)(2,1)} %broadcast_in_dim.2), calls=%async_computation | async-start | bytes 4194304 | tf_op jit(solution)/shard_map/all_to_all | solution.py:471
  16.4 3.3 %columns.1.refs_2_ = bf16[8,640,128]{2,1,0:T(8,128)(2,1)} custom-call(bf16[128,5120]{1,0:T(8,128)(2,1)S(1)} %copy-done), custom_call_target="tpu_custom_call" | custom-call | tf_op jit(solution)/shard_map/columns/pallas_call | solution.py:259
  19.7 5.6 %copy.24 = bf16[5120,2,256]{2,0,1:T(8,128)(2,1)} copy(bf16[5120,2,256]{2,1,0:T(2,128)(2,1)} %param.9) | data formatting | bytes 10485760 | tf_op args[1]
  25.3 1.5 %reshape.27.refs_1_.own_hbm = bf16[8,128,512]{2,1,0:T(8,128)(2,1)} reshape(bf16[8,128,2,256]{3,2,1,0:T(2,128)(2,1)S(1)} %copy-done.6) | data formatting | bytes 2097152 | tf_op jit(solution)/shard_map/reshape | solution.py:492
  26.7 18.9 %all-to-all-done = bf16[16,256,256]{2,1,0:T(8,128)(2,1)S(1)} async-done(((bf16[16,256,256]{2,1,0:T(8,128)(2,1)}), bf16[16,256,256]{2,1,0:T(8,128)(2,1)S(1)}, u32[]{:S(2)}, u32[]{:S(2)}) %all-to-all-start) | async-done | bytes 2097184 | tf_op jit(solution)/shard_map/all_to_all | solution.py:471
  45.6 2.6 %collective-permute-start.1 = (bf16[32,128,256]{2,1,0:T(8,128)(2,1)S(1)}, bf16[32,128,256]{2,1,0:T(8,128)(2,1)}, u32[]{:S(2)}, u32[]{:S(2)}) collective-permute-start(bf16[32,128,256]{2,1,0:T(8,128)(2,1)S(1)} %after.4.near), channel_id=1, source_target_pairs={{0,4},{4,0},{1,5},{5,1},{2,6},{6,2},{3,7},{7,3},{8,12},{12,8},{9,1... | collective-permute-start | bytes 6291464 | tf_op jit(solution)/shard_map/ppermute | solution.py:467
  48.3 3.5 %all-to-all-start.1 = ((bf16[8,640,128]{2,1,0:T(8,128)(2,1)}), bf16[8,640,128]{2,1,0:T(8,128)(2,1)S(1)}, u32[]{:S(2)}, u32[]{:S(2)}) async-start(bf16[8,640,128]{2,1,0:T(8,128)(2,1)} %columns.1.refs_2_), calls=%async_computation.1 | async-start | bytes 2621440 | tf_op jit(solution)/shard_map/all_to_all | solution.py:471
  51.8 0.4 collective-permute-done.1.far
  52.2 7.2 %attention.1 = (bf16[8,128,1280]{2,1,0:T(8,128)(2,1)}, bf16[8,128,1280]{2,1,0:T(8,128)(2,1)}, bf16[8,128,512]{2,1,0:T(8,128)(2,1)}, bf16[16,128,256]{2,1,0:T(8,1...) custom-call(s32[32]{0:T(128)S(1)} %copy-done.4, ...), custom_call_target="tpu_custom_call" | custom-call | flops 10066329600 | bytes 16777216 | tf_op jit(solution)/shard_map/attention/pallas_call | solution.py:429
  59.4 10.3 %all-to-all-done.1.refs_1_.hidden = bf16[8,640,128]{2,1,0:T(8,128)(2,1)S(1)} async-done(((bf16[8,640,128]{2,1,0:T(8,128)(2,1)}), bf16[8,640,128]{2,1,0:T(8,128)(2,1)S(1)}, u32[]{:S(2)}, u32[]{:S(2)}) %all-to-all-start.1) | async-done | bytes 1310752 | tf_op jit(solution)/shard_map/all_to_all | solution.py:471
  69.7 0.9 collective-permute-start.2
  70.6 3.0 %collective-permute-done.2.got = bf16[16,128,256]{2,1,0:T(8,128)(2,1)S(1)} collective-permute-done((bf16[16,128,256]{2,1,0:T(8,128)(2,1)}, bf16[16,128,256]{2,1,0:T(8,128)(2,1)S(1)}, u32[]{:S(2)}, u32[]{:S(2)}) %collective-permute-start.2) | collective-permute-done | bytes 1048608 | tf_op jit(solution)/shard_map/ppermute | solution.py:467
  73.7 0.2 split.2
  73.9 5.3 %collective-permute-start.3 = (bf16[4,128,256]{2,1,0:T(8,128)(2,1)S(1)}, bf16[4,128,256]{2,1,0:T(8,128)(2,1)S(1)}, u32[]{:S(2)}, u32[]{:S(2)}) collective-permute-start(bf16[4,128,256]{2,1,0:T(8,128)(2,1)S(1)} %get-tuple-element.42), channel_id=1, source_target_pairs={{0,32},{32,64},{64,96},{96,0},{1,33},{33,65},{65,97},{97,1},{2,34}... | collective-permute-start | bytes 786440 | tf_op jit(solution)/shard_map/ppermute | solution.py:504
  79.2 8.2 %collective-permute-start.4 = (bf16[4,128,256]{2,1,0:T(8,128)(2,1)S(1)}, bf16[4,128,256]{2,1,0:T(8,128)(2,1)S(1)}, u32[]{:S(2)}, u32[]{:S(2)}) collective-permute-start(bf16[4,128,256]{2,1,0:T(8,128)(2,1)S(1)} %get-tuple-element.43), channel_id=1, source_target_pairs={{0,64},{32,96},{64,0},{96,32},{1,65},{33,97},{65,1},{97,33},{2,66}... | collective-permute-start | bytes 786440 | tf_op jit(solution)/shard_map/ppermute | solution.py:504
  87.3 2.0 %collective-permute-start.5 = (bf16[4,128,256]{2,1,0:T(8,128)(2,1)S(1)}, bf16[4,128,256]{2,1,0:T(8,128)(2,1)S(1)}, u32[]{:S(2)}, u32[]{:S(2)}) collective-permute-start(bf16[4,128,256]{2,1,0:T(8,128)(2,1)S(1)} %get-tuple-element.44), channel_id=1, source_target_pairs={{0,96},{32,0},{64,32},{96,64},{1,97},{33,1},{65,33},{97,65},{2,98}... | collective-permute-start | bytes 786440 | tf_op jit(solution)/shard_map/ppermute | solution.py:504
  89.7 3.1 %collective-permute-start.10 = (bf16[4,128,256]{2,1,0:T(8,128)(2,1)S(1)}, bf16[4,128,256]{2,1,0:T(8,128)(2,1)S(1)}, u32[]{:S(2)}, u32[]{:S(2)}) collective-permute-start(bf16[4,128,256]{2,1,0:T(8,128)(2,1)S(1)} %get-tuple-element.52), channel_id=1, source_target_pairs={{0,8},{8,16},{16,24},{24,0},{1,9},{9,17},{17,25},{25,1},{2,10},{10... | collective-permute-start | bytes 786440 | tf_op jit(solution)/shard_map/ppermute | solution.py:504
  92.8 2.8 %collective-permute-start.12 = (bf16[4,128,256]{2,1,0:T(8,128)(2,1)S(1)}, bf16[4,128,256]{2,1,0:T(8,128)(2,1)S(1)}, u32[]{:S(2)}, u32[]{:S(2)}) collective-permute-start(bf16[4,128,256]{2,1,0:T(8,128)(2,1)S(1)} %get-tuple-element.54), channel_id=1, source_target_pairs={{0,24},{8,0},{16,8},{24,16},{1,25},{9,1},{17,9},{25,17},{2,26},{10... | collective-permute-start | bytes 786440 | tf_op jit(solution)/shard_map/ppermute | solution.py:504
  95.6 3.8 %collective-permute-done.4.refs_2_ = bf16[4,128,256]{2,1,0:T(8,128)(2,1)S(1)} collective-permute-done((bf16[4,128,256]{2,1,0:T(8,128)(2,1)S(1)}, bf16[4,128,256]{2,1,0:T(8,128)(2,1)S(1)}, u32[]{:S(2)}, u32[]{:S(2)}) %collective-permute-start.4) | collective-permute-done | bytes 262176 | tf_op jit(solution)/shard_map/ppermute | solution.py:504
  99.7 2.5 %hold.1.refs_1_.weight = bf16[2,5120,256]{2,1,0:T(8,128)(2,1)S(1)} custom-call(bf16[2,5120,256]{2,1,0:T(8,128)(2,1)} %after.6.source), custom_call_target="tpu_custom_call" | custom-call | tf_op jit(solution)/shard_map/hold/pallas_call | solution.py:365
  102.2 4.0 %collective-permute-start.7 = (bf16[128,256]{1,0:T(8,128)(2,1)S(1)}, bf16[128,256]{1,0:T(8,128)(2,1)S(1)}, u32[]{:S(2)}, u32[]{:S(2)}) collective-permute-start(bf16[128,256]{1,0:T(8,128)(2,1)S(1)} %get-tuple-element.47), channel_id=1, source_target_pairs={{0,16},{8,24},{16,0},{24,8},{1,17},{9,25},{17,1},{25,9},{2,18},{10... | collective-permute-start | bytes 196616 | tf_op jit(solution)/shard_map/ppermute | solution.py:504
  106.3 0.7 collective-permute-start.13
  107.1 3.0 %collective-permute-start.14 = (bf16[128,256]{1,0:T(8,128)(2,1)S(1)}, bf16[128,256]{1,0:T(8,128)(2,1)S(1)}, u32[]{:S(2)}, u32[]{:S(2)}) collective-permute-start(bf16[128,256]{1,0:T(8,128)(2,1)S(1)} %get-tuple-element.57), channel_id=1, source_target_pairs={{0,64},{32,96},{64,0},{96,32},{1,65},{33,97},{65,1},{97,33},{2,66}... | collective-permute-start | bytes 196616 | tf_op jit(solution)/shard_map/ppermute | solution.py:504
  110.1 0.8 collective-permute-start.15
  110.8 1.6 %collective-permute-done.14.refs_6_ = bf16[128,256]{1,0:T(8,128)(2,1)S(1)} collective-permute-done((bf16[128,256]{1,0:T(8,128)(2,1)S(1)}, bf16[128,256]{1,0:T(8,128)(2,1)S(1)}, u32[]{:S(2)}, u32[]{:S(2)}) %collective-permute-start.14) | collective-permute-done | bytes 65568 | tf_op jit(solution)/shard_map/ppermute | solution.py:504
  112.4 1.1 collective-permute-done.15.refs_7_
  113.5 1.5 %collective-permute-start.18 = (bf16[128,512]{1,0:T(8,128)(2,1)S(1)}, bf16[128,512]{1,0:T(8,128)(2,1)S(1)}, u32[]{:S(2)}, u32[]{:S(2)}) collective-permute-start(bf16[128,512]{1,0:T(8,128)(2,1)S(1)} %block.1.refs_0_), channel_id=1, source_target_pairs={{0,24},{8,0},{16,8},{24,16},{1,25},{9,1},{17,9},{25,17},{2,26},{10... | collective-permute-start | bytes 393224 | tf_op jit(solution)/shard_map/ppermute | solution.py:504
  115.0 1.6 %collective-permute-start.17 = (bf16[128,512]{1,0:T(8,128)(2,1)S(1)}, bf16[128,512]{1,0:T(8,128)(2,1)S(1)}, u32[]{:S(2)}, u32[]{:S(2)}) collective-permute-start(bf16[128,512]{1,0:T(8,128)(2,1)S(1)} %block.1.refs_0_), channel_id=1, source_target_pairs={{0,16},{8,24},{16,0},{24,8},{1,17},{9,25},{17,1},{25,9},{2,18},{10... | collective-permute-start | bytes 393224 | tf_op jit(solution)/shard_map/ppermute | solution.py:504
  116.6 2.2 %prompt.1 = (bf16[128,1280]{1,0:T(8,128)(2,1)S(1)}, bf16[128,1280]{1,0:T(8,128)(2,1)}, bf16[128,1280]{1,0:T(8,128)(2,1)S(1)}, bf16[128,1280]{1,0:T(8,128)(2,1)}) custom-call(bf16[128,512]{1,0:T(8,128)(2,1)S(1)} %block.1.refs_0_, bf16[2,5120,256]{2,1,0:T(8,128)(2,1)S(1)} %hold.1.refs_1_.weight), custom_call_target="tpu_custom_call" | custom-call | flops 671088640 | bytes 4194304 | tf_op jit(solution)/shard_map/prompt/pallas_call | solution.py:389
  118.9 2.7 %collective-permute-start.26 = (bf16[128,1280]{1,0:T(8,128)(2,1)S(1)}, bf16[128,1280]{1,0:T(8,128)(2,1)S(1)}, u32[]{:S(2)}, u32[]{:S(2)}) collective-permute-start(bf16[128,1280]{1,0:T(8,128)(2,1)S(1)} %get-tuple-element.64), channel_id=1, source_target_pairs={{0,2},{1,3},{2,0},{3,1},{4,6},{5,7},{6,4},{7,5},{8,10},{9,11},{10,... | collective-permute-start | bytes 983048 | tf_op jit(solution)/shard_map/ppermute | solution.py:504
  121.6 3.7 %collective-permute-start.19 = (bf16[128,512]{1,0:T(8,128)(2,1)S(1)}, bf16[128,512]{1,0:T(8,128)(2,1)S(1)}, u32[]{:S(2)}, u32[]{:S(2)}) collective-permute-start(bf16[128,512]{1,0:T(8,128)(2,1)S(1)} %block.1.refs_0_), channel_id=1, source_target_pairs={{0,4},{4,0},{1,5},{5,1},{2,6},{6,2},{3,7},{7,3},{8,12},{12,8},{9,1... | collective-permute-start | bytes 393224 | tf_op jit(solution)/shard_map/ppermute | solution.py:467
  125.3 0.5 collective-permute-start.21
  125.8 0.4 collective-permute-start.20
  126.3 1.2 collective-permute-start.27
  127.5 1.5 %collective-permute-start.28 = (bf16[128,1280]{1,0:T(8,128)(2,1)}, bf16[128,1280]{1,0:T(8,128)(2,1)S(1)}, u32[]{:S(2)}, u32[]{:S(2)}) collective-permute-start(bf16[128,1280]{1,0:T(8,128)(2,1)} %get-tuple-element.66), channel_id=1, source_target_pairs={{0,3},{1,0},{2,1},{3,2},{4,7},{5,4},{6,5},{7,6},{8,11},{9,8},{10,9... | collective-permute-start | bytes 983048 | tf_op jit(solution)/shard_map/ppermute | solution.py:504
  129.0 1.7 %term.1 = (bf16[160,512]{1,0:T(8,128)(2,1)S(1)}, bf16[160,512]{1,0:T(8,128)(2,1)}, bf16[160,512]{1,0:T(8,128)(2,1)}, bf16[160,512]{1,0:T(8,128)(2,1)}) custom-call(bf16[8,640,128]{2,1,0:T(8,128)(2,1)S(1)} %all-to-all-done.1.refs_1_.hidden, bf16[128,512]{1,0:T(8,128)(2,1)S(1)} %block.1.refs_0_, bf16[128,512]{1,0:T(8,128)(2,1)S(1)} %collective-permute-done.16.refs_1_, ...), custom_call_target="tpu_custom_call" | custom-call | flops 2000000000 | bytes 10000000 | tf_op jit(solution)/shard_map/term/pallas_call | solution.py:346
  130.7 2.2 %collective-permute-start.23 = (bf16[160,512]{1,0:T(8,128)(2,1)}, bf16[160,512]{1,0:T(8,128)(2,1)S(1)}, u32[]{:S(2)}, u32[]{:S(2)}) collective-permute-start(bf16[160,512]{1,0:T(8,128)(2,1)} %get-tuple-element.60), channel_id=1, source_target_pairs={{0,64},{32,96},{64,0},{96,32},{1,65},{33,97},{65,1},{97,33},{2,66}... | collective-permute-start | bytes 491528 | tf_op jit(solution)/shard_map/ppermute | solution.py:504
  132.9 1.7 %collective-permute-start.24 = (bf16[160,512]{1,0:T(8,128)(2,1)}, bf16[160,512]{1,0:T(8,128)(2,1)S(1)}, u32[]{:S(2)}, u32[]{:S(2)}) collective-permute-start(bf16[160,512]{1,0:T(8,128)(2,1)} %get-tuple-element.61), channel_id=1, source_target_pairs={{0,32},{32,64},{64,96},{96,0},{1,33},{33,65},{65,97},{97,1},{2,34}... | collective-permute-start | bytes 491528 | tf_op jit(solution)/shard_map/ppermute | solution.py:504
  134.6 1.0 collective-permute-start.25
  135.6 2.1 %reshape.29 = bf16[8,128,2,256]{3,2,1,0:T(2,128)(2,1)} reshape(bf16[8,128,512]{2,1,0:T(8,128)(2,1)} %get-tuple-element.38) | data formatting | bytes 2097152 | tf_op jit(solution)/shard_map/reshape | solution.py:501
  137.7 0.9 sum.3
  138.6 2.7 %collective-permute-done.24.refs_2_ = bf16[160,512]{1,0:T(8,128)(2,1)S(1)} collective-permute-done((bf16[160,512]{1,0:T(8,128)(2,1)}, bf16[160,512]{1,0:T(8,128)(2,1)S(1)}, u32[]{:S(2)}, u32[]{:S(2)}) %collective-permute-start.24) | collective-permute-done | bytes 163872 | tf_op jit(solution)/shard_map/ppermute | solution.py:504
  141.3 0.3 collective-permute-done.25.refs_3_
  141.7 0.9 reshape.30
  (55 shorter events, 1.1 us)
Async XLA Ops:
  4.4 2.4 %collective-permute-start = (bf16[128,256]{1,0:T(8,128)(2,1)S(1)}, bf16[128,256]{1,0:T(8,128)(2,1)S(1)}, u32[]{:S(2)}, u32[]{:S(2)}) collective-permute-start(bf16[128,256]{1,0:T(8,128)(2,1)S(1)} %select_bitcast_fusion), channel_id=1, source_target_pairs={{0,4},{4,0},{1,5},{5,1},{2,6},{6,2},{3,7},{7,3},{8,12},{12,8},{9,1... | collective-permute-start | bytes 196616 | tf_op jit(solution)/shard_map/ppermute | solution.py:467
  8.4 8.0 %copy-start = (bf16[128,5120]{1,0:T(8,128)(2,1)S(1)}, bf16[128,5120]{1,0:T(8,128)(2,1)}, u32[]{:S(2)}) copy-start(bf16[128,5120]{1,0:T(8,128)(2,1)} %hidden.1) | copy-start | bytes 3932164
  8.4 37.2 %all-to-all-start = ((bf16[16,256,256]{2,1,0:T(8,128)(2,1)}), bf16[16,256,256]{2,1,0:T(8,128)(2,1)S(1)}, u32[]{:S(2)}, u32[]{:S(2)}) async-start(bf16[16,256,256]{2,1,0:T(8,128)(2,1)} %broadcast_in_dim.2), calls=%async_computation | async-start | bytes 4194304 | tf_op jit(solution)/shard_map/all_to_all | solution.py:471
  19.7 5.6 %copy-start.6 = (bf16[8,128,2,256]{3,2,1,0:T(2,128)(2,1)S(1)}, bf16[8,128,2,256]{3,2,1,0:T(2,128)(2,1)}, u32[]{:S(2)}) copy-start(bf16[8,128,2,256]{3,2,1,0:T(2,128)(2,1)} %param.12) | copy-start | bytes 3145732
  45.6 6.6 %copy-start.3 = (s32[32,8]{0,1:T(8,128)S(1)}, s32[32,8]{0,1:T(8,128)}, u32[]{:S(2)}) copy-start(s32[32,8]{0,1:T(8,128)} %param.14) | copy-start | bytes 3076
  45.6 6.6 %copy-start.4 = (s32[32]{0:T(128)S(1)}, s32[32]{0:T(128)}, u32[]{:S(2)}) copy-start(s32[32]{0:T(128)} %pack_counts.1) | copy-start | bytes 388
  45.6 6.6 %copy-start.5 = (s32[32]{0:T(128)S(1)}, s32[32]{0:T(128)}, u32[]{:S(2)}) copy-start(s32[32]{0:T(128)} %block_group.1) | copy-start | bytes 388
  45.6 6.5 %collective-permute-start.1 = (bf16[32,128,256]{2,1,0:T(8,128)(2,1)S(1)}, bf16[32,128,256]{2,1,0:T(8,128)(2,1)}, u32[]{:S(2)}, u32[]{:S(2)}) collective-permute-start(bf16[32,128,256]{2,1,0:T(8,128)(2,1)S(1)} %after.4.near), channel_id=1, source_target_pairs={{0,4},{4,0},{1,5},{5,1},{2,6},{6,2},{3,7},{7,3},{8,12},{12,8},{9,1... | collective-permute-start | bytes 6291464 | tf_op jit(solution)/shard_map/ppermute | solution.py:467
  48.3 21.4 %all-to-all-start.1 = ((bf16[8,640,128]{2,1,0:T(8,128)(2,1)}), bf16[8,640,128]{2,1,0:T(8,128)(2,1)S(1)}, u32[]{:S(2)}, u32[]{:S(2)}) async-start(bf16[8,640,128]{2,1,0:T(8,128)(2,1)} %columns.1.refs_2_), calls=%async_computation.1 | async-start | bytes 2621440 | tf_op jit(solution)/shard_map/all_to_all | solution.py:471
  59.4 11.2 %copy-start.7 = (bf16[16,128,256]{2,1,0:T(8,128)(2,1)S(1)}, bf16[16,128,256]{2,1,0:T(8,128)(2,1)}, u32[]{:S(2)}) copy-start(bf16[16,128,256]{2,1,0:T(8,128)(2,1)} %get-tuple-element.50) | copy-start | bytes 3145732
  59.4 14.3 %copy-start.2 = (bf16[16,128,256]{2,1,0:T(8,128)(2,1)S(1)}, bf16[16,128,256]{2,1,0:T(8,128)(2,1)}, u32[]{:S(2)}) copy-start(bf16[16,128,256]{2,1,0:T(8,128)(2,1)} %get-tuple-element.39.keep) | copy-start | bytes 3145732
  69.7 19.6 %copy-start.1 = (bf16[16,128,256]{2,1,0:T(8,128)(2,1)S(1)}, bf16[16,128,256]{2,1,0:T(8,128)(2,1)}, u32[]{:S(2)}) copy-start(bf16[16,128,256]{2,1,0:T(8,128)(2,1)} %get-tuple-element.49.keep) | copy-start | bytes 3145732
  69.7 4.0 %collective-permute-start.2 = (bf16[16,128,256]{2,1,0:T(8,128)(2,1)}, bf16[16,128,256]{2,1,0:T(8,128)(2,1)S(1)}, u32[]{:S(2)}, u32[]{:S(2)}) collective-permute-start(bf16[16,128,256]{2,1,0:T(8,128)(2,1)} %after.5.refs_1_), channel_id=1, source_target_pairs={{0,4},{4,0},{1,5},{5,1},{2,6},{6,2},{3,7},{7,3},{8,12},{12,8},{9,1... | collective-permute-start | bytes 3145736 | tf_op jit(solution)/shard_map/ppermute | solution.py:467
  70.6 18.8 %collective-permute-start.9 = (bf16[16,128,256]{2,1,0:T(8,128)(2,1)S(1)}, bf16[16,128,256]{2,1,0:T(8,128)(2,1)S(1)}, u32[]{:S(2)}, u32[]{:S(2)}) collective-permute-start(bf16[16,128,256]{2,1,0:T(8,128)(2,1)S(1)} %copy-done.7), channel_id=1, source_target_pairs={{0,4},{4,0},{1,5},{5,1},{2,6},{6,2},{3,7},{7,3},{8,12},{12,8},{9,1... | collective-permute-start | bytes 3145736 | tf_op jit(solution)/shard_map/ppermute | solution.py:467
  73.9 18.9 %collective-permute-start.3 = (bf16[4,128,256]{2,1,0:T(8,128)(2,1)S(1)}, bf16[4,128,256]{2,1,0:T(8,128)(2,1)S(1)}, u32[]{:S(2)}, u32[]{:S(2)}) collective-permute-start(bf16[4,128,256]{2,1,0:T(8,128)(2,1)S(1)} %get-tuple-element.42), channel_id=1, source_target_pairs={{0,32},{32,64},{64,96},{96,0},{1,33},{33,65},{65,97},{97,1},{2,34}... | collective-permute-start | bytes 786440 | tf_op jit(solution)/shard_map/ppermute | solution.py:504
  79.2 20.3 %collective-permute-start.4 = (bf16[4,128,256]{2,1,0:T(8,128)(2,1)S(1)}, bf16[4,128,256]{2,1,0:T(8,128)(2,1)S(1)}, u32[]{:S(2)}, u32[]{:S(2)}) collective-permute-start(bf16[4,128,256]{2,1,0:T(8,128)(2,1)S(1)} %get-tuple-element.43), channel_id=1, source_target_pairs={{0,64},{32,96},{64,0},{96,32},{1,65},{33,97},{65,1},{97,33},{2,66}... | collective-permute-start | bytes 786440 | tf_op jit(solution)/shard_map/ppermute | solution.py:504
  87.3 12.1 %collective-permute-start.5 = (bf16[4,128,256]{2,1,0:T(8,128)(2,1)S(1)}, bf16[4,128,256]{2,1,0:T(8,128)(2,1)S(1)}, u32[]{:S(2)}, u32[]{:S(2)}) collective-permute-start(bf16[4,128,256]{2,1,0:T(8,128)(2,1)S(1)} %get-tuple-element.44), channel_id=1, source_target_pairs={{0,96},{32,0},{64,32},{96,64},{1,97},{33,1},{65,33},{97,65},{2,98}... | collective-permute-start | bytes 786440 | tf_op jit(solution)/shard_map/ppermute | solution.py:504
  89.6 16.6 %collective-permute-start.11 = (bf16[4,128,256]{2,1,0:T(8,128)(2,1)S(1)}, bf16[4,128,256]{2,1,0:T(8,128)(2,1)S(1)}, u32[]{:S(2)}, u32[]{:S(2)}) collective-permute-start(bf16[4,128,256]{2,1,0:T(8,128)(2,1)S(1)} %get-tuple-element.53), channel_id=1, source_target_pairs={{0,16},{8,24},{16,0},{24,8},{1,17},{9,25},{17,1},{25,9},{2,18},{10... | collective-permute-start | bytes 786440 | tf_op jit(solution)/shard_map/ppermute | solution.py:504
  89.7 16.5 %collective-permute-start.10 = (bf16[4,128,256]{2,1,0:T(8,128)(2,1)S(1)}, bf16[4,128,256]{2,1,0:T(8,128)(2,1)S(1)}, u32[]{:S(2)}, u32[]{:S(2)}) collective-permute-start(bf16[4,128,256]{2,1,0:T(8,128)(2,1)S(1)} %get-tuple-element.52), channel_id=1, source_target_pairs={{0,8},{8,16},{16,24},{24,0},{1,9},{9,17},{17,25},{25,1},{2,10},{10... | collective-permute-start | bytes 786440 | tf_op jit(solution)/shard_map/ppermute | solution.py:504
  92.8 13.4 %collective-permute-start.12 = (bf16[4,128,256]{2,1,0:T(8,128)(2,1)S(1)}, bf16[4,128,256]{2,1,0:T(8,128)(2,1)S(1)}, u32[]{:S(2)}, u32[]{:S(2)}) collective-permute-start(bf16[4,128,256]{2,1,0:T(8,128)(2,1)S(1)} %get-tuple-element.54), channel_id=1, source_target_pairs={{0,24},{8,0},{16,8},{24,16},{1,25},{9,1},{17,9},{25,17},{2,26},{10... | collective-permute-start | bytes 786440 | tf_op jit(solution)/shard_map/ppermute | solution.py:504
  99.6 10.5 %collective-permute-start.6 = (bf16[128,256]{1,0:T(8,128)(2,1)S(1)}, bf16[128,256]{1,0:T(8,128)(2,1)S(1)}, u32[]{:S(2)}, u32[]{:S(2)}) collective-permute-start(bf16[128,256]{1,0:T(8,128)(2,1)S(1)} %get-tuple-element.46), channel_id=1, source_target_pairs={{0,8},{8,16},{16,24},{24,0},{1,9},{9,17},{17,25},{25,1},{2,10},{10... | collective-permute-start | bytes 196616 | tf_op jit(solution)/shard_map/ppermute | solution.py:504
  102.2 8.7 %collective-permute-start.7 = (bf16[128,256]{1,0:T(8,128)(2,1)S(1)}, bf16[128,256]{1,0:T(8,128)(2,1)S(1)}, u32[]{:S(2)}, u32[]{:S(2)}) collective-permute-start(bf16[128,256]{1,0:T(8,128)(2,1)S(1)} %get-tuple-element.47), channel_id=1, source_target_pairs={{0,16},{8,24},{16,0},{24,8},{1,17},{9,25},{17,1},{25,9},{2,18},{10... | collective-permute-start | bytes 196616 | tf_op jit(solution)/shard_map/ppermute | solution.py:504
  106.2 4.7 %collective-permute-start.8 = (bf16[128,256]{1,0:T(8,128)(2,1)S(1)}, bf16[128,256]{1,0:T(8,128)(2,1)S(1)}, u32[]{:S(2)}, u32[]{:S(2)}) collective-permute-start(bf16[128,256]{1,0:T(8,128)(2,1)S(1)} %get-tuple-element.48), channel_id=1, source_target_pairs={{0,24},{8,0},{16,8},{24,16},{1,25},{9,1},{17,9},{25,17},{2,26},{10... | collective-permute-start | bytes 196616 | tf_op jit(solution)/shard_map/ppermute | solution.py:504
  106.3 4.5 %collective-permute-start.13 = (bf16[128,256]{1,0:T(8,128)(2,1)S(1)}, bf16[128,256]{1,0:T(8,128)(2,1)S(1)}, u32[]{:S(2)}, u32[]{:S(2)}) collective-permute-start(bf16[128,256]{1,0:T(8,128)(2,1)S(1)} %get-tuple-element.56), channel_id=1, source_target_pairs={{0,32},{32,64},{64,96},{96,0},{1,33},{33,65},{65,97},{97,1},{2,34}... | collective-permute-start | bytes 196616 | tf_op jit(solution)/shard_map/ppermute | solution.py:504
  107.1 5.3 %collective-permute-start.14 = (bf16[128,256]{1,0:T(8,128)(2,1)S(1)}, bf16[128,256]{1,0:T(8,128)(2,1)S(1)}, u32[]{:S(2)}, u32[]{:S(2)}) collective-permute-start(bf16[128,256]{1,0:T(8,128)(2,1)S(1)} %get-tuple-element.57), channel_id=1, source_target_pairs={{0,64},{32,96},{64,0},{96,32},{1,65},{33,97},{65,1},{97,33},{2,66}... | collective-permute-start | bytes 196616 | tf_op jit(solution)/shard_map/ppermute | solution.py:504
  110.1 3.4 %collective-permute-start.15 = (bf16[128,256]{1,0:T(8,128)(2,1)S(1)}, bf16[128,256]{1,0:T(8,128)(2,1)S(1)}, u32[]{:S(2)}, u32[]{:S(2)}) collective-permute-start(bf16[128,256]{1,0:T(8,128)(2,1)S(1)} %get-tuple-element.58), channel_id=1, source_target_pairs={{0,96},{32,0},{64,32},{96,64},{1,97},{33,1},{65,33},{97,65},{2,98}... | collective-permute-start | bytes 196616 | tf_op jit(solution)/shard_map/ppermute | solution.py:504
  113.5 11.7 %collective-permute-start.18 = (bf16[128,512]{1,0:T(8,128)(2,1)S(1)}, bf16[128,512]{1,0:T(8,128)(2,1)S(1)}, u32[]{:S(2)}, u32[]{:S(2)}) collective-permute-start(bf16[128,512]{1,0:T(8,128)(2,1)S(1)} %block.1.refs_0_), channel_id=1, source_target_pairs={{0,24},{8,0},{16,8},{24,16},{1,25},{9,1},{17,9},{25,17},{2,26},{10... | collective-permute-start | bytes 393224 | tf_op jit(solution)/shard_map/ppermute | solution.py:504
  115.0 10.3 %collective-permute-start.17 = (bf16[128,512]{1,0:T(8,128)(2,1)S(1)}, bf16[128,512]{1,0:T(8,128)(2,1)S(1)}, u32[]{:S(2)}, u32[]{:S(2)}) collective-permute-start(bf16[128,512]{1,0:T(8,128)(2,1)S(1)} %block.1.refs_0_), channel_id=1, source_target_pairs={{0,16},{8,24},{16,0},{24,8},{1,17},{9,25},{17,1},{25,9},{2,18},{10... | collective-permute-start | bytes 393224 | tf_op jit(solution)/shard_map/ppermute | solution.py:504
  116.6 9.2 %collective-permute-start.16 = (bf16[128,512]{1,0:T(8,128)(2,1)S(1)}, bf16[128,512]{1,0:T(8,128)(2,1)S(1)}, u32[]{:S(2)}, u32[]{:S(2)}) collective-permute-start(bf16[128,512]{1,0:T(8,128)(2,1)S(1)} %block.1.refs_0_), channel_id=1, source_target_pairs={{0,8},{8,16},{16,24},{24,0},{1,9},{9,17},{17,25},{25,1},{2,10},{10... | collective-permute-start | bytes 393224 | tf_op jit(solution)/shard_map/ppermute | solution.py:504
  118.9 15.7 %collective-permute-start.26 = (bf16[128,1280]{1,0:T(8,128)(2,1)S(1)}, bf16[128,1280]{1,0:T(8,128)(2,1)S(1)}, u32[]{:S(2)}, u32[]{:S(2)}) collective-permute-start(bf16[128,1280]{1,0:T(8,128)(2,1)S(1)} %get-tuple-element.64), channel_id=1, source_target_pairs={{0,2},{1,3},{2,0},{3,1},{4,6},{5,7},{6,4},{7,5},{8,10},{9,11},{10,... | collective-permute-start | bytes 983048 | tf_op jit(solution)/shard_map/ppermute | solution.py:504
  121.6 4.6 %collective-permute-start.19 = (bf16[128,512]{1,0:T(8,128)(2,1)S(1)}, bf16[128,512]{1,0:T(8,128)(2,1)S(1)}, u32[]{:S(2)}, u32[]{:S(2)}) collective-permute-start(bf16[128,512]{1,0:T(8,128)(2,1)S(1)} %block.1.refs_0_), channel_id=1, source_target_pairs={{0,4},{4,0},{1,5},{5,1},{2,6},{6,2},{3,7},{7,3},{8,12},{12,8},{9,1... | collective-permute-start | bytes 393224 | tf_op jit(solution)/shard_map/ppermute | solution.py:467
  125.3 2.2 %collective-permute-start.22 = (bf16[128,512]{1,0:T(8,128)(2,1)S(1)}, bf16[128,512]{1,0:T(8,128)(2,1)S(1)}, u32[]{:S(2)}, u32[]{:S(2)}) collective-permute-start(bf16[128,512]{1,0:T(8,128)(2,1)S(1)} %collective-permute-done.18.refs_3_), channel_id=1, source_target_pairs={{0,4},{4,0},{1,5},{5,1},{2,6},{6,2},{3,7},{7,3},{8,12},{12,8},{9,1... | collective-permute-start | bytes 393224 | tf_op jit(solution)/shard_map/ppermute | solution.py:467
  125.3 3.7 %collective-permute-start.21 = (bf16[128,512]{1,0:T(8,128)(2,1)S(1)}, bf16[128,512]{1,0:T(8,128)(2,1)S(1)}, u32[]{:S(2)}, u32[]{:S(2)}) collective-permute-start(bf16[128,512]{1,0:T(8,128)(2,1)S(1)} %collective-permute-done.17.refs_2_), channel_id=1, source_target_pairs={{0,4},{4,0},{1,5},{5,1},{2,6},{6,2},{3,7},{7,3},{8,12},{12,8},{9,1... | collective-permute-start | bytes 393224 | tf_op jit(solution)/shard_map/ppermute | solution.py:467
  125.8 3.2 %collective-permute-start.20 = (bf16[128,512]{1,0:T(8,128)(2,1)S(1)}, bf16[128,512]{1,0:T(8,128)(2,1)S(1)}, u32[]{:S(2)}, u32[]{:S(2)}) collective-permute-start(bf16[128,512]{1,0:T(8,128)(2,1)S(1)} %collective-permute-done.16.refs_1_), channel_id=1, source_target_pairs={{0,4},{4,0},{1,5},{5,1},{2,6},{6,2},{3,7},{7,3},{8,12},{12,8},{9,1... | collective-permute-start | bytes 393224 | tf_op jit(solution)/shard_map/ppermute | solution.py:467
  126.3 11.5 %collective-permute-start.27 = (bf16[128,1280]{1,0:T(8,128)(2,1)}, bf16[128,1280]{1,0:T(8,128)(2,1)S(1)}, u32[]{:S(2)}, u32[]{:S(2)}) collective-permute-start(bf16[128,1280]{1,0:T(8,128)(2,1)} %get-tuple-element.65), channel_id=1, source_target_pairs={{0,1},{1,2},{2,3},{3,0},{4,5},{5,6},{6,7},{7,4},{8,9},{9,10},{10,1... | collective-permute-start | bytes 983048 | tf_op jit(solution)/shard_map/ppermute | solution.py:504
  127.5 10.3 %collective-permute-start.28 = (bf16[128,1280]{1,0:T(8,128)(2,1)}, bf16[128,1280]{1,0:T(8,128)(2,1)S(1)}, u32[]{:S(2)}, u32[]{:S(2)}) collective-permute-start(bf16[128,1280]{1,0:T(8,128)(2,1)} %get-tuple-element.66), channel_id=1, source_target_pairs={{0,3},{1,0},{2,1},{3,2},{4,7},{5,4},{6,5},{7,6},{8,11},{9,8},{10,9... | collective-permute-start | bytes 983048 | tf_op jit(solution)/shard_map/ppermute | solution.py:504
  130.7 7.9 %collective-permute-start.23 = (bf16[160,512]{1,0:T(8,128)(2,1)}, bf16[160,512]{1,0:T(8,128)(2,1)S(1)}, u32[]{:S(2)}, u32[]{:S(2)}) collective-permute-start(bf16[160,512]{1,0:T(8,128)(2,1)} %get-tuple-element.60), channel_id=1, source_target_pairs={{0,64},{32,96},{64,0},{96,32},{1,65},{33,97},{65,1},{97,33},{2,66}... | collective-permute-start | bytes 491528 | tf_op jit(solution)/shard_map/ppermute | solution.py:504
  132.9 8.4 %collective-permute-start.24 = (bf16[160,512]{1,0:T(8,128)(2,1)}, bf16[160,512]{1,0:T(8,128)(2,1)S(1)}, u32[]{:S(2)}, u32[]{:S(2)}) collective-permute-start(bf16[160,512]{1,0:T(8,128)(2,1)} %get-tuple-element.61), channel_id=1, source_target_pairs={{0,32},{32,64},{64,96},{96,0},{1,33},{33,65},{65,97},{97,1},{2,34}... | collective-permute-start | bytes 491528 | tf_op jit(solution)/shard_map/ppermute | solution.py:504
  134.6 7.0 %collective-permute-start.25 = (bf16[160,512]{1,0:T(8,128)(2,1)}, bf16[160,512]{1,0:T(8,128)(2,1)S(1)}, u32[]{:S(2)}, u32[]{:S(2)}) collective-permute-start(bf16[160,512]{1,0:T(8,128)(2,1)} %get-tuple-element.62), channel_id=1, source_target_pairs={{0,96},{32,0},{64,32},{96,64},{1,97},{33,1},{65,33},{97,65},{2,98}... | collective-permute-start | bytes 491528 | tf_op jit(solution)/shard_map/ppermute | solution.py:504

commit v7 on v6

--- a/solution.py
+++ b/solution.py
@@ -171,14 +171,15 @@
             for copy in loads(slot + 2):
                 copy.start()
 
+        together(softmax(slot, 1))
+        together(gradients(slot, 0))
+
         @pl.when(later > slot)
         def _():
             for copy in loads(later):
                 copy.wait()
-
-        together(softmax(slot, 1))
-        together(gradients(slot, 0))
-        together(softmax(later, 0))
+            together(softmax(later, 0))
+
         together(gradients(slot, 1))
         for copy in stores(slot):
             copy.start()

time: 145 us -> 147 us (1.014)
  Pallas kernels: 18.8 us -> 28.2 us
  waiting for transfers between devices: 43 us -> 35.4 us
    ppermute x8, starting transfers between devices: 9.68 us -> 20 us  [swap_cores(): return lax.ppermute(array, 'c', [(0, 1), (1, 0)])]
    pallas_call x1, Pallas kernels: 7.22 us -> 16.6 us  [attention(): pl.pallas_call(attention_kernel, in_specs=[smem] * 3 + [anywhere] * 3 + [...]
    all_to_all x2, waiting for transfers between devices: 29.1 us -> 19.7 us  [exchange(): return lax.all_to_all(array, axes, 0, 0, tiled=True)]
    ppermute x21, starting transfers between devices: 43.4 us -> 34.1 us  [ring(): return lax.ppermute(array, axis, [(i, (i + step) % 4) for i in range(4)])]
    ppermute x21, waiting for transfers between devices: 9.46 us -> 12.5 us  [ring(): return lax.ppermute(array, axis, [(i, (i + step) % 4) for i in range(4)])]
  transfers between devices with their start and end apart: 31 -> 31, of which waited for: 10 -> 11; matrix products, arithmetic and copies ran while one was open for 6% -> 6% of each run, Pallas kernels for 13% -> 19%
where the time goes in v7:
time: 147 us; the launch traced here: 145 us
  starting transfers between devices  65.5 us (45%)
  waiting for transfers between devices  35.4 us (24%)
  Pallas kernels  28.2 us (19%)
  local copies, waits for them, and re-layouts  11.7 us (8%)
  matrix products  3.75 us (3%)
    ppermute x21, starting transfers between devices, ring(): return lax.ppermute(array, axis, [(i, (i + step) % 4) for i in range(4)])  34.1 us
    ppermute x8, starting transfers between devices, swap_cores(): return lax.ppermute(array, 'c', [(0, 1), (1, 0)])  20 us
    all_to_all x2, waiting for transfers between devices, exchange(): return lax.all_to_all(array, axes, 0, 0, tiled=True)  19.7 us
    pallas_call x1, Pallas kernels, attention(): pl.pallas_call(attention_kernel, in_specs=[smem] * 3 + [anywhere] * 3 + [...  16.6 us
    ppermute x21, waiting for transfers between devices, ring(): return lax.ppermute(array, axis, [(i, (i + step) % 4) for i in range(4)])  12.5 us
    all_to_all x2, starting transfers between devices, exchange(): return lax.all_to_all(array, axes, 0, 0, tiled=True)  11.5 us
    unnamed x17, local copies, waits for them, and re-layouts  5.61 us
    dot_general x1, matrix products, body(): jnp.einsum('pd,dkc->pkc', prompt_hidden, kv_weight, preferred_element_typ...  3.75 us
  transfers between devices with their start and end apart: 31, of which 11 were waited for; matrix products, arithmetic and copies ran while one was open for 6% of the time, Pallas kernels for 19%

profile of v7, /device:TPU:1, one launch (start us, length us, event | category | flops | bytes accessed | tf_op | source)
XLA Modules:
  0.0 145.4 jit_solution(8199520342073816358)
XLA Ops:
  0.6 3.8 %fusion.3 = bf16[128,2,256]{2,0,1:T(8,128)(2,1)S(1)} fusion(bf16[5120,2,256]{2,1,0:T(2,128)(2,1)} %param.9, bf16[128,5120]{1,0:T(8,128)(2,1)} %hidden.1), kind=kOutput, calls=%fused_computation.4 | convolution fusion | flops 671154176 | bytes 6684672 | tf_op jit(solution)/shard_map/pd,dkc->pkc/dot_general | solution.py:482
  4.4 1.5 %collective-permute-start = (bf16[128,256]{1,0:T(8,128)(2,1)S(1)}, bf16[128,256]{1,0:T(8,128)(2,1)S(1)}, u32[]{:S(2)}, u32[]{:S(2)}) collective-permute-start(bf16[128,256]{1,0:T(8,128)(2,1)S(1)} %select_bitcast_fusion), channel_id=1, source_target_pairs={{0,4},{4,0},{1,5},{5,1},{2,6},{6,2},{3,7},{7,3},{8,12},{12,8},{9,1... | collective-permute-start | bytes 196616 | tf_op jit(solution)/shard_map/ppermute | solution.py:468
  5.9 0.9 collective-permute-done
  6.9 1.5 %broadcast_in_dim.2 = bf16[16,256,256]{2,1,0:T(8,128)(2,1)} broadcast(bf16[256,256]{1,0:T(8,128)(2,1)S(1)} %pad_maximum_fusion), dimensions={1,2} | broadcast | bytes 2228224 | tf_op jit(solution)/shard_map/broadcast_in_dim | solution.py:490
  8.4 8.0 %all-to-all-start = ((bf16[16,256,256]{2,1,0:T(8,128)(2,1)}), bf16[16,256,256]{2,1,0:T(8,128)(2,1)S(1)}, u32[]{:S(2)}, u32[]{:S(2)}) async-start(bf16[16,256,256]{2,1,0:T(8,128)(2,1)} %broadcast_in_dim.2), calls=%async_computation | async-start | bytes 4194304 | tf_op jit(solution)/shard_map/all_to_all | solution.py:472
  16.4 3.3 %columns.1.refs_2_ = bf16[8,640,128]{2,1,0:T(8,128)(2,1)} custom-call(bf16[128,5120]{1,0:T(8,128)(2,1)S(1)} %copy-done), custom_call_target="tpu_custom_call" | custom-call | tf_op jit(solution)/shard_map/columns/pallas_call | solution.py:260
  19.7 5.6 %copy.24 = bf16[5120,2,256]{2,0,1:T(8,128)(2,1)} copy(bf16[5120,2,256]{2,1,0:T(2,128)(2,1)} %param.9) | data formatting | bytes 10485760 | tf_op args[1]
  25.3 1.5 %reshape.27.refs_1_.own_hbm = bf16[8,128,512]{2,1,0:T(8,128)(2,1)} reshape(bf16[8,128,2,256]{3,2,1,0:T(2,128)(2,1)S(1)} %copy-done.6) | data formatting | bytes 2097152 | tf_op jit(solution)/shard_map/reshape | solution.py:493
  26.7 18.9 %all-to-all-done = bf16[16,256,256]{2,1,0:T(8,128)(2,1)S(1)} async-done(((bf16[16,256,256]{2,1,0:T(8,128)(2,1)}), bf16[16,256,256]{2,1,0:T(8,128)(2,1)S(1)}, u32[]{:S(2)}, u32[]{:S(2)}) %all-to-all-start) | async-done | bytes 2097184 | tf_op jit(solution)/shard_map/all_to_all | solution.py:472
  45.6 2.6 %collective-permute-start.1 = (bf16[32,128,256]{2,1,0:T(8,128)(2,1)S(1)}, bf16[32,128,256]{2,1,0:T(8,128)(2,1)}, u32[]{:S(2)}, u32[]{:S(2)}) collective-permute-start(bf16[32,128,256]{2,1,0:T(8,128)(2,1)S(1)} %after.4.near), channel_id=1, source_target_pairs={{0,4},{4,0},{1,5},{5,1},{2,6},{6,2},{3,7},{7,3},{8,12},{12,8},{9,1... | collective-permute-start | bytes 6291464 | tf_op jit(solution)/shard_map/ppermute | solution.py:468
  48.3 3.5 %all-to-all-start.1 = ((bf16[8,640,128]{2,1,0:T(8,128)(2,1)}), bf16[8,640,128]{2,1,0:T(8,128)(2,1)S(1)}, u32[]{:S(2)}, u32[]{:S(2)}) async-start(bf16[8,640,128]{2,1,0:T(8,128)(2,1)} %columns.1.refs_2_), calls=%async_computation.1 | async-start | bytes 2621440 | tf_op jit(solution)/shard_map/all_to_all | solution.py:472
  51.8 0.4 collective-permute-done.1.far
  52.2 16.6 %attention.1 = (bf16[8,128,1280]{2,1,0:T(8,128)(2,1)}, bf16[8,128,1280]{2,1,0:T(8,128)(2,1)}, bf16[8,128,512]{2,1,0:T(8,128)(2,1)}, bf16[16,128,256]{2,1,0:T(8,1...) custom-call(s32[32]{0:T(128)S(1)} %copy-done.4, ...), custom_call_target="tpu_custom_call" | custom-call | flops 10066329600 | bytes 16777216 | tf_op jit(solution)/shard_map/attention/pallas_call | solution.py:430
  68.8 0.9 all-to-all-done.1.refs_1_.hidden
  69.7 10.3 %collective-permute-start.2 = (bf16[16,128,256]{2,1,0:T(8,128)(2,1)}, bf16[16,128,256]{2,1,0:T(8,128)(2,1)S(1)}, u32[]{:S(2)}, u32[]{:S(2)}) collective-permute-start(bf16[16,128,256]{2,1,0:T(8,128)(2,1)} %after.5.refs_1_), channel_id=1, source_target_pairs={{0,4},{4,0},{1,5},{5,1},{2,6},{6,2},{3,7},{7,3},{8,12},{12,8},{9,1... | collective-permute-start | bytes 3145736 | tf_op jit(solution)/shard_map/ppermute | solution.py:468
  80.0 1.1 collective-permute-start.9
  81.1 1.4 collective-permute-done.2.got
  82.7 5.7 %collective-permute-start.3 = (bf16[4,128,256]{2,1,0:T(8,128)(2,1)S(1)}, bf16[4,128,256]{2,1,0:T(8,128)(2,1)S(1)}, u32[]{:S(2)}, u32[]{:S(2)}) collective-permute-start(bf16[4,128,256]{2,1,0:T(8,128)(2,1)S(1)} %get-tuple-element.42), channel_id=1, source_target_pairs={{0,32},{32,64},{64,96},{96,0},{1,33},{33,65},{65,97},{97,1},{2,34}... | collective-permute-start | bytes 786440 | tf_op jit(solution)/shard_map/ppermute | solution.py:505
  88.4 2.6 %collective-permute-start.4 = (bf16[4,128,256]{2,1,0:T(8,128)(2,1)S(1)}, bf16[4,128,256]{2,1,0:T(8,128)(2,1)S(1)}, u32[]{:S(2)}, u32[]{:S(2)}) collective-permute-start(bf16[4,128,256]{2,1,0:T(8,128)(2,1)S(1)} %get-tuple-element.43), channel_id=1, source_target_pairs={{0,64},{32,96},{64,0},{96,32},{1,65},{33,97},{65,1},{97,33},{2,66}... | collective-permute-start | bytes 786440 | tf_op jit(solution)/shard_map/ppermute | solution.py:505
  91.3 2.7 %collective-permute-start.11 = (bf16[4,128,256]{2,1,0:T(8,128)(2,1)S(1)}, bf16[4,128,256]{2,1,0:T(8,128)(2,1)S(1)}, u32[]{:S(2)}, u32[]{:S(2)}) collective-permute-start(bf16[4,128,256]{2,1,0:T(8,128)(2,1)S(1)} %get-tuple-element.53), channel_id=1, source_target_pairs={{0,16},{8,24},{16,0},{24,8},{1,17},{9,25},{17,1},{25,9},{2,18},{10... | collective-permute-start | bytes 786440 | tf_op jit(solution)/shard_map/ppermute | solution.py:505
  94.0 2.3 %collective-permute-done.3.refs_1_ = bf16[4,128,256]{2,1,0:T(8,128)(2,1)S(1)} collective-permute-done((bf16[4,128,256]{2,1,0:T(8,128)(2,1)S(1)}, bf16[4,128,256]{2,1,0:T(8,128)(2,1)S(1)}, u32[]{:S(2)}, u32[]{:S(2)}) %collective-permute-start.3) | collective-permute-done | bytes 262176 | tf_op jit(solution)/shard_map/ppermute | solution.py:505
  96.2 3.4 %collective-permute-start.12 = (bf16[4,128,256]{2,1,0:T(8,128)(2,1)S(1)}, bf16[4,128,256]{2,1,0:T(8,128)(2,1)S(1)}, u32[]{:S(2)}, u32[]{:S(2)}) collective-permute-start(bf16[4,128,256]{2,1,0:T(8,128)(2,1)S(1)} %get-tuple-element.54), channel_id=1, source_target_pairs={{0,24},{8,0},{16,8},{24,16},{1,25},{9,1},{17,9},{25,17},{2,26},{10... | collective-permute-start | bytes 786440 | tf_op jit(solution)/shard_map/ppermute | solution.py:505
  99.6 3.0 %collective-permute-done.4.refs_2_ = bf16[4,128,256]{2,1,0:T(8,128)(2,1)S(1)} collective-permute-done((bf16[4,128,256]{2,1,0:T(8,128)(2,1)S(1)}, bf16[4,128,256]{2,1,0:T(8,128)(2,1)S(1)}, u32[]{:S(2)}, u32[]{:S(2)}) %collective-permute-start.4) | collective-permute-done | bytes 262176 | tf_op jit(solution)/shard_map/ppermute | solution.py:505
  102.9 2.5 %hold.1.refs_1_.weight = bf16[2,5120,256]{2,1,0:T(8,128)(2,1)S(1)} custom-call(bf16[2,5120,256]{2,1,0:T(8,128)(2,1)} %after.6.source), custom_call_target="tpu_custom_call" | custom-call | tf_op jit(solution)/shard_map/hold/pallas_call | solution.py:366
  105.4 2.3 %collective-permute-start.7 = (bf16[128,256]{1,0:T(8,128)(2,1)S(1)}, bf16[128,256]{1,0:T(8,128)(2,1)S(1)}, u32[]{:S(2)}, u32[]{:S(2)}) collective-permute-start(bf16[128,256]{1,0:T(8,128)(2,1)S(1)} %get-tuple-element.47), channel_id=1, source_target_pairs={{0,16},{8,24},{16,0},{24,8},{1,17},{9,25},{17,1},{25,9},{2,18},{10... | collective-permute-start | bytes 196616 | tf_op jit(solution)/shard_map/ppermute | solution.py:505
  107.7 1.0 collective-permute-start.8
  108.8 1.8 %collective-permute-start.13 = (bf16[128,256]{1,0:T(8,128)(2,1)S(1)}, bf16[128,256]{1,0:T(8,128)(2,1)S(1)}, u32[]{:S(2)}, u32[]{:S(2)}) collective-permute-start(bf16[128,256]{1,0:T(8,128)(2,1)S(1)} %get-tuple-element.56), channel_id=1, source_target_pairs={{0,32},{32,64},{64,96},{96,0},{1,33},{33,65},{65,97},{97,1},{2,34}... | collective-permute-start | bytes 196616 | tf_op jit(solution)/shard_map/ppermute | solution.py:505
  110.6 2.6 %collective-permute-start.14 = (bf16[128,256]{1,0:T(8,128)(2,1)S(1)}, bf16[128,256]{1,0:T(8,128)(2,1)S(1)}, u32[]{:S(2)}, u32[]{:S(2)}) collective-permute-start(bf16[128,256]{1,0:T(8,128)(2,1)S(1)} %get-tuple-element.57), channel_id=1, source_target_pairs={{0,64},{32,96},{64,0},{96,32},{1,65},{33,97},{65,1},{97,33},{2,66}... | collective-permute-start | bytes 196616 | tf_op jit(solution)/shard_map/ppermute | solution.py:505
  113.2 0.6 collective-permute-start.15
  113.8 1.8 %collective-permute-done.14.refs_6_ = bf16[128,256]{1,0:T(8,128)(2,1)S(1)} collective-permute-done((bf16[128,256]{1,0:T(8,128)(2,1)S(1)}, bf16[128,256]{1,0:T(8,128)(2,1)S(1)}, u32[]{:S(2)}, u32[]{:S(2)}) %collective-permute-start.14) | collective-permute-done | bytes 65568 | tf_op jit(solution)/shard_map/ppermute | solution.py:505
  115.6 1.1 collective-permute-done.15.refs_7_
  116.8 0.4 collective-permute-start.18
  117.1 1.0 collective-permute-start.17
  118.2 0.8 collective-permute-start.16
  118.9 2.2 %prompt.1 = (bf16[128,1280]{1,0:T(8,128)(2,1)S(1)}, bf16[128,1280]{1,0:T(8,128)(2,1)}, bf16[128,1280]{1,0:T(8,128)(2,1)S(1)}, bf16[128,1280]{1,0:T(8,128)(2,1)}) custom-call(bf16[128,512]{1,0:T(8,128)(2,1)S(1)} %block.1.refs_0_, bf16[2,5120,256]{2,1,0:T(8,128)(2,1)S(1)} %hold.1.refs_1_.weight), custom_call_target="tpu_custom_call" | custom-call | flops 671088640 | bytes 4194304 | tf_op jit(solution)/shard_map/prompt/pallas_call | solution.py:390
  121.2 2.7 %collective-permute-start.26 = (bf16[128,1280]{1,0:T(8,128)(2,1)S(1)}, bf16[128,1280]{1,0:T(8,128)(2,1)S(1)}, u32[]{:S(2)}, u32[]{:S(2)}) collective-permute-start(bf16[128,1280]{1,0:T(8,128)(2,1)S(1)} %get-tuple-element.64), channel_id=1, source_target_pairs={{0,2},{1,3},{2,0},{3,1},{4,6},{5,7},{6,4},{7,5},{8,10},{9,11},{10,... | collective-permute-start | bytes 983048 | tf_op jit(solution)/shard_map/ppermute | solution.py:505
  123.9 3.9 %collective-permute-start.19 = (bf16[128,512]{1,0:T(8,128)(2,1)S(1)}, bf16[128,512]{1,0:T(8,128)(2,1)S(1)}, u32[]{:S(2)}, u32[]{:S(2)}) collective-permute-start(bf16[128,512]{1,0:T(8,128)(2,1)S(1)} %block.1.refs_0_), channel_id=1, source_target_pairs={{0,4},{4,0},{1,5},{5,1},{2,6},{6,2},{3,7},{7,3},{8,12},{12,8},{9,1... | collective-permute-start | bytes 393224 | tf_op jit(solution)/shard_map/ppermute | solution.py:468
  127.8 0.5 collective-permute-start.21
  128.4 0.4 collective-permute-done.19.refs_4_
  129.1 2.3 %collective-permute-start.28 = (bf16[128,1280]{1,0:T(8,128)(2,1)}, bf16[128,1280]{1,0:T(8,128)(2,1)S(1)}, u32[]{:S(2)}, u32[]{:S(2)}) collective-permute-start(bf16[128,1280]{1,0:T(8,128)(2,1)} %get-tuple-element.66), channel_id=1, source_target_pairs={{0,3},{1,0},{2,1},{3,2},{4,7},{5,4},{6,5},{7,6},{8,11},{9,8},{10,9... | collective-permute-start | bytes 983048 | tf_op jit(solution)/shard_map/ppermute | solution.py:505
  131.4 1.7 %term.1 = (bf16[160,512]{1,0:T(8,128)(2,1)S(1)}, bf16[160,512]{1,0:T(8,128)(2,1)}, bf16[160,512]{1,0:T(8,128)(2,1)}, bf16[160,512]{1,0:T(8,128)(2,1)}) custom-call(bf16[8,640,128]{2,1,0:T(8,128)(2,1)S(1)} %all-to-all-done.1.refs_1_.hidden, bf16[128,512]{1,0:T(8,128)(2,1)S(1)} %block.1.refs_0_, bf16[128,512]{1,0:T(8,128)(2,1)S(1)} %collective-permute-done.16.refs_1_, ...), custom_call_target="tpu_custom_call" | custom-call | flops 2000000000 | bytes 10000000 | tf_op jit(solution)/shard_map/term/pallas_call | solution.py:347
  133.2 1.2 collective-permute-start.23
  134.4 1.2 collective-permute-start.24
  135.6 1.5 %collective-permute-start.25 = (bf16[160,512]{1,0:T(8,128)(2,1)}, bf16[160,512]{1,0:T(8,128)(2,1)S(1)}, u32[]{:S(2)}, u32[]{:S(2)}) collective-permute-start(bf16[160,512]{1,0:T(8,128)(2,1)} %get-tuple-element.62), channel_id=1, source_target_pairs={{0,96},{32,0},{64,32},{96,64},{1,97},{33,1},{65,33},{97,65},{2,98}... | collective-permute-start | bytes 491528 | tf_op jit(solution)/shard_map/ppermute | solution.py:505
  137.1 2.1 %reshape.29 = bf16[8,128,2,256]{3,2,1,0:T(2,128)(2,1)} reshape(bf16[8,128,512]{2,1,0:T(8,128)(2,1)} %get-tuple-element.38) | data formatting | bytes 2097152 | tf_op jit(solution)/shard_map/reshape | solution.py:502
  139.2 0.9 sum.3
  140.1 4.3 %collective-permute-done.24.refs_2_ = bf16[160,512]{1,0:T(8,128)(2,1)S(1)} collective-permute-done((bf16[160,512]{1,0:T(8,128)(2,1)}, bf16[160,512]{1,0:T(8,128)(2,1)S(1)}, u32[]{:S(2)}, u32[]{:S(2)}) %collective-permute-start.24) | collective-permute-done | bytes 163872 | tf_op jit(solution)/shard_map/ppermute | solution.py:505
  144.5 0.9 reshape.30
  (55 shorter events, 1.6 us)
Async XLA Ops:
  4.4 2.4 %collective-permute-start = (bf16[128,256]{1,0:T(8,128)(2,1)S(1)}, bf16[128,256]{1,0:T(8,128)(2,1)S(1)}, u32[]{:S(2)}, u32[]{:S(2)}) collective-permute-start(bf16[128,256]{1,0:T(8,128)(2,1)S(1)} %select_bitcast_fusion), channel_id=1, source_target_pairs={{0,4},{4,0},{1,5},{5,1},{2,6},{6,2},{3,7},{7,3},{8,12},{12,8},{9,1... | collective-permute-start | bytes 196616 | tf_op jit(solution)/shard_map/ppermute | solution.py:468
  8.4 8.0 %copy-start = (bf16[128,5120]{1,0:T(8,128)(2,1)S(1)}, bf16[128,5120]{1,0:T(8,128)(2,1)}, u32[]{:S(2)}) copy-start(bf16[128,5120]{1,0:T(8,128)(2,1)} %hidden.1) | copy-start | bytes 3932164
  8.4 37.2 %all-to-all-start = ((bf16[16,256,256]{2,1,0:T(8,128)(2,1)}), bf16[16,256,256]{2,1,0:T(8,128)(2,1)S(1)}, u32[]{:S(2)}, u32[]{:S(2)}) async-start(bf16[16,256,256]{2,1,0:T(8,128)(2,1)} %broadcast_in_dim.2), calls=%async_computation | async-start | bytes 4194304 | tf_op jit(solution)/shard_map/all_to_all | solution.py:472
  19.7 5.6 %copy-start.6 = (bf16[8,128,2,256]{3,2,1,0:T(2,128)(2,1)S(1)}, bf16[8,128,2,256]{3,2,1,0:T(2,128)(2,1)}, u32[]{:S(2)}) copy-start(bf16[8,128,2,256]{3,2,1,0:T(2,128)(2,1)} %param.12) | copy-start | bytes 3145732
  45.6 6.6 %copy-start.3 = (s32[32,8]{0,1:T(8,128)S(1)}, s32[32,8]{0,1:T(8,128)}, u32[]{:S(2)}) copy-start(s32[32,8]{0,1:T(8,128)} %param.14) | copy-start | bytes 3076
  45.6 6.6 %copy-start.4 = (s32[32]{0:T(128)S(1)}, s32[32]{0:T(128)}, u32[]{:S(2)}) copy-start(s32[32]{0:T(128)} %pack_counts.1) | copy-start | bytes 388
  45.6 6.6 %copy-start.5 = (s32[32]{0:T(128)S(1)}, s32[32]{0:T(128)}, u32[]{:S(2)}) copy-start(s32[32]{0:T(128)} %block_group.1) | copy-start | bytes 388
  45.6 6.5 %collective-permute-start.1 = (bf16[32,128,256]{2,1,0:T(8,128)(2,1)S(1)}, bf16[32,128,256]{2,1,0:T(8,128)(2,1)}, u32[]{:S(2)}, u32[]{:S(2)}) collective-permute-start(bf16[32,128,256]{2,1,0:T(8,128)(2,1)S(1)} %after.4.near), channel_id=1, source_target_pairs={{0,4},{4,0},{1,5},{5,1},{2,6},{6,2},{3,7},{7,3},{8,12},{12,8},{9,1... | collective-permute-start | bytes 6291464 | tf_op jit(solution)/shard_map/ppermute | solution.py:468
  48.3 21.4 %all-to-all-start.1 = ((bf16[8,640,128]{2,1,0:T(8,128)(2,1)}), bf16[8,640,128]{2,1,0:T(8,128)(2,1)S(1)}, u32[]{:S(2)}, u32[]{:S(2)}) async-start(bf16[8,640,128]{2,1,0:T(8,128)(2,1)} %columns.1.refs_2_), calls=%async_computation.1 | async-start | bytes 2621440 | tf_op jit(solution)/shard_map/all_to_all | solution.py:472
  68.8 11.2 %copy-start.7 = (bf16[16,128,256]{2,1,0:T(8,128)(2,1)S(1)}, bf16[16,128,256]{2,1,0:T(8,128)(2,1)}, u32[]{:S(2)}) copy-start(bf16[16,128,256]{2,1,0:T(8,128)(2,1)} %get-tuple-element.50) | copy-start | bytes 3145732
  68.8 13.7 %copy-start.2 = (bf16[16,128,256]{2,1,0:T(8,128)(2,1)S(1)}, bf16[16,128,256]{2,1,0:T(8,128)(2,1)}, u32[]{:S(2)}) copy-start(bf16[16,128,256]{2,1,0:T(8,128)(2,1)} %get-tuple-element.39.keep) | copy-start | bytes 3145732
  69.7 21.3 %copy-start.1 = (bf16[16,128,256]{2,1,0:T(8,128)(2,1)S(1)}, bf16[16,128,256]{2,1,0:T(8,128)(2,1)}, u32[]{:S(2)}) copy-start(bf16[16,128,256]{2,1,0:T(8,128)(2,1)} %get-tuple-element.49.keep) | copy-start | bytes 3145732
  69.7 12.8 %collective-permute-start.2 = (bf16[16,128,256]{2,1,0:T(8,128)(2,1)}, bf16[16,128,256]{2,1,0:T(8,128)(2,1)S(1)}, u32[]{:S(2)}, u32[]{:S(2)}) collective-permute-start(bf16[16,128,256]{2,1,0:T(8,128)(2,1)} %after.5.refs_1_), channel_id=1, source_target_pairs={{0,4},{4,0},{1,5},{5,1},{2,6},{6,2},{3,7},{7,3},{8,12},{12,8},{9,1... | collective-permute-start | bytes 3145736 | tf_op jit(solution)/shard_map/ppermute | solution.py:468
  80.0 11.1 %collective-permute-start.9 = (bf16[16,128,256]{2,1,0:T(8,128)(2,1)S(1)}, bf16[16,128,256]{2,1,0:T(8,128)(2,1)S(1)}, u32[]{:S(2)}, u32[]{:S(2)}) collective-permute-start(bf16[16,128,256]{2,1,0:T(8,128)(2,1)S(1)} %copy-done.7), channel_id=1, source_target_pairs={{0,4},{4,0},{1,5},{5,1},{2,6},{6,2},{3,7},{7,3},{8,12},{12,8},{9,1... | collective-permute-start | bytes 3145736 | tf_op jit(solution)/shard_map/ppermute | solution.py:468
  82.7 13.5 %collective-permute-start.3 = (bf16[4,128,256]{2,1,0:T(8,128)(2,1)S(1)}, bf16[4,128,256]{2,1,0:T(8,128)(2,1)S(1)}, u32[]{:S(2)}, u32[]{:S(2)}) collective-permute-start(bf16[4,128,256]{2,1,0:T(8,128)(2,1)S(1)} %get-tuple-element.42), channel_id=1, source_target_pairs={{0,32},{32,64},{64,96},{96,0},{1,33},{33,65},{65,97},{97,1},{2,34}... | collective-permute-start | bytes 786440 | tf_op jit(solution)/shard_map/ppermute | solution.py:505
  88.4 14.3 %collective-permute-start.4 = (bf16[4,128,256]{2,1,0:T(8,128)(2,1)S(1)}, bf16[4,128,256]{2,1,0:T(8,128)(2,1)S(1)}, u32[]{:S(2)}, u32[]{:S(2)}) collective-permute-start(bf16[4,128,256]{2,1,0:T(8,128)(2,1)S(1)} %get-tuple-element.43), channel_id=1, source_target_pairs={{0,64},{32,96},{64,0},{96,32},{1,65},{33,97},{65,1},{97,33},{2,66}... | collective-permute-start | bytes 786440 | tf_op jit(solution)/shard_map/ppermute | solution.py:505
  91.0 11.7 %collective-permute-start.5 = (bf16[4,128,256]{2,1,0:T(8,128)(2,1)S(1)}, bf16[4,128,256]{2,1,0:T(8,128)(2,1)S(1)}, u32[]{:S(2)}, u32[]{:S(2)}) collective-permute-start(bf16[4,128,256]{2,1,0:T(8,128)(2,1)S(1)} %get-tuple-element.44), channel_id=1, source_target_pairs={{0,96},{32,0},{64,32},{96,64},{1,97},{33,1},{65,33},{97,65},{2,98}... | collective-permute-start | bytes 786440 | tf_op jit(solution)/shard_map/ppermute | solution.py:505
  91.3 16.5 %collective-permute-start.11 = (bf16[4,128,256]{2,1,0:T(8,128)(2,1)S(1)}, bf16[4,128,256]{2,1,0:T(8,128)(2,1)S(1)}, u32[]{:S(2)}, u32[]{:S(2)}) collective-permute-start(bf16[4,128,256]{2,1,0:T(8,128)(2,1)S(1)} %get-tuple-element.53), channel_id=1, source_target_pairs={{0,16},{8,24},{16,0},{24,8},{1,17},{9,25},{17,1},{25,9},{2,18},{10... | collective-permute-start | bytes 786440 | tf_op jit(solution)/shard_map/ppermute | solution.py:505
  94.0 14.8 %collective-permute-start.10 = (bf16[4,128,256]{2,1,0:T(8,128)(2,1)S(1)}, bf16[4,128,256]{2,1,0:T(8,128)(2,1)S(1)}, u32[]{:S(2)}, u32[]{:S(2)}) collective-permute-start(bf16[4,128,256]{2,1,0:T(8,128)(2,1)S(1)} %get-tuple-element.52), channel_id=1, source_target_pairs={{0,8},{8,16},{16,24},{24,0},{1,9},{9,17},{17,25},{25,1},{2,10},{10... | collective-permute-start | bytes 786440 | tf_op jit(solution)/shard_map/ppermute | solution.py:505
  96.2 12.5 %collective-permute-start.12 = (bf16[4,128,256]{2,1,0:T(8,128)(2,1)S(1)}, bf16[4,128,256]{2,1,0:T(8,128)(2,1)S(1)}, u32[]{:S(2)}, u32[]{:S(2)}) collective-permute-start(bf16[4,128,256]{2,1,0:T(8,128)(2,1)S(1)} %get-tuple-element.54), channel_id=1, source_target_pairs={{0,24},{8,0},{16,8},{24,16},{1,25},{9,1},{17,9},{25,17},{2,26},{10... | collective-permute-start | bytes 786440 | tf_op jit(solution)/shard_map/ppermute | solution.py:505
  102.8 10.4 %collective-permute-start.6 = (bf16[128,256]{1,0:T(8,128)(2,1)S(1)}, bf16[128,256]{1,0:T(8,128)(2,1)S(1)}, u32[]{:S(2)}, u32[]{:S(2)}) collective-permute-start(bf16[128,256]{1,0:T(8,128)(2,1)S(1)} %get-tuple-element.46), channel_id=1, source_target_pairs={{0,8},{8,16},{16,24},{24,0},{1,9},{9,17},{17,25},{25,1},{2,10},{10... | collective-permute-start | bytes 196616 | tf_op jit(solution)/shard_map/ppermute | solution.py:505
  105.4 8.3 %collective-permute-start.7 = (bf16[128,256]{1,0:T(8,128)(2,1)S(1)}, bf16[128,256]{1,0:T(8,128)(2,1)S(1)}, u32[]{:S(2)}, u32[]{:S(2)}) collective-permute-start(bf16[128,256]{1,0:T(8,128)(2,1)S(1)} %get-tuple-element.47), channel_id=1, source_target_pairs={{0,16},{8,24},{16,0},{24,8},{1,17},{9,25},{17,1},{25,9},{2,18},{10... | collective-permute-start | bytes 196616 | tf_op jit(solution)/shard_map/ppermute | solution.py:505
  107.7 6.0 %collective-permute-start.8 = (bf16[128,256]{1,0:T(8,128)(2,1)S(1)}, bf16[128,256]{1,0:T(8,128)(2,1)S(1)}, u32[]{:S(2)}, u32[]{:S(2)}) collective-permute-start(bf16[128,256]{1,0:T(8,128)(2,1)S(1)} %get-tuple-element.48), channel_id=1, source_target_pairs={{0,24},{8,0},{16,8},{24,16},{1,25},{9,1},{17,9},{25,17},{2,26},{10... | collective-permute-start | bytes 196616 | tf_op jit(solution)/shard_map/ppermute | solution.py:505
  108.8 4.9 %collective-permute-start.13 = (bf16[128,256]{1,0:T(8,128)(2,1)S(1)}, bf16[128,256]{1,0:T(8,128)(2,1)S(1)}, u32[]{:S(2)}, u32[]{:S(2)}) collective-permute-start(bf16[128,256]{1,0:T(8,128)(2,1)S(1)} %get-tuple-element.56), channel_id=1, source_target_pairs={{0,32},{32,64},{64,96},{96,0},{1,33},{33,65},{65,97},{97,1},{2,34}... | collective-permute-start | bytes 196616 | tf_op jit(solution)/shard_map/ppermute | solution.py:505
  110.6 5.0 %collective-permute-start.14 = (bf16[128,256]{1,0:T(8,128)(2,1)S(1)}, bf16[128,256]{1,0:T(8,128)(2,1)S(1)}, u32[]{:S(2)}, u32[]{:S(2)}) collective-permute-start(bf16[128,256]{1,0:T(8,128)(2,1)S(1)} %get-tuple-element.57), channel_id=1, source_target_pairs={{0,64},{32,96},{64,0},{96,32},{1,65},{33,97},{65,1},{97,33},{2,66}... | collective-permute-start | bytes 196616 | tf_op jit(solution)/shard_map/ppermute | solution.py:505
  113.2 3.5 %collective-permute-start.15 = (bf16[128,256]{1,0:T(8,128)(2,1)S(1)}, bf16[128,256]{1,0:T(8,128)(2,1)S(1)}, u32[]{:S(2)}, u32[]{:S(2)}) collective-permute-start(bf16[128,256]{1,0:T(8,128)(2,1)S(1)} %get-tuple-element.58), channel_id=1, source_target_pairs={{0,96},{32,0},{64,32},{96,64},{1,97},{33,1},{65,33},{97,65},{2,98}... | collective-permute-start | bytes 196616 | tf_op jit(solution)/shard_map/ppermute | solution.py:505
  116.8 11.0 %collective-permute-start.18 = (bf16[128,512]{1,0:T(8,128)(2,1)S(1)}, bf16[128,512]{1,0:T(8,128)(2,1)S(1)}, u32[]{:S(2)}, u32[]{:S(2)}) collective-permute-start(bf16[128,512]{1,0:T(8,128)(2,1)S(1)} %block.1.refs_0_), channel_id=1, source_target_pairs={{0,24},{8,0},{16,8},{24,16},{1,25},{9,1},{17,9},{25,17},{2,26},{10... | collective-permute-start | bytes 393224 | tf_op jit(solution)/shard_map/ppermute | solution.py:505
  117.1 10.6 %collective-permute-start.17 = (bf16[128,512]{1,0:T(8,128)(2,1)S(1)}, bf16[128,512]{1,0:T(8,128)(2,1)S(1)}, u32[]{:S(2)}, u32[]{:S(2)}) collective-permute-start(bf16[128,512]{1,0:T(8,128)(2,1)S(1)} %block.1.refs_0_), channel_id=1, source_target_pairs={{0,16},{8,24},{16,0},{24,8},{1,17},{9,25},{17,1},{25,9},{2,18},{10... | collective-permute-start | bytes 393224 | tf_op jit(solution)/shard_map/ppermute | solution.py:505
  118.2 10.1 %collective-permute-start.16 = (bf16[128,512]{1,0:T(8,128)(2,1)S(1)}, bf16[128,512]{1,0:T(8,128)(2,1)S(1)}, u32[]{:S(2)}, u32[]{:S(2)}) collective-permute-start(bf16[128,512]{1,0:T(8,128)(2,1)S(1)} %block.1.refs_0_), channel_id=1, source_target_pairs={{0,8},{8,16},{16,24},{24,0},{1,9},{9,17},{17,25},{25,1},{2,10},{10... | collective-permute-start | bytes 393224 | tf_op jit(solution)/shard_map/ppermute | solution.py:505
  121.2 14.4 %collective-permute-start.26 = (bf16[128,1280]{1,0:T(8,128)(2,1)S(1)}, bf16[128,1280]{1,0:T(8,128)(2,1)S(1)}, u32[]{:S(2)}, u32[]{:S(2)}) collective-permute-start(bf16[128,1280]{1,0:T(8,128)(2,1)S(1)} %get-tuple-element.64), channel_id=1, source_target_pairs={{0,2},{1,3},{2,0},{3,1},{4,6},{5,7},{6,4},{7,5},{8,10},{9,11},{10,... | collective-permute-start | bytes 983048 | tf_op jit(solution)/shard_map/ppermute | solution.py:505
  123.9 4.9 %collective-permute-start.19 = (bf16[128,512]{1,0:T(8,128)(2,1)S(1)}, bf16[128,512]{1,0:T(8,128)(2,1)S(1)}, u32[]{:S(2)}, u32[]{:S(2)}) collective-permute-start(bf16[128,512]{1,0:T(8,128)(2,1)S(1)} %block.1.refs_0_), channel_id=1, source_target_pairs={{0,4},{4,0},{1,5},{5,1},{2,6},{6,2},{3,7},{7,3},{8,12},{12,8},{9,1... | collective-permute-start | bytes 393224 | tf_op jit(solution)/shard_map/ppermute | solution.py:468
  127.8 1.3 collective-permute-start.22
  127.8 3.7 %collective-permute-start.21 = (bf16[128,512]{1,0:T(8,128)(2,1)S(1)}, bf16[128,512]{1,0:T(8,128)(2,1)S(1)}, u32[]{:S(2)}, u32[]{:S(2)}) collective-permute-start(bf16[128,512]{1,0:T(8,128)(2,1)S(1)} %collective-permute-done.17.refs_2_), channel_id=1, source_target_pairs={{0,4},{4,0},{1,5},{5,1},{2,6},{6,2},{3,7},{7,3},{8,12},{12,8},{9,1... | collective-permute-start | bytes 393224 | tf_op jit(solution)/shard_map/ppermute | solution.py:468
  128.3 3.2 %collective-permute-start.20 = (bf16[128,512]{1,0:T(8,128)(2,1)S(1)}, bf16[128,512]{1,0:T(8,128)(2,1)S(1)}, u32[]{:S(2)}, u32[]{:S(2)}) collective-permute-start(bf16[128,512]{1,0:T(8,128)(2,1)S(1)} %collective-permute-done.16.refs_1_), channel_id=1, source_target_pairs={{0,4},{4,0},{1,5},{5,1},{2,6},{6,2},{3,7},{7,3},{8,12},{12,8},{9,1... | collective-permute-start | bytes 393224 | tf_op jit(solution)/shard_map/ppermute | solution.py:468
  128.8 10.5 %collective-permute-start.27 = (bf16[128,1280]{1,0:T(8,128)(2,1)}, bf16[128,1280]{1,0:T(8,128)(2,1)S(1)}, u32[]{:S(2)}, u32[]{:S(2)}) collective-permute-start(bf16[128,1280]{1,0:T(8,128)(2,1)} %get-tuple-element.65), channel_id=1, source_target_pairs={{0,1},{1,2},{2,3},{3,0},{4,5},{5,6},{6,7},{7,4},{8,9},{9,10},{10,1... | collective-permute-start | bytes 983048 | tf_op jit(solution)/shard_map/ppermute | solution.py:505
  129.1 10.1 %collective-permute-start.28 = (bf16[128,1280]{1,0:T(8,128)(2,1)}, bf16[128,1280]{1,0:T(8,128)(2,1)S(1)}, u32[]{:S(2)}, u32[]{:S(2)}) collective-permute-start(bf16[128,1280]{1,0:T(8,128)(2,1)} %get-tuple-element.66), channel_id=1, source_target_pairs={{0,3},{1,0},{2,1},{3,2},{4,7},{5,4},{6,5},{7,6},{8,11},{9,8},{10,9... | collective-permute-start | bytes 983048 | tf_op jit(solution)/shard_map/ppermute | solution.py:505
  133.2 6.9 %collective-permute-start.23 = (bf16[160,512]{1,0:T(8,128)(2,1)}, bf16[160,512]{1,0:T(8,128)(2,1)S(1)}, u32[]{:S(2)}, u32[]{:S(2)}) collective-permute-start(bf16[160,512]{1,0:T(8,128)(2,1)} %get-tuple-element.60), channel_id=1, source_target_pairs={{0,64},{32,96},{64,0},{96,32},{1,65},{33,97},{65,1},{97,33},{2,66}... | collective-permute-start | bytes 491528 | tf_op jit(solution)/shard_map/ppermute | solution.py:505
  134.4 10.0 %collective-permute-start.24 = (bf16[160,512]{1,0:T(8,128)(2,1)}, bf16[160,512]{1,0:T(8,128)(2,1)S(1)}, u32[]{:S(2)}, u32[]{:S(2)}) collective-permute-start(bf16[160,512]{1,0:T(8,128)(2,1)} %get-tuple-element.61), channel_id=1, source_target_pairs={{0,32},{32,64},{64,96},{96,0},{1,33},{33,65},{65,97},{97,1},{2,34}... | collective-permute-start | bytes 491528 | tf_op jit(solution)/shard_map/ppermute | solution.py:505
  135.6 8.8 %collective-permute-start.25 = (bf16[160,512]{1,0:T(8,128)(2,1)}, bf16[160,512]{1,0:T(8,128)(2,1)S(1)}, u32[]{:S(2)}, u32[]{:S(2)}) collective-permute-start(bf16[160,512]{1,0:T(8,128)(2,1)} %get-tuple-element.62), channel_id=1, source_target_pairs={{0,96},{32,0},{64,32},{96,64},{1,97},{33,1},{65,33},{97,65},{2,98}... | collective-permute-start | bytes 491528 | tf_op jit(solution)/shard_map/ppermute | solution.py:505
